TPU v7x, 128 devices: a whole 4x4x4 slice. The times are simulated.
128 devices in a mesh: gx: 8 (over y, core), gy: 4 (over z), af: 4 (over x).
Axes of the slice: x: 4, y: 4, z: 4, core: 2. Of those that a mesh axis runs over, the one named last changes fastest.
Arguments:
- press_matrix: float32 [8, 64, 2048], P(None, 'gx', ('gy', 'af')), may hold values from -1.5 to 1.5
- cond_matrix: float32 [8, 64, 2048], P(None, 'gx', ('gy', 'af')), may hold values from 0.05 to 0.5
- accum_matrix: float32 [8, 64, 2048], P(None, 'gx', ('gy', 'af')), may hold values from 0.5 to 2
- press_frac: float32 [512, 256], P(('gx', 'gy', 'af')), may hold values from -1.5 to 1.5
- accum_frac: float32 [512, 256], P(('gx', 'gy', 'af')), may hold values from 0.3 to 1
- trans_chain: float32 [512, 256], P(('gx', 'gy', 'af')), may hold values from 0.1 to 1
- couple_mf: float32 [512, 256], P(('gx', 'gy', 'af')), may hold values from 0.7 to 1.4
- couple_fm: float32 [512, 256], P(('gx', 'gy', 'af')), may hold values from 0.6 to 1.2
- conn_tile: int32 [512, 256], P(('gx', 'gy', 'af')), may hold values from 0 to 127, as said below
- conn_layer: int32 [512, 256], P(('gx', 'gy', 'af')), may hold values from 0 to 7
- conn_cell: int32 [512, 256], P(('gx', 'gy', 'af')), may hold values from 0 to 1023
- inter_delta: int32 [512], P(('gx', 'gy', 'af')), may hold values from 0 to 4, as said below
- inter_from: int32 [512], P(('gx', 'gy', 'af')), may hold values from 0 to 255
- inter_to: int32 [512], P(('gx', 'gy', 'af')), may hold values from 0 to 255
- inter_trans: float32 [512], P(('gx', 'gy', 'af')), may hold values from 0.5 to 2
- well_tile: int32 [32], replicated, may hold values from 0 to 127
- well_cell: int32 [32], replicated, may hold values from 0 to 1023
- well_rate: float32 [32], replicated, may hold values from -8 to 8
Outputs:
- res_matrix: float32 [8, 64, 2048], P(None, 'gx', ('gy', 'af'))
- res_fracture: float32 [512, 256], P(('gx', 'gy', 'af'))
- adj_matrix: float32 [8, 64, 2048], P(None, 'gx', ('gy', 'af'))
- adj_fracture: float32 [512, 256], P(('gx', 'gy', 'af'))
Inputs may be any that keep to these rules, and one draw needn't show every extreme that they name: `conn_tile`: in each aligned run of 1024 segments (blocks k * 4 to (k + 1) * 4 - 1), at most 16 segments lie in cells of one tile; in every draw some tile holds exactly 16 segments of every such run. b + inter_delta(b) never passes the last block; the value 4 is reached.
All inputs are finite; a program needn't handle non-finite values.
Results may differ from a plain program's by a relative error of at most 0.00013.
Values sent between devices are 32-bit elements; how exact they have to be, the bound alone decides.
No kernel may reach another device: no remote copies, remote signals or barrier semaphores. Data moves between devices by JAX's collectives and lax.ppermute only.
A program may use at most 64 MiB of HBM per device.

v0:
```python
import jax
import jax.numpy as jnp
from jax import lax
from jax.experimental import pallas as pl
from jax.experimental.pallas import tpu as pltpu
from jax.sharding import PartitionSpec as P

ITERS = 8
CAP = 16
TILES = 128
ROWS = 64
EXT = 24
LAYERS = 8
SLOTS = CAP * TILES
ALL = ("gx", "gy", "af")
YA = ("gy", "af")
f32 = jnp.float32
bf16 = jnp.bfloat16
i32 = jnp.int32


def iota(shape, axis):
    return lax.broadcasted_iota(i32, shape, axis)


def parts(value):
    high = value.astype(bf16)
    return high, (value - high.astype(f32)).astype(bf16)


def dot_nn(a, b):
    return lax.dot_general(a, b, (((1,), (0,)), ((), ())), preferred_element_type=f32)


def dot_nt(a, b):
    return lax.dot_general(a, b, (((1,), (1,)), ((), ())), preferred_element_type=f32)


def dot_tn(a, b):
    return lax.dot_general(a, b, (((0,), (0,)), ((), ())), preferred_element_type=f32)


def as_row(rows):
    return jnp.concatenate([rows[i : i + 1] for i in range(rows.shape[0])], axis=1)


def as_rows(row):
    return jnp.concatenate([row[:, i : i + 128] for i in range(0, row.shape[1], 128)], axis=0)


def total(value):
    return jnp.sum(jnp.sum(value, axis=1, keepdims=True), axis=0, keepdims=True)


def fold(value):
    return jnp.concatenate([value[:, :128], value[:, 128:]], axis=0)


def unfold(value):
    return jnp.concatenate([value[:4], value[4:]], axis=1)


def seg_code():
    row = iota((8, 128), 0)
    return (row % 4) * 256 + (row // 4) * 128 + iota((8, 128), 1)


def chain(tnext, field):
    lane = iota((8, 128), 1)
    ahead = pltpu.roll(field, 127, 1)
    ahead = jnp.where(lane == 127, pltpu.roll(ahead, 4, 0), ahead)
    behind = pltpu.roll(tnext * field, 1, 1)
    behind = jnp.where(lane == 0, pltpu.roll(behind, 4, 0), behind)
    return tnext * ahead + behind


def owner_hot(owner_row):
    return (iota((TILES, 1024), 0) == owner_row).astype(bf16)


def rank_mask(rank_row):
    return iota((CAP, 1024), 0) == rank_row


def to_slots(values, hot, mask):
    halves = ([], [])
    for value in values:
        row = as_row(value)
        for half, part in zip(halves, parts(row)):
            half.append(jnp.where(mask, part.astype(f32), 0.0).astype(bf16))
    both = jnp.concatenate([jnp.concatenate(half, axis=0) for half in halves], axis=1)
    return dot_nt(both, jnp.concatenate([hot, hot], axis=1))


def from_slots(table, hot, mask):
    high, low = parts(table)
    rows = dot_nn(jnp.concatenate([high, low], axis=1), jnp.concatenate([hot, hot], axis=0))
    return as_rows(jnp.sum(jnp.where(mask, rows, 0.0), axis=0, keepdims=True))


def cell_hot(index_row):
    columns = (iota((128, SLOTS), 0) == (index_row & 127)).astype(bf16)
    return columns, iota((ROWS, SLOTS), 0) == (index_row >> 7)


def scatter(tables, columns, mask):
    stacked = []
    for table in tables:
        for part in parts(as_row(table)):
            stacked.append(jnp.where(mask, part.astype(f32), 0.0).astype(bf16))
    sums = dot_nt(jnp.concatenate(stacked, axis=0), columns)
    return [
        (sums[2 * i * ROWS : (2 * i + 1) * ROWS] + sums[(2 * i + 1) * ROWS : (2 * i + 2) * ROWS]).reshape(LAYERS, 8, 128)
        for i in range(len(tables))
    ]


def gather(fields, columns, mask):
    stacked = []
    for field in fields:
        stacked.extend(parts(field.reshape(ROWS, 128)))
    rows = dot_nn(jnp.concatenate(stacked, axis=0), columns)
    out = []
    for i in range(len(fields)):
        both = rows[2 * i * ROWS : (2 * i + 1) * ROWS] + rows[(2 * i + 1) * ROWS : (2 * i + 2) * ROWS]
        out.append(as_rows(jnp.sum(jnp.where(mask, both, 0.0), axis=0, keepdims=True)))
    return out


def faces_of(field):
    rows = iota((16, 128), 0)
    lanes = iota((16, 128), 1)
    pick = (((rows == 0) & (lanes == 0)) | ((rows == 1) & (lanes == 127))).astype(bf16)
    both = dot_nt(jnp.concatenate([pick, pick], axis=1), jnp.concatenate(parts(field), axis=1))
    return both[0:1], both[1:2]


def columns_of(left, right):
    width = left.shape[1]
    held = [part.astype(f32) for row in (left, right) for part in parts(row)]
    held = jnp.concatenate(held + [jnp.zeros((12, width), f32)], axis=0).astype(bf16)
    rows = iota((16, 128), 0)
    lanes = iota((16, 128), 1)
    place = (((rows < 2) & (lanes == 0)) | ((rows >= 2) & (rows < 4) & (lanes == 127))).astype(bf16)
    return dot_tn(held, place)


def up_x(v):
    return jnp.concatenate([v[:, 1:], jnp.zeros_like(v[:, :1])], axis=1)


def down_x(v):
    return jnp.concatenate([jnp.zeros_like(v[:, :1]), v[:, :-1]], axis=1)


def up_z(v):
    return jnp.concatenate([v[1:], jnp.zeros_like(v[:1])], axis=0)


def down_z(v):
    return jnp.concatenate([jnp.zeros_like(v[:1]), v[:-1]], axis=0)


def up_y(v, halo):
    return jnp.where(iota(v.shape, 2) == 127, halo, pltpu.roll(v, 127, 2))


def down_y(v, first):
    return jnp.where(iota(v.shape, 2) == 0, first, pltpu.roll(v, 1, 2))


def stencil(tx, ty, tz, ty_first, field, halo):
    out = tx * up_x(field) + down_x(tx * field)
    out = out + ty * up_y(field, halo) + down_y(ty * field, ty_first * halo)
    return out + tz * up_z(field) + down_z(tz * field)


def harmonic(first, second):
    both = first + second
    return jnp.where(both > 0.0, 2.0 * first * second / jnp.where(both > 0.0, both, 1.0), 0.0)


def read_faces(me, got_ref, start, width):
    along = me & 15
    before = got_ref[jnp.maximum(me - 1, 0), :, start : start + width]
    after = got_ref[jnp.minimum(me + 1, TILES - 1), :, start : start + width]
    return jnp.where(along > 0, before, 0.0), jnp.where(along < 15, after, 0.0)


def put_faces(me, out_ref, start, first, last):
    width = first.shape[1]
    out_ref[jnp.maximum(me - 1, 0), :, start : start + width] = first
    out_ref[jnp.minimum(me + 1, TILES - 1), :, start : start + width] = last


def edge_codes(delta_ref, to_ref, b):
    block = b + delta_ref[b]
    code = block * 256 + to_ref[b]
    return jnp.where(block < 4, code, -1), jnp.where(block >= 4, code - 1024, -1)


def spread(rows, shift):
    lane = iota(rows.shape, 1)
    inside = (lane >= shift) if shift > 0 else (lane < TILES + shift)
    return jnp.where(inside, pltpu.roll(rows, shift % TILES, 1), 0.0)


def store_slots(out_ref, rows):
    for i in range(0, rows.shape[0], 128):
        out_ref[:, 0, i : i + 128] = rows[i : i + 128].T


def load_slots(got_ref, count):
    return jnp.concatenate([got_ref[:, 0, i : i + 128].T for i in range(0, count, 128)], axis=0)


def begin_kernel(
    me_ref, delta_ref, from_ref, to_ref, trans_ref,
    press_ref, cond_ref, left_ref, right_ref,
    press_frac_ref, follow_ref, accum_ref, chain_ref, mf_ref, fm_ref,
    tile_ref, layer_ref, cell_ref,
    out_ref, seg_ref,
):
    me = me_ref[0]
    code = seg_code()
    owner = fold(tile_ref[...])
    owner_row = as_row(owner)
    hot = owner_hot(owner_row)
    before = (iota((128, 128), 0) < iota((128, 128), 1)).astype(bf16)
    base = jnp.zeros((TILES, 1), f32)
    ranks = []
    for c in range(8):
        part = hot[:, c * 128 : (c + 1) * 128]
        wide = part.astype(f32)
        count = dot_nn(part, before) + base
        ranks.append(jnp.sum(wide * count, axis=0, keepdims=True))
        base = base + jnp.sum(wide, axis=1, keepdims=True)
    rank_row = jnp.concatenate(ranks, axis=1).astype(i32)
    rank = as_rows(rank_row)
    mask = rank_mask(rank_row)

    press = fold(press_frac_ref[...])
    follow = fold(follow_ref[...])
    fm = fold(fm_ref[...])
    mf = fold(mf_ref[...])
    last = code % 256 == 255
    tnext = jnp.where(last, 0.0, fold(chain_ref[...]))
    tprev = pltpu.roll(tnext, 1, 1)
    tprev = jnp.where(iota((8, 128), 1) == 0, pltpu.roll(tprev, 4, 0), tprev)
    diag = fold(accum_ref[...]) + tnext + tprev + fm
    inverse = 1.0 / diag
    partial = diag * press - chain(tnext, press)
    edges = []
    for b in range(4):
        here, there = edge_codes(delta_ref, to_ref, b)
        picked = total(jnp.where(code == here, press, 0.0) + jnp.where(code == there, follow, 0.0))
        at = code == b * 256 + from_ref[b]
        partial = partial - jnp.where(at, trans_ref[b] * picked, 0.0)
    first = inverse * partial
    weight = inverse * fm
    for b in range(4):
        here, there = edge_codes(delta_ref, to_ref, b)
        at = code == b * 256 + from_ref[b]
        edges.append(jnp.full((1, 128), there.astype(f32)))
        place = jnp.where(at, (owner * CAP + rank).astype(f32), 0.0)
        for value in (place, jnp.where(at, trans_ref[b] * first, 0.0), jnp.where(at, trans_ref[b] * weight, 0.0)):
            edges.append(jnp.broadcast_to(total(value), (1, 128)))
    where_cell = (fold(layer_ref[...]) * 1024 + fold(cell_ref[...]) + 1).astype(f32)
    slots = to_slots([where_cell, mf * press, fm * first, fm * weight], hot, mask)
    rows = jnp.concatenate([spread(slots, 16), slots, spread(slots, -16)] + edges + [jnp.zeros((48, 128), f32)], axis=0)
    store_slots(out_ref, rows)
    wide = [
        jnp.concatenate([left_ref[i], ref[...], right_ref[i]], axis=1).reshape(LAYERS * EXT, 128)
        for i, ref in enumerate((press_ref, cond_ref))
    ]
    put_faces(me, out_ref, 256, *faces_of(jnp.concatenate(wide, axis=0)))
    for i, value in enumerate((tnext, inverse, partial, fm, mf, owner.astype(f32), rank.astype(f32))):
        seg_ref[i] = value


def cells_kernel(
    me_ref, well_tile_ref, well_cell_ref, well_rate_ref,
    got_ref, press_ref, cond_ref, accum_ref, left_ref, right_ref,
    out_ref, cells_ref, field_ref, index_ref, edge_ref, res_ref,
):
    me = me_ref[0]
    slots = load_slots(got_ref, 256)
    press, cond, accum = (
        jnp.concatenate([left_ref[i], ref[...], right_ref[i]], axis=1)
        for i, ref in enumerate((press_ref, cond_ref, accum_ref))
    )
    sums = []
    for side in range(3):
        table = slots[side * 64 : side * 64 + 64]
        index = table[:CAP].astype(i32) - 1
        index_ref[side * CAP : side * CAP + CAP] = index
        columns, mask = cell_hot(as_row(index))
        sums.append(scatter([table[16:32], table[32:48], table[48:64]], columns, mask))
        if side == 1:
            own_columns, own_mask = columns, mask
    flow, first, weight = (jnp.concatenate([sums[side][i] for side in range(3)], axis=1) for i in range(3))

    halos = columns_of(*read_faces(me, got_ref, 256, 2 * LAYERS * EXT))
    press_halo = halos[: LAYERS * EXT].reshape(LAYERS, EXT, 128)
    cond_halo = halos[LAYERS * EXT :].reshape(LAYERS, EXT, 128)
    lane = iota((LAYERS, EXT, 128), 2)
    tx = harmonic(cond, up_x(cond))
    ty = harmonic(cond, up_y(cond, cond_halo))
    tz = 0.5 * harmonic(cond, up_z(cond))
    ty_first = jnp.where(lane == 0, harmonic(cond, cond_halo), 0.0)
    diag = accum + tx + down_x(tx) + ty + down_y(ty, ty_first) + tz + down_z(tz)
    inverse = jnp.where(diag > 0.0, 1.0 / jnp.where(diag > 0.0, diag, 1.0), 0.0)

    x0 = ((me >> 4) - 1) * 8
    y0 = (me & 15) * 128
    plane_x = iota((EXT, 128), 0) + x0
    plane_y = iota((EXT, 128), 1) + y0
    source = jnp.zeros((EXT, 128), f32)
    for w in range(well_tile_ref.shape[0]):
        tile = well_tile_ref[w]
        cell = well_cell_ref[w]
        at = (plane_x == (tile >> 4) * 8 + (cell >> 7)) & (plane_y == (tile & 15) * 128 + (cell & 127))
        source = source + jnp.where(at, well_rate_ref[w], 0.0)

    res = diag * press - stencil(tx, ty, tz, ty_first, press, press_halo) - flow - source[None]
    field = inverse * res
    for i, value in enumerate((tx, ty, tz, ty_first, inverse, res, first - weight * press)):
        cells_ref[i] = value
    field_ref[...] = field
    res_ref[...] = res[:, 8:16]
    before = got_ref[jnp.maximum(me - 1, 0), :, 128:256]
    edge_ref[...] = jnp.broadcast_to(jnp.where(me > 0, before, -1.0), (8, 128))

    taken = gather([press_ref[...], field[:, 8:16]], own_columns, own_mask)
    store_slots(out_ref, jnp.concatenate(taken + [spread(taken[0], 1), jnp.zeros((80, 128), f32)], axis=0))
    put_faces(me, out_ref, 128, *faces_of(field.reshape(LAYERS * EXT, 128)))


def edge_in(row, k, i):
    at = 64 + 4 * k + i
    return row[:, at : at + 1]


def step_kernel(
    first, final,
    me_ref, delta_ref, from_ref, to_ref, trans_ref,
    got_ref, cells_ref, field_ref, index_ref, edge_ref, seg_ref, *rest,
):
    me = me_ref[0]
    if not first:
        frac_ref, resf_ref, *rest = rest
    slots = load_slots(got_ref, 128)
    code = seg_code()
    code_f = code.astype(f32)
    tnext, inverse_f, partial, fm, mf, owner, rank = (seg_ref[i] for i in range(7))
    hot = owner_hot(as_row(owner.astype(i32)))
    mask = rank_mask(as_row(rank.astype(i32)))
    edge = edge_ref[0:1]

    if first:
        resf = partial - fm * from_slots(slots[0:16], hot, mask)
        frac = inverse_f * resf
        here = from_slots(slots[16:32], hot, mask)
    else:
        resf = resf_ref[...]
        frac = frac_ref[...]
        here = from_slots(slots[0:16], hot, mask)
    gain = resf + chain(tnext, frac) + mf * here
    for b in range(4):
        target, _ = edge_codes(delta_ref, to_ref, b)
        at = code == b * 256 + from_ref[b]
        term = trans_ref[b] * total(jnp.where(at, frac, 0.0))
        gain = gain + jnp.where(code == target, term, 0.0)
        if first:
            place = (iota((CAP, 128), 1) * CAP + iota((CAP, 128), 0)).astype(f32)
            there = total(jnp.where(place == edge_in(edge, b, 1), slots[32:48], 0.0))
            term = edge_in(edge, b, 2) - edge_in(edge, b, 3) * there
        else:
            term = got_ref[jnp.maximum(me - 1, 0), :, 64 + b : 65 + b]
        gain = gain + jnp.where(code_f == edge_in(edge, b, 0), term, 0.0)
    frac = inverse_f * gain

    tx, ty, tz, ty_first, inverse, res = (cells_ref[i] for i in range(6))
    field = field_ref[...]
    if first:
        flow = cells_ref[6]
        own_columns, own_mask = cell_hot(as_row(index_ref[CAP : 2 * CAP]))
    else:
        flow = []
        for side in range(3):
            columns, rows = cell_hot(as_row(index_ref[side * CAP : side * CAP + CAP]))
            flow.extend(scatter([slots[16 + side * CAP : 32 + side * CAP]], columns, rows))
            if side == 1:
                own_columns, own_mask = columns, rows
        flow = jnp.concatenate(flow, axis=1)
    halo = columns_of(*read_faces(me, got_ref, 128, LAYERS * EXT)).reshape(LAYERS, EXT, 128)
    field = inverse * (res + stencil(tx, ty, tz, ty_first, field, halo) + flow)

    if final:
        adj_matrix_ref, adj_fracture_ref = rest
        adj_matrix_ref[...] = field[:, 8:16]
        adj_fracture_ref[...] = unfold(frac)
        return
    out_ref, new_field_ref, new_frac_ref = rest[:3]
    if first:
        resf_out_ref, res_fracture_ref = rest[3:]
        resf_out_ref[...] = resf
        res_fracture_ref[...] = unfold(resf)
    new_field_ref[...] = field
    new_frac_ref[...] = frac
    taken = gather([field[:, 8:16]], own_columns, own_mask)
    terms = to_slots([fm * frac], hot, mask)
    edges = []
    for b in range(4):
        at = code == b * 256 + from_ref[b]
        edges.append(jnp.broadcast_to(trans_ref[b] * total(jnp.where(at, frac, 0.0)), (1, 128)))
    rows = taken + [spread(terms, 16), terms, spread(terms, -16)] + edges + [jnp.zeros((60, 128), f32)]
    store_slots(out_ref, jnp.concatenate(rows, axis=0))
    put_faces(me, out_ref, 128, *faces_of(field.reshape(LAYERS * EXT, 128)))


def call(kernel, name, scalars, arrays, outs):
    spec = [pl.BlockSpec(memory_space=pltpu.SMEM)] * len(scalars)
    spec += [pl.BlockSpec(memory_space=pltpu.VMEM)] * len(arrays)
    return pl.pallas_call(
        kernel,
        name=name,
        out_shape=[jax.ShapeDtypeStruct(shape, kind) for shape, kind in outs],
        in_specs=spec,
        out_specs=[pl.BlockSpec(memory_space=pltpu.VMEM)] * len(outs),
        compiler_params=pltpu.CompilerParams(vmem_limit_bytes=48 * 1024 * 1024),
    )(*scalars, *arrays)


def exchange(message):
    return lax.all_to_all(message, ALL, split_axis=0, concat_axis=0, tiled=True)


def passed(block, axis, distance):
    count = lax.axis_size(axis)
    return lax.ppermute(block, axis, [(i - distance, i) for i in range(count) if 0 <= i - distance < count])


def body(
    press_matrix, cond_matrix, accum_matrix, press_frac, accum_frac, trans_chain, couple_mf, couple_fm,
    conn_tile, conn_layer, conn_cell, inter_delta, inter_from, inter_to, inter_trans, well_tile, well_cell, well_rate,
):
    me = lax.axis_index(ALL).astype(i32).reshape(1)
    stacked = jnp.stack([press_matrix, cond_matrix, accum_matrix])
    left = passed(stacked, "gx", 1)
    right = passed(stacked, "gx", -1)
    follow = passed(press_frac, ALL, -1)
    edges = (inter_delta, inter_from, inter_to, inter_trans)
    wide = (LAYERS, EXT, 128)
    tile = (LAYERS, 8, 128)
    seg = (8, 128)

    message, segs = call(
        begin_kernel,
        "begin",
        (me, *edges),
        (press_matrix, cond_matrix, left, right, press_frac, follow, accum_frac, trans_chain, couple_mf, couple_fm,
         conn_tile, conn_layer, conn_cell),
        [((TILES, 1, 640), f32), ((7, *seg), f32)],
    )
    got = exchange(message)
    message, cells, field, index, edge, res_matrix = call(
        cells_kernel,
        "cells",
        (me, well_tile, well_cell, well_rate),
        (got, press_matrix, cond_matrix, accum_matrix, left, right),
        [((TILES, 1, 384), f32), ((7, *wide), f32), (wide, f32), ((48, 128), i32), (seg, f32), (tile, f32)],
    )
    got = exchange(message)

    def step(first, final, got, field, more, outs):
        def kernel(*refs):
            step_kernel(first, final, *refs)

        return call(kernel, "step", (me, *edges), (got, cells, field, index, edge, segs, *more), outs)

    going = [((TILES, 1, 384), f32), (wide, f32), (seg, f32)]
    message, field, frac, resf, res_fracture = step(
        True, False, got, field, (), going + [(seg, f32), ((4, 256), f32)]
    )
    for _ in range(ITERS - 3):
        got = exchange(message)
        message, field, frac = step(False, False, got, field, (frac, resf), going)
    got = exchange(message)
    adj_matrix, adj_fracture = step(False, True, got, field, (frac, resf), [(tile, f32), ((4, 256), f32)])
    return res_matrix, res_fracture, adj_matrix, adj_fracture


def solution(mesh):
    cells = P(None, "gx", YA)
    segs = P(ALL, None)
    blocks = P(ALL)
    in_specs = (cells,) * 3 + (segs,) * 8 + (blocks,) * 4 + (P(),) * 3
    return jax.shard_map(body, mesh=mesh, in_specs=in_specs, out_specs=(cells, segs, cells, segs), check_vma=False)
```

profile of v0, /device:TPU:1, one launch (start us, length us, event | category | flops | bytes accessed | tf_op | source)
XLA Modules:
  0.0 161.7 jit_solution(8317524936836338562)
XLA Ops:
  0.7 0.8 pad_maximum_fusion
  1.5 3.3 %collective-permute-start.1 = (f32[3,8,8,128]{3,2,1,0:T(8,128)S(1)}, f32[3,8,8,128]{3,2,1,0:T(8,128)S(1)}, u32[]{:S(2)}, u32[]{:S(2)}) collective-permute-start(f32[3,8,8,128]{3,2,1,0:T(8,128)S(1)} %pad_maximum_fusion), channel_id=1, source_target_pairs={{16,0},{32,16},{48,32},{64,48},{80,64},{96,80},{112,96},{17,1},{33... | collective-permute-start | bytes 294920 | tf_op jit(solution)/shard_map/ppermute | solution.py:441
  4.8 3.2 %collective-permute-start = (f32[3,8,8,128]{3,2,1,0:T(8,128)S(1)}, f32[3,8,8,128]{3,2,1,0:T(8,128)S(1)}, u32[]{:S(2)}, u32[]{:S(2)}) collective-permute-start(f32[3,8,8,128]{3,2,1,0:T(8,128)S(1)} %pad_maximum_fusion), channel_id=1, source_target_pairs={{0,16},{16,32},{32,48},{48,64},{64,80},{80,96},{96,112},{1,17},{17... | collective-permute-start | bytes 294920 | tf_op jit(solution)/shard_map/ppermute | solution.py:441
  8.0 7.1 %collective-permute-start.2 = (f32[4,256]{1,0:T(4,128)S(1)}, f32[4,256]{1,0:T(4,128)S(1)}, u32[]{:S(2)}, u32[]{:S(2)}) collective-permute-start(f32[4,256]{1,0:T(4,128)S(1)} %copy-done.7), channel_id=1, source_target_pairs={{1,0},{2,1},{3,2},{4,3},{5,4},{6,5},{7,6},{8,7},{9,8},{10,9},{11,1... | collective-permute-start | bytes 12296 | tf_op jit(solution)/shard_map/ppermute | solution.py:441
  15.1 0.0 copy-start.13
  15.1 0.0 copy-start.10
  15.2 0.6 collective-permute-done.2.follow_ref
  16.0 1.4 begin.1
  17.4 23.0 %all_to_all.40.got_ref = f32[128,1,640]{2,1,0:T(1,128)S(1)} all-to-all(f32[128,1,640]{2,1,0:T(1,128)S(1)} %get-tuple-element.34), channel_id=1, replica_groups=mesh['gx'=8,'gy'=4,'af'=4] {'gx','gy','af'}, dimensions={0} | all-to-all | bytes 655360 | tf_op jit(solution)/shard_map/all_to_all | solution.py:436
  40.4 3.3 %cells.1 = (f32[128,1,384]{2,1,0:T(1,128)S(1)}, f32[7,8,24,128]{3,2,1,0:T(8,128)S(1)}, f32[8,24,128]{2,1,0:T(8,128)S(1)}, s32[48,128]{1,0:T(8,128)S(1)}, f32[8,128]{1,0:T(8,128)S(1)}, /*index=5*/f32[8,8,128]{2,1,0:T(8,128)}) custom-call(s32[1]{0:T(128)} %bitcast.me_ref.refs_0_, s32[32]{0:T(128)S(1)} %copy-done.15, s32[32]{0:T(128)S(1)} %copy-done.16, ...), custom_call_target="tpu_custom_call" | custom-call | tf_op jit(solution)/shard_map/cells/pallas_call | solution.py:425
  43.7 14.6 %all_to_all.41.refs_5_ = f32[128,1,384]{2,1,0:T(1,128)S(1)} all-to-all(f32[128,1,384]{2,1,0:T(1,128)S(1)} %get-tuple-element.36), channel_id=1, replica_groups=mesh['gx'=8,'gy'=4,'af'=4] {'gx','gy','af'}, dimensions={0} | all-to-all | bytes 393216 | tf_op jit(solution)/shard_map/all_to_all | solution.py:436
  58.3 2.4 %step.7 = (f32[128,1,384]{2,1,0:T(1,128)S(1)}, f32[8,24,128]{2,1,0:T(8,128)S(1)}, f32[8,128]{1,0:T(8,128)S(1)}, f32[8,128]{1,0:T(8,128)S(1)}, f32[4,256]{1,0:T(4,128)}) custom-call(s32[1]{0:T(128)} %bitcast.me_ref.refs_0_, s32[4]{0:T(128)S(1)} %copy-done.3, s32[4]{0:T(128)S(1)} %copy-done.4, s32[4]{0:T(128)S(1)} %copy-done.5, f32[4]{0:T(128)S(1)} %copy-done.6, ...), custom_call_target="tpu_custom_call" | custom-call | tf_op jit(solution)/shard_map/step/pallas_call | solution.py:425
  60.6 14.6 %all_to_all.42.refs_5_ = f32[128,1,384]{2,1,0:T(1,128)S(1)} all-to-all(f32[128,1,384]{2,1,0:T(1,128)S(1)} %get-tuple-element.43), channel_id=1, replica_groups=mesh['gx'=8,'gy'=4,'af'=4] {'gx','gy','af'}, dimensions={0} | all-to-all | bytes 393216 | tf_op jit(solution)/shard_map/all_to_all | solution.py:436
  75.2 2.3 %step.8 = (f32[128,1,384]{2,1,0:T(1,128)S(1)}, f32[8,24,128]{2,1,0:T(8,128)S(1)}, f32[8,128]{1,0:T(8,128)S(1)}) custom-call(s32[1]{0:T(128)} %bitcast.me_ref.refs_0_, s32[4]{0:T(128)S(1)} %copy-done.3, s32[4]{0:T(128)S(1)} %copy-done.4, s32[4]{0:T(128)S(1)} %copy-done.5, f32[4]{0:T(128)S(1)} %copy-done.6, f32[128,1,384]{2,1,0:T(1,128)S(1)} %all_to_all.42.refs_5_, ...), custom_call_target="tpu_custom_call" | custom-call | tf_op jit(solution)/shard_map/step/pallas_call | solution.py:425
  77.6 14.6 %all_to_all.43.refs_5_ = f32[128,1,384]{2,1,0:T(1,128)S(1)} all-to-all(f32[128,1,384]{2,1,0:T(1,128)S(1)} %get-tuple-element.47), channel_id=1, replica_groups=mesh['gx'=8,'gy'=4,'af'=4] {'gx','gy','af'}, dimensions={0} | all-to-all | bytes 393216 | tf_op jit(solution)/shard_map/all_to_all | solution.py:436
  92.2 2.3 %step.9 = (f32[128,1,384]{2,1,0:T(1,128)S(1)}, f32[8,24,128]{2,1,0:T(8,128)S(1)}, f32[8,128]{1,0:T(8,128)S(1)}) custom-call(s32[1]{0:T(128)} %bitcast.me_ref.refs_0_, s32[4]{0:T(128)S(1)} %copy-done.3, s32[4]{0:T(128)S(1)} %copy-done.4, s32[4]{0:T(128)S(1)} %copy-done.5, f32[4]{0:T(128)S(1)} %copy-done.6, f32[128,1,384]{2,1,0:T(1,128)S(1)} %all_to_all.43.refs_5_, ...), custom_call_target="tpu_custom_call" | custom-call | tf_op jit(solution)/shard_map/step/pallas_call | solution.py:425
  94.5 14.6 %all_to_all.44.refs_5_ = f32[128,1,384]{2,1,0:T(1,128)S(1)} all-to-all(f32[128,1,384]{2,1,0:T(1,128)S(1)} %get-tuple-element.50), channel_id=1, replica_groups=mesh['gx'=8,'gy'=4,'af'=4] {'gx','gy','af'}, dimensions={0} | all-to-all | bytes 393216 | tf_op jit(solution)/shard_map/all_to_all | solution.py:436
  109.1 2.3 %step.10 = (f32[128,1,384]{2,1,0:T(1,128)S(1)}, f32[8,24,128]{2,1,0:T(8,128)S(1)}, f32[8,128]{1,0:T(8,128)S(1)}) custom-call(s32[1]{0:T(128)} %bitcast.me_ref.refs_0_, s32[4]{0:T(128)S(1)} %copy-done.3, s32[4]{0:T(128)S(1)} %copy-done.4, s32[4]{0:T(128)S(1)} %copy-done.5, f32[4]{0:T(128)S(1)} %copy-done.6, f32[128,1,384]{2,1,0:T(1,128)S(1)} %all_to_all.44.refs_5_, ...), custom_call_target="tpu_custom_call" | custom-call | tf_op jit(solution)/shard_map/step/pallas_call | solution.py:425
  111.4 14.6 %all_to_all.45.refs_5_ = f32[128,1,384]{2,1,0:T(1,128)S(1)} all-to-all(f32[128,1,384]{2,1,0:T(1,128)S(1)} %get-tuple-element.53), channel_id=1, replica_groups=mesh['gx'=8,'gy'=4,'af'=4] {'gx','gy','af'}, dimensions={0} | all-to-all | bytes 393216 | tf_op jit(solution)/shard_map/all_to_all | solution.py:436
  126.0 2.3 %step.11 = (f32[128,1,384]{2,1,0:T(1,128)S(1)}, f32[8,24,128]{2,1,0:T(8,128)S(1)}, f32[8,128]{1,0:T(8,128)S(1)}) custom-call(s32[1]{0:T(128)} %bitcast.me_ref.refs_0_, s32[4]{0:T(128)S(1)} %copy-done.3, s32[4]{0:T(128)S(1)} %copy-done.4, s32[4]{0:T(128)S(1)} %copy-done.5, f32[4]{0:T(128)S(1)} %copy-done.6, f32[128,1,384]{2,1,0:T(1,128)S(1)} %all_to_all.45.refs_5_, ...), custom_call_target="tpu_custom_call" | custom-call | tf_op jit(solution)/shard_map/step/pallas_call | solution.py:425
  128.4 14.6 %all_to_all.46.refs_5_ = f32[128,1,384]{2,1,0:T(1,128)S(1)} all-to-all(f32[128,1,384]{2,1,0:T(1,128)S(1)} %get-tuple-element.56), channel_id=1, replica_groups=mesh['gx'=8,'gy'=4,'af'=4] {'gx','gy','af'}, dimensions={0} | all-to-all | bytes 393216 | tf_op jit(solution)/shard_map/all_to_all | solution.py:436
  143.0 2.3 %step.12 = (f32[128,1,384]{2,1,0:T(1,128)S(1)}, f32[8,24,128]{2,1,0:T(8,128)S(1)}, f32[8,128]{1,0:T(8,128)S(1)}) custom-call(s32[1]{0:T(128)} %bitcast.me_ref.refs_0_, s32[4]{0:T(128)S(1)} %copy-done.3, s32[4]{0:T(128)S(1)} %copy-done.4, s32[4]{0:T(128)S(1)} %copy-done.5, f32[4]{0:T(128)S(1)} %copy-done.6, f32[128,1,384]{2,1,0:T(1,128)S(1)} %all_to_all.46.refs_5_, ...), custom_call_target="tpu_custom_call" | custom-call | tf_op jit(solution)/shard_map/step/pallas_call | solution.py:425
  145.3 14.6 %all_to_all.47.refs_5_ = f32[128,1,384]{2,1,0:T(1,128)S(1)} all-to-all(f32[128,1,384]{2,1,0:T(1,128)S(1)} %get-tuple-element.59), channel_id=1, replica_groups=mesh['gx'=8,'gy'=4,'af'=4] {'gx','gy','af'}, dimensions={0} | all-to-all | bytes 393216 | tf_op jit(solution)/shard_map/all_to_all | solution.py:436
  159.9 1.7 %step.13 = (f32[8,8,128]{2,1,0:T(8,128)}, f32[4,256]{1,0:T(4,128)}) custom-call(s32[1]{0:T(128)} %bitcast.me_ref.refs_0_, s32[4]{0:T(128)S(1)} %copy-done.3, s32[4]{0:T(128)S(1)} %copy-done.4, s32[4]{0:T(128)S(1)} %copy-done.5, f32[4]{0:T(128)S(1)} %copy-done.6, f32[128,1,384]{2,1,0:T(1,128)S(1)} %all_to_all.47.refs_5_, ...), custom_call_target="tpu_custom_call" | custom-call | tf_op jit(solution)/shard_map/step/pallas_call | solution.py:425
  (36 shorter events, 0.1 us)
Async XLA Ops:
  0.6 7.4 %copy-start.7 = (f32[4,256]{1,0:T(4,128)S(1)}, f32[4,256]{1,0:T(4,128)}, u32[]{:S(2)}) copy-start(f32[4,256]{1,0:T(4,128)} %press_frac_ref.1) | copy-start | bytes 12292
  0.6 15.2 %copy-start = (f32[8,8,128]{2,1,0:T(8,128)S(1)}, f32[8,8,128]{2,1,0:T(8,128)}, u32[]{:S(2)}) copy-start(f32[8,8,128]{2,1,0:T(8,128)} %press_ref.3) | copy-start | bytes 98308
  0.7 15.2 %copy-start.1 = (f32[8,8,128]{2,1,0:T(8,128)S(1)}, f32[8,8,128]{2,1,0:T(8,128)}, u32[]{:S(2)}) copy-start(f32[8,8,128]{2,1,0:T(8,128)} %cond_ref.3) | copy-start | bytes 98308
  0.7 15.2 %copy-start.14 = (s32[4,256]{1,0:T(4,128)S(1)}, s32[4,256]{1,0:T(4,128)}, u32[]{:S(2)}) copy-start(s32[4,256]{1,0:T(4,128)} %cell_ref.1) | copy-start | bytes 12292
  1.5 14.3 %collective-permute-start.1 = (f32[3,8,8,128]{3,2,1,0:T(8,128)S(1)}, f32[3,8,8,128]{3,2,1,0:T(8,128)S(1)}, u32[]{:S(2)}, u32[]{:S(2)}) collective-permute-start(f32[3,8,8,128]{3,2,1,0:T(8,128)S(1)} %pad_maximum_fusion), channel_id=1, source_target_pairs={{16,0},{32,16},{48,32},{64,48},{80,64},{96,80},{112,96},{17,1},{33... | collective-permute-start | bytes 294920 | tf_op jit(solution)/shard_map/ppermute | solution.py:441
  4.8 11.0 %collective-permute-start = (f32[3,8,8,128]{3,2,1,0:T(8,128)S(1)}, f32[3,8,8,128]{3,2,1,0:T(8,128)S(1)}, u32[]{:S(2)}, u32[]{:S(2)}) collective-permute-start(f32[3,8,8,128]{3,2,1,0:T(8,128)S(1)} %pad_maximum_fusion), channel_id=1, source_target_pairs={{0,16},{16,32},{32,48},{48,64},{64,80},{80,96},{96,112},{1,17},{17... | collective-permute-start | bytes 294920 | tf_op jit(solution)/shard_map/ppermute | solution.py:441
  8.0 7.8 %collective-permute-start.2 = (f32[4,256]{1,0:T(4,128)S(1)}, f32[4,256]{1,0:T(4,128)S(1)}, u32[]{:S(2)}, u32[]{:S(2)}) collective-permute-start(f32[4,256]{1,0:T(4,128)S(1)} %copy-done.7), channel_id=1, source_target_pairs={{1,0},{2,1},{3,2},{4,3},{5,4},{6,5},{7,6},{8,7},{9,8},{10,9},{11,1... | collective-permute-start | bytes 12296 | tf_op jit(solution)/shard_map/ppermute | solution.py:441
  15.1 0.8 copy-start.13
  15.1 0.8 copy-start.12
  15.1 0.8 copy-start.11
  15.1 0.8 copy-start.10
  15.1 0.8 copy-start.9
  15.2 0.8 copy-start.8
  15.2 0.7 copy-start.6
  15.2 0.7 copy-start.3
  15.2 0.7 copy-start.4
  15.2 0.7 copy-start.5
  17.3 23.1 %copy-start.2 = (f32[8,8,128]{2,1,0:T(8,128)S(1)}, f32[8,8,128]{2,1,0:T(8,128)}, u32[]{:S(2)}) copy-start(f32[8,8,128]{2,1,0:T(8,128)} %accum_ref.3) | copy-start | bytes 98308
  17.3 23.0 %copy-start.15 = (s32[32]{0:T(128)S(1)}, s32[32]{0:T(128)}, u32[]{:S(2)}) copy-start(s32[32]{0:T(128)} %well_tile_ref.1) | copy-start | bytes 388
  17.3 23.0 %copy-start.16 = (s32[32]{0:T(128)S(1)}, s32[32]{0:T(128)}, u32[]{:S(2)}) copy-start(s32[32]{0:T(128)} %well_cell_ref.1) | copy-start | bytes 388
  17.4 23.0 %copy-start.17 = (f32[32]{0:T(128)S(1)}, f32[32]{0:T(128)}, u32[]{:S(2)}) copy-start(f32[32]{0:T(128)} %well_rate_ref.1) | copy-start | bytes 388
where the time goes:
time: 162 us
  blocking collectives  125 us (77%)
  Pallas kernels  20.3 us (13%)
  starting transfers between devices  13.6 us (8%)
    all_to_all x8, blocking collectives, exchange(): return lax.all_to_all(message, ALL, split_axis=0, concat_axis=0, tiled=True)  125 us
    pallas_call x9, Pallas kernels, call(): pl.pallas_call(kernel, name=name, out_shape=[jax.ShapeDtypeStruct(shape,...  20.3 us
    ppermute x3, starting transfers between devices, passed(): lax.ppermute(block, axis, [(i - distance, i) for i in range(count) if 0 <...  13.6 us
  transfers between devices with their start and end apart: 3, of which 1 were waited for; matrix products, arithmetic and copies ran while one was open for 0% of the time, Pallas kernels for 0%

commit v1 on v0

--- a/solution.py
+++ b/solution.py
@@ -99,8 +99,9 @@
 
 
 def cell_hot(index_row):
-    columns = (iota((128, SLOTS), 0) == (index_row & 127)).astype(bf16)
-    return columns, iota((ROWS, SLOTS), 0) == (index_row >> 7)
+    count = index_row.shape[1]
+    columns = (iota((128, count), 0) == (index_row & 127)).astype(bf16)
+    return columns, iota((ROWS, count), 0) == (index_row >> 7)
 
 
 def scatter(tables, columns, mask):
@@ -180,17 +181,19 @@
     return jnp.where(both > 0.0, 2.0 * first * second / jnp.where(both > 0.0, both, 1.0), 0.0)
 
 
-def read_faces(me, got_ref, start, width):
+def read_faces(me, got_ref, start, width, across=0):
     along = me & 15
-    before = got_ref[jnp.maximum(me - 1, 0), :, start : start + width]
-    after = got_ref[jnp.minimum(me + 1, TILES - 1), :, start : start + width]
-    return jnp.where(along > 0, before, 0.0), jnp.where(along < 15, after, 0.0)
-
-
-def put_faces(me, out_ref, start, first, last):
+    line = (me >> 4) + across // 16
+    inside = (line >= 0) & (line < 8)
+    before = got_ref[jnp.clip(me + across - 1, 0, TILES - 1), :, start : start + width]
+    after = got_ref[jnp.clip(me + across + 1, 0, TILES - 1), :, start : start + width]
+    return jnp.where(inside & (along > 0), before, 0.0), jnp.where(inside & (along < 15), after, 0.0)
+
+
+def put_faces(me, out_ref, start, first, last, across=0):
     width = first.shape[1]
-    out_ref[jnp.maximum(me - 1, 0), :, start : start + width] = first
-    out_ref[jnp.minimum(me + 1, TILES - 1), :, start : start + width] = last
+    for at, face in ((me + across - 1, first), (me + across + 1, last)):
+        out_ref[jnp.where((at >= 0) & (at < TILES), at, me), :, start : start + width] = face
 
 
 def edge_codes(delta_ref, to_ref, b):
@@ -207,20 +210,22 @@
 
 def store_slots(out_ref, rows):
     for i in range(0, rows.shape[0], 128):
-        out_ref[:, 0, i : i + 128] = rows[i : i + 128].T
+        part = rows[i : i + 128].T
+        out_ref[:, 0, i : i + part.shape[1]] = part
 
 
 def load_slots(got_ref, count):
     return jnp.concatenate([got_ref[:, 0, i : i + 128].T for i in range(0, count, 128)], axis=0)
 
 
-def begin_kernel(
-    me_ref, delta_ref, from_ref, to_ref, trans_ref,
-    press_ref, cond_ref, left_ref, right_ref,
-    press_frac_ref, follow_ref, accum_ref, chain_ref, mf_ref, fm_ref,
-    tile_ref, layer_ref, cell_ref,
-    out_ref, seg_ref,
-):
+def begin_kernel(me_ref, delta_ref, from_ref, to_ref, trans_ref, *refs):
+    given, (out_ref, seg_ref), held, sems = refs[:10], refs[10:12], refs[12:22], refs[22]
+    copies = [pltpu.make_async_copy(a, b, sems.at[i]) for i, (a, b) in enumerate(zip(given, held))]
+    for copy in copies:
+        copy.start()
+    for copy in copies:
+        copy.wait()
+    tile_ref, layer_ref, cell_ref, press_frac_ref, accum_ref, chain_ref, mf_ref, fm_ref, press_ref, cond_ref = held
     me = me_ref[0]
     code = seg_code()
     owner = fold(tile_ref[...])
@@ -240,7 +245,6 @@
     mask = rank_mask(rank_row)
 
     press = fold(press_frac_ref[...])
-    follow = fold(follow_ref[...])
     fm = fold(fm_ref[...])
     mf = fold(mf_ref[...])
     last = code % 256 == 255
@@ -250,37 +254,40 @@
     diag = fold(accum_ref[...]) + tnext + tprev + fm
     inverse = 1.0 / diag
     partial = diag * press - chain(tnext, press)
+    for b in range(4):
+        here, _ = edge_codes(delta_ref, to_ref, b)
+        at = code == b * 256 + from_ref[b]
+        partial = partial - jnp.where(at, trans_ref[b] * total(jnp.where(code == here, press, 0.0)), 0.0)
+    where_cell = (fold(layer_ref[...]) * 1024 + fold(cell_ref[...]) + 1).astype(f32)
+    slots = to_slots([where_cell, mf * press, fm * inverse * fm], hot, mask)
+    place = (owner * CAP + rank).astype(f32)
     edges = []
     for b in range(4):
-        here, there = edge_codes(delta_ref, to_ref, b)
-        picked = total(jnp.where(code == here, press, 0.0) + jnp.where(code == there, follow, 0.0))
+        _, there = edge_codes(delta_ref, to_ref, b)
         at = code == b * 256 + from_ref[b]
-        partial = partial - jnp.where(at, trans_ref[b] * picked, 0.0)
-    first = inverse * partial
-    weight = inverse * fm
-    for b in range(4):
-        here, there = edge_codes(delta_ref, to_ref, b)
-        at = code == b * 256 + from_ref[b]
+        gain = trans_ref[b] * inverse
         edges.append(jnp.full((1, 128), there.astype(f32)))
-        place = jnp.where(at, (owner * CAP + rank).astype(f32), 0.0)
-        for value in (place, jnp.where(at, trans_ref[b] * first, 0.0), jnp.where(at, trans_ref[b] * weight, 0.0)):
-            edges.append(jnp.broadcast_to(total(value), (1, 128)))
-    where_cell = (fold(layer_ref[...]) * 1024 + fold(cell_ref[...]) + 1).astype(f32)
-    slots = to_slots([where_cell, mf * press, fm * first, fm * weight], hot, mask)
-    rows = jnp.concatenate([spread(slots, 16), slots, spread(slots, -16)] + edges + [jnp.zeros((48, 128), f32)], axis=0)
-    store_slots(out_ref, rows)
-    wide = [
-        jnp.concatenate([left_ref[i], ref[...], right_ref[i]], axis=1).reshape(LAYERS * EXT, 128)
-        for i, ref in enumerate((press_ref, cond_ref))
-    ]
-    put_faces(me, out_ref, 256, *faces_of(jnp.concatenate(wide, axis=0)))
-    for i, value in enumerate((tnext, inverse, partial, fm, mf, owner.astype(f32), rank.astype(f32))):
+        for value in (place, where_cell, gain * fm, gain * partial, gain * trans_ref[b]):
+            edges.append(jnp.broadcast_to(total(jnp.where(at, value, 0.0)), (1, 128)))
+        edges.append(jnp.full((1, 128), trans_ref[b]))
+        edges.append(jnp.zeros((1, 128), f32))
+    rows = [spread(slots, 16), slots, spread(slots, -16)] + edges + [jnp.zeros((80, 128), f32)]
+    store_slots(out_ref, jnp.concatenate(rows, axis=0))
+    first_face, last_face = faces_of(jnp.concatenate([press_ref[...].reshape(ROWS, 128), cond_ref[...].reshape(ROWS, 128)], axis=0))
+    for across in (-16, 0, 16):
+        put_faces(me, out_ref, 256, first_face, last_face, across)
+    for i, value in enumerate((tnext, inverse, partial, fm, mf, owner.astype(f32), rank.astype(f32), press)):
         seg_ref[i] = value
+
+
+def edge_in(row, k, i):
+    at = 16 + 8 * k + i
+    return row[:, at : at + 1]
 
 
 def cells_kernel(
     me_ref, well_tile_ref, well_cell_ref, well_rate_ref,
-    got_ref, press_ref, cond_ref, accum_ref, left_ref, right_ref,
+    got_ref, press_ref, cond_ref, accum_ref, left_ref, right_ref, seg_ref,
     out_ref, cells_ref, field_ref, index_ref, edge_ref, res_ref,
 ):
     me = me_ref[0]
@@ -291,18 +298,18 @@
     )
     sums = []
     for side in range(3):
-        table = slots[side * 64 : side * 64 + 64]
+        table = slots[side * 48 : side * 48 + 48]
         index = table[:CAP].astype(i32) - 1
         index_ref[side * CAP : side * CAP + CAP] = index
         columns, mask = cell_hot(as_row(index))
-        sums.append(scatter([table[16:32], table[32:48], table[48:64]], columns, mask))
+        sums.append(scatter([table[16:32], table[32:48]], columns, mask))
         if side == 1:
             own_columns, own_mask = columns, mask
-    flow, first, weight = (jnp.concatenate([sums[side][i] for side in range(3)], axis=1) for i in range(3))
-
-    halos = columns_of(*read_faces(me, got_ref, 256, 2 * LAYERS * EXT))
-    press_halo = halos[: LAYERS * EXT].reshape(LAYERS, EXT, 128)
-    cond_halo = halos[LAYERS * EXT :].reshape(LAYERS, EXT, 128)
+    flow, weight = (jnp.concatenate([sums[side][i] for side in range(3)], axis=1) for i in range(2))
+
+    halos = [columns_of(*read_faces(me, got_ref, 256, 2 * ROWS, across)) for across in (-16, 0, 16)]
+    press_halo = jnp.concatenate([halo[:ROWS].reshape(LAYERS, 8, 128) for halo in halos], axis=1)
+    cond_halo = jnp.concatenate([halo[ROWS:].reshape(LAYERS, 8, 128) for halo in halos], axis=1)
     lane = iota((LAYERS, EXT, 128), 2)
     tx = harmonic(cond, up_x(cond))
     ty = harmonic(cond, up_y(cond, cond_halo))
@@ -324,27 +331,40 @@
 
     res = diag * press - stencil(tx, ty, tz, ty_first, press, press_halo) - flow - source[None]
     field = inverse * res
-    for i, value in enumerate((tx, ty, tz, ty_first, inverse, res, first - weight * press)):
+    for i, value in enumerate((tx, ty, tz, ty_first, inverse, res, weight * press)):
         cells_ref[i] = value
     field_ref[...] = field
     res_ref[...] = res[:, 8:16]
-    before = got_ref[jnp.maximum(me - 1, 0), :, 128:256]
-    edge_ref[...] = jnp.broadcast_to(jnp.where(me > 0, before, -1.0), (8, 128))
+
+    code = seg_code().astype(f32)
+    _, inverse_f, partial, fm, _, owner, rank, press_f = (seg_ref[i] for i in range(8))
+    edge = jnp.where(me > 0, got_ref[jnp.maximum(me - 1, 0), :, 128:256], -1.0)
+    lane = iota((1, 128), 1)
+    cells, terms, picks = [], [], []
+    for k in range(4):
+        there = edge_in(edge, k, 0)
+        picked = total(jnp.where(code == there, press_f, 0.0))
+        at = (lane == (edge_in(edge, k, 1).astype(i32) >> 4)) & (there >= 0.0)
+        cells.append(jnp.where(at, edge_in(edge, k, 2), 0.0))
+        terms.append(jnp.where(at, -edge_in(edge, k, 3) * picked, 0.0))
+        picks.append(jnp.broadcast_to(picked, (1, 128)))
+        edge = jnp.where(lane == 16 + 8 * k + 4, edge - edge_in(edge, k, 5) * picked, edge)
+    edge_ref[...] = jnp.broadcast_to(edge, (8, 128))
+    late = jnp.concatenate(cells + terms, axis=0)
+    hot = owner_hot(as_row(owner.astype(i32)))
+    first = to_slots([fm * inverse_f * partial], hot, rank_mask(as_row(rank.astype(i32))))
 
     taken = gather([press_ref[...], field[:, 8:16]], own_columns, own_mask)
-    store_slots(out_ref, jnp.concatenate(taken + [spread(taken[0], 1), jnp.zeros((80, 128), f32)], axis=0))
+    rows = taken + [spread(taken[0], 1)]
+    rows += [spread(first, 16), first, spread(first, -16), spread(late, 16), late, spread(late, -16)]
+    store_slots(out_ref, jnp.concatenate(rows + picks + [jnp.zeros((4, 128), f32)], axis=0))
     put_faces(me, out_ref, 128, *faces_of(field.reshape(LAYERS * EXT, 128)))
-
-
-def edge_in(row, k, i):
-    at = 64 + 4 * k + i
-    return row[:, at : at + 1]
 
 
 def step_kernel(
     first, final,
     me_ref, delta_ref, from_ref, to_ref, trans_ref,
-    got_ref, cells_ref, field_ref, index_ref, edge_ref, seg_ref, *rest,
+    got_ref, cells_ref, field_ref, index_ref, seg_ref, edge_ref, *rest,
 ):
     me = me_ref[0]
     if not first:
@@ -359,6 +379,11 @@
 
     if first:
         resf = partial - fm * from_slots(slots[0:16], hot, mask)
+        after = got_ref[jnp.minimum(me + 1, TILES - 1), :, 0:128]
+        for b in range(4):
+            _, there = edge_codes(delta_ref, to_ref, b)
+            at = (code == b * 256 + from_ref[b]) & (there >= 0)
+            resf = resf - jnp.where(at, trans_ref[b] * after[:, 120 + b : 121 + b], 0.0)
         frac = inverse_f * resf
         here = from_slots(slots[16:32], hot, mask)
     else:
@@ -366,6 +391,7 @@
         frac = frac_ref[...]
         here = from_slots(slots[0:16], hot, mask)
     gain = resf + chain(tnext, frac) + mf * here
+    before = got_ref[jnp.maximum(me - 1, 0), :, 64:256]
     for b in range(4):
         target, _ = edge_codes(delta_ref, to_ref, b)
         at = code == b * 256 + from_ref[b]
@@ -374,26 +400,31 @@
         if first:
             place = (iota((CAP, 128), 1) * CAP + iota((CAP, 128), 0)).astype(f32)
             there = total(jnp.where(place == edge_in(edge, b, 1), slots[32:48], 0.0))
-            term = edge_in(edge, b, 2) - edge_in(edge, b, 3) * there
+            term = edge_in(edge, b, 4) - edge_in(edge, b, 3) * there
         else:
-            term = got_ref[jnp.maximum(me - 1, 0), :, 64 + b : 65 + b]
+            term = before[:, EXT * b : EXT * b + 1]
         gain = gain + jnp.where(code_f == edge_in(edge, b, 0), term, 0.0)
     frac = inverse_f * gain
 
     tx, ty, tz, ty_first, inverse, res = (cells_ref[i] for i in range(6))
     field = field_ref[...]
+    flow = []
+    for side in range(3):
+        index = index_ref[side * CAP : side * CAP + CAP]
+        if first:
+            late = slots[96 + 8 * side : 104 + 8 * side]
+            index = jnp.concatenate([index, late[:4].astype(i32) - 1], axis=0)
+            table = jnp.concatenate([slots[48 + side * CAP : 64 + side * CAP], late[4:]], axis=0)
+        else:
+            table = slots[16 + side * CAP : 32 + side * CAP]
+        columns, rows = cell_hot(as_row(index))
+        flow.extend(scatter([table], columns, rows))
+        if side == 1:
+            own_columns, own_mask = columns[:, :SLOTS], rows[:, :SLOTS]
+    flow = jnp.concatenate(flow, axis=1)
     if first:
-        flow = cells_ref[6]
-        own_columns, own_mask = cell_hot(as_row(index_ref[CAP : 2 * CAP]))
-    else:
-        flow = []
-        for side in range(3):
-            columns, rows = cell_hot(as_row(index_ref[side * CAP : side * CAP + CAP]))
-            flow.extend(scatter([slots[16 + side * CAP : 32 + side * CAP]], columns, rows))
-            if side == 1:
-                own_columns, own_mask = columns, rows
-        flow = jnp.concatenate(flow, axis=1)
-    halo = columns_of(*read_faces(me, got_ref, 128, LAYERS * EXT)).reshape(LAYERS, EXT, 128)
+        flow = flow - cells_ref[6]
+    halo = columns_of(*read_faces(me, got_ref, 128 if first else 64, LAYERS * EXT)).reshape(LAYERS, EXT, 128)
     field = inverse * (res + stencil(tx, ty, tz, ty_first, field, halo) + flow)
 
     if final:
@@ -410,25 +441,26 @@
     new_frac_ref[...] = frac
     taken = gather([field[:, 8:16]], own_columns, own_mask)
     terms = to_slots([fm * frac], hot, mask)
-    edges = []
+    store_slots(out_ref, jnp.concatenate(taken + [spread(terms, 16), terms, spread(terms, -16)], axis=0))
+    begin, end = faces_of(field.reshape(LAYERS * EXT, 128))
+    lane = iota(end.shape, 1)
     for b in range(4):
         at = code == b * 256 + from_ref[b]
-        edges.append(jnp.broadcast_to(trans_ref[b] * total(jnp.where(at, frac, 0.0)), (1, 128)))
-    rows = taken + [spread(terms, 16), terms, spread(terms, -16)] + edges + [jnp.zeros((60, 128), f32)]
-    store_slots(out_ref, jnp.concatenate(rows, axis=0))
-    put_faces(me, out_ref, 128, *faces_of(field.reshape(LAYERS * EXT, 128)))
-
-
-def call(kernel, name, scalars, arrays, outs):
+        end = jnp.where(lane == EXT * b, trans_ref[b] * total(jnp.where(at, frac, 0.0)), end)
+    put_faces(me, out_ref, 64, begin, end)
+
+
+def call(kernel, name, scalars, arrays, outs, space=pltpu.VMEM, scratch=(), limit=48 * 1024 * 1024):
     spec = [pl.BlockSpec(memory_space=pltpu.SMEM)] * len(scalars)
-    spec += [pl.BlockSpec(memory_space=pltpu.VMEM)] * len(arrays)
+    spec += [pl.BlockSpec(memory_space=space)] * len(arrays)
     return pl.pallas_call(
         kernel,
         name=name,
         out_shape=[jax.ShapeDtypeStruct(shape, kind) for shape, kind in outs],
         in_specs=spec,
         out_specs=[pl.BlockSpec(memory_space=pltpu.VMEM)] * len(outs),
-        compiler_params=pltpu.CompilerParams(vmem_limit_bytes=48 * 1024 * 1024),
+        scratch_shapes=list(scratch),
+        compiler_params=pltpu.CompilerParams(vmem_limit_bytes=limit),
     )(*scalars, *arrays)
 
 
@@ -449,26 +481,28 @@
     stacked = jnp.stack([press_matrix, cond_matrix, accum_matrix])
     left = passed(stacked, "gx", 1)
     right = passed(stacked, "gx", -1)
-    follow = passed(press_frac, ALL, -1)
     edges = (inter_delta, inter_from, inter_to, inter_trans)
     wide = (LAYERS, EXT, 128)
     tile = (LAYERS, 8, 128)
     seg = (8, 128)
 
+    given = (conn_tile, conn_layer, conn_cell, press_frac, accum_frac, trans_chain, couple_mf, couple_fm, press_matrix, cond_matrix)
     message, segs = call(
         begin_kernel,
         "begin",
         (me, *edges),
-        (press_matrix, cond_matrix, left, right, press_frac, follow, accum_frac, trans_chain, couple_mf, couple_fm,
-         conn_tile, conn_layer, conn_cell),
-        [((TILES, 1, 640), f32), ((7, *seg), f32)],
+        given,
+        [((TILES, 1, 384), f32), ((8, *seg), f32)],
+        pl.ANY,
+        [pltpu.VMEM(a.shape, a.dtype) for a in given] + [pltpu.SemaphoreType.DMA((len(given),))],
+        64 * 1024 * 1024,
     )
     got = exchange(message)
     message, cells, field, index, edge, res_matrix = call(
         cells_kernel,
         "cells",
         (me, well_tile, well_cell, well_rate),
-        (got, press_matrix, cond_matrix, accum_matrix, left, right),
+        (got, press_matrix, cond_matrix, accum_matrix, left, right, segs),
         [((TILES, 1, 384), f32), ((7, *wide), f32), (wide, f32), ((48, 128), i32), (seg, f32), (tile, f32)],
     )
     got = exchange(message)
@@ -477,9 +511,9 @@
         def kernel(*refs):
             step_kernel(first, final, *refs)
 
-        return call(kernel, "step", (me, *edges), (got, cells, field, index, edge, segs, *more), outs)
-
-    going = [((TILES, 1, 384), f32), (wide, f32), (seg, f32)]
+        return call(kernel, "step", (me, *edges), (got, cells, field, index, segs, edge, *more), outs)
+
+    going = [((TILES, 1, 256), f32), (wide, f32), (seg, f32)]
     message, field, frac, resf, res_fracture = step(
         True, False, got, field, (), going + [(seg, f32), ((4, 256), f32)]
     )

time: 162 us -> 149 us (0.920)
  blocking collectives: 125 us -> 103 us
  waiting for transfers between devices: 0.61 us -> 5 us
  starting transfers between devices: 13.6 us -> 17.2 us
    all_to_all x8 -> x7, blocking collectives: 125 us -> 103 us  [exchange(): return lax.all_to_all(message, ALL, split_axis=0, concat_axis=0, tiled=True)]
    all_to_all x0 -> x1, starting transfers between devices: none -> 11.5 us  [exchange(): return lax.all_to_all(message, ALL, split_axis=0, concat_axis=0, tiled=True)]
    ppermute x3 -> x2, starting transfers between devices: 13.6 us -> 5.69 us  [passed(): lax.ppermute(block, axis, [(i - distance, i) for i in range(count) if 0 <...]
    all_to_all x0 -> x1, waiting for transfers between devices: none -> 3.38 us  [exchange(): return lax.all_to_all(message, ALL, split_axis=0, concat_axis=0, tiled=True)]
  transfers between devices with their start and end apart: 3 -> 3, of which waited for: 1 -> 3; matrix products, arithmetic and copies ran while one was open for 0% -> 0% of each run, Pallas kernels for 0% -> 0%
where the time goes in v1:
time: 149 us
  blocking collectives  103 us (69%)
  Pallas kernels  21.8 us (15%)
  starting transfers between devices  17.2 us (12%)
  waiting for transfers between devices  5 us (3%)
    all_to_all x7, blocking collectives, exchange(): return lax.all_to_all(message, ALL, split_axis=0, concat_axis=0, tiled=True)  103 us
    pallas_call x9, Pallas kernels, call(): pl.pallas_call(kernel, name=name, out_shape=[jax.ShapeDtypeStruct(shape,...  21.8 us
    all_to_all x1, starting transfers between devices, exchange(): return lax.all_to_all(message, ALL, split_axis=0, concat_axis=0, tiled=True)  11.5 us
    ppermute x2, starting transfers between devices, passed(): lax.ppermute(block, axis, [(i - distance, i) for i in range(count) if 0 <...  5.69 us
    all_to_all x1, waiting for transfers between devices, exchange(): return lax.all_to_all(message, ALL, split_axis=0, concat_axis=0, tiled=True)  3.38 us
  transfers between devices with their start and end apart: 3, of which 3 were waited for; matrix products, arithmetic and copies ran while one was open for 0% of the time, Pallas kernels for 0%

profile of v1, /device:TPU:1, one launch (start us, length us, event | category | flops | bytes accessed | tf_op | source)
XLA Modules:
  0.0 148.7 jit_solution(9788461535174041114)
XLA Ops:
  0.6 3.2 %begin.1 = (f32[128,1,384]{2,1,0:T(1,128)}, f32[8,8,128]{2,1,0:T(8,128)}) custom-call(s32[1]{0:T(128)} %bitcast.me_ref.refs_0_, s32[4]{0:T(128)} %refs_1_.15, s32[4]{0:T(128)} %refs_2_.15, s32[4]{0:T(128)} %refs_3_.15, f32[4]{0:T(128)} %refs_4_.15, s32[4,256]{1,0:T(4,128)} %refs_0_.1, s32[4,256]{1,0:T(4,128)} %refs_1_.8, s32[4,256]{1,0:T(4,128)} %refs_2_.8, ...), custom_call_target="tpu_custom_call" | custom-call | tf_op jit(solution)/shard_map/begin/pallas_call | solution.py:456
  3.8 11.5 %all-to-all-start = ((f32[128,1,384]{2,1,0:T(1,128)}), f32[128,1,384]{2,1,0:T(1,128)S(1)}, u32[]{:S(2)}, u32[]{:S(2)}) async-start(f32[128,1,384]{2,1,0:T(1,128)} %get-tuple-element.34), calls=%async_computation | async-start | bytes 393216 | tf_op jit(solution)/shard_map/all_to_all | solution.py:468
  15.4 3.1 %collective-permute-start.1 = (f32[3,8,8,128]{3,2,1,0:T(8,128)S(1)}, f32[3,8,8,128]{3,2,1,0:T(8,128)S(1)}, u32[]{:S(2)}, u32[]{:S(2)}) collective-permute-start(f32[3,8,8,128]{3,2,1,0:T(8,128)S(1)} %pad_maximum_fusion), channel_id=1, source_target_pairs={{16,0},{32,16},{48,32},{64,48},{80,64},{96,80},{112,96},{17,1},{33... | collective-permute-start | bytes 294920 | tf_op jit(solution)/shard_map/ppermute | solution.py:473
  18.6 2.6 %collective-permute-start = (f32[3,8,8,128]{3,2,1,0:T(8,128)S(1)}, f32[3,8,8,128]{3,2,1,0:T(8,128)S(1)}, u32[]{:S(2)}, u32[]{:S(2)}) collective-permute-start(f32[3,8,8,128]{3,2,1,0:T(8,128)S(1)} %pad_maximum_fusion), channel_id=1, source_target_pairs={{0,16},{16,32},{32,48},{48,64},{64,80},{80,96},{96,112},{1,17},{17... | collective-permute-start | bytes 294920 | tf_op jit(solution)/shard_map/ppermute | solution.py:473
  21.2 1.1 collective-permute-done.1.right_ref
  22.2 0.5 collective-permute-done.left_ref
  22.8 3.4 %all-to-all-done.got_ref = f32[128,1,384]{2,1,0:T(1,128)S(1)} async-done(((f32[128,1,384]{2,1,0:T(1,128)}), f32[128,1,384]{2,1,0:T(1,128)S(1)}, u32[]{:S(2)}, u32[]{:S(2)}) %all-to-all-start) | async-done | bytes 196640 | tf_op jit(solution)/shard_map/all_to_all | solution.py:468
  26.2 3.1 %cells.1 = (f32[128,1,384]{2,1,0:T(1,128)S(1)}, f32[7,8,24,128]{3,2,1,0:T(8,128)S(1)}, f32[8,24,128]{2,1,0:T(8,128)S(1)}, s32[48,128]{1,0:T(8,128)S(1)}, f32[8,128]{1,0:T(8,128)S(1)}, /*index=5*/f32[8,8,128]{2,1,0:T(8,128)}) custom-call(s32[1]{0:T(128)} %bitcast.me_ref.refs_0_, s32[32]{0:T(128)S(1)} %copy-done.8, s32[32]{0:T(128)S(1)} %copy-done.9, ...), custom_call_target="tpu_custom_call" | custom-call | tf_op jit(solution)/shard_map/cells/pallas_call | solution.py:456
  29.2 18.0 %all_to_all.40.refs_5_ = f32[128,1,384]{2,1,0:T(1,128)S(1)} all-to-all(f32[128,1,384]{2,1,0:T(1,128)S(1)} %get-tuple-element.37), channel_id=1, replica_groups=mesh['gx'=8,'gy'=4,'af'=4] {'gx','gy','af'}, dimensions={0} | all-to-all | bytes 393216 | tf_op jit(solution)/shard_map/all_to_all | solution.py:468
  47.2 0.6 copy-done.4
  47.9 0.0 copy-done.5
  47.9 2.4 %step.7 = (f32[128,1,256]{2,1,0:T(1,128)S(1)}, f32[8,24,128]{2,1,0:T(8,128)S(1)}, f32[8,128]{1,0:T(8,128)S(1)}, f32[8,128]{1,0:T(8,128)S(1)}, f32[4,256]{1,0:T(4,128)}) custom-call(s32[1]{0:T(128)} %bitcast.me_ref.refs_0_, s32[4]{0:T(128)S(1)} %copy-done.4, s32[4]{0:T(128)S(1)} %copy-done.5, s32[4]{0:T(128)S(1)} %copy-done.6, f32[4]{0:T(128)S(1)} %copy-done.7, ...), custom_call_target="tpu_custom_call" | custom-call | tf_op jit(solution)/shard_map/step/pallas_call | solution.py:456
  50.3 14.2 %all_to_all.41.refs_5_ = f32[128,1,256]{2,1,0:T(1,128)S(1)} all-to-all(f32[128,1,256]{2,1,0:T(1,128)S(1)} %get-tuple-element.43), channel_id=1, replica_groups=mesh['gx'=8,'gy'=4,'af'=4] {'gx','gy','af'}, dimensions={0} | all-to-all | bytes 262144 | tf_op jit(solution)/shard_map/all_to_all | solution.py:468
  64.6 2.3 %step.8 = (f32[128,1,256]{2,1,0:T(1,128)S(1)}, f32[8,24,128]{2,1,0:T(8,128)S(1)}, f32[8,128]{1,0:T(8,128)S(1)}) custom-call(s32[1]{0:T(128)} %bitcast.me_ref.refs_0_, s32[4]{0:T(128)S(1)} %copy-done.4, s32[4]{0:T(128)S(1)} %copy-done.5, s32[4]{0:T(128)S(1)} %copy-done.6, f32[4]{0:T(128)S(1)} %copy-done.7, f32[128,1,256]{2,1,0:T(1,128)S(1)} %all_to_all.41.refs_5_, ...), custom_call_target="tpu_custom_call" | custom-call | tf_op jit(solution)/shard_map/step/pallas_call | solution.py:456
  66.9 14.2 %all_to_all.42.refs_5_ = f32[128,1,256]{2,1,0:T(1,128)S(1)} all-to-all(f32[128,1,256]{2,1,0:T(1,128)S(1)} %get-tuple-element.47), channel_id=1, replica_groups=mesh['gx'=8,'gy'=4,'af'=4] {'gx','gy','af'}, dimensions={0} | all-to-all | bytes 262144 | tf_op jit(solution)/shard_map/all_to_all | solution.py:468
  81.0 2.3 %step.9 = (f32[128,1,256]{2,1,0:T(1,128)S(1)}, f32[8,24,128]{2,1,0:T(8,128)S(1)}, f32[8,128]{1,0:T(8,128)S(1)}) custom-call(s32[1]{0:T(128)} %bitcast.me_ref.refs_0_, s32[4]{0:T(128)S(1)} %copy-done.4, s32[4]{0:T(128)S(1)} %copy-done.5, s32[4]{0:T(128)S(1)} %copy-done.6, f32[4]{0:T(128)S(1)} %copy-done.7, f32[128,1,256]{2,1,0:T(1,128)S(1)} %all_to_all.42.refs_5_, ...), custom_call_target="tpu_custom_call" | custom-call | tf_op jit(solution)/shard_map/step/pallas_call | solution.py:456
  83.3 14.2 %all_to_all.43.refs_5_ = f32[128,1,256]{2,1,0:T(1,128)S(1)} all-to-all(f32[128,1,256]{2,1,0:T(1,128)S(1)} %get-tuple-element.50), channel_id=1, replica_groups=mesh['gx'=8,'gy'=4,'af'=4] {'gx','gy','af'}, dimensions={0} | all-to-all | bytes 262144 | tf_op jit(solution)/shard_map/all_to_all | solution.py:468
  97.5 2.3 %step.10 = (f32[128,1,256]{2,1,0:T(1,128)S(1)}, f32[8,24,128]{2,1,0:T(8,128)S(1)}, f32[8,128]{1,0:T(8,128)S(1)}) custom-call(s32[1]{0:T(128)} %bitcast.me_ref.refs_0_, s32[4]{0:T(128)S(1)} %copy-done.4, s32[4]{0:T(128)S(1)} %copy-done.5, s32[4]{0:T(128)S(1)} %copy-done.6, f32[4]{0:T(128)S(1)} %copy-done.7, f32[128,1,256]{2,1,0:T(1,128)S(1)} %all_to_all.43.refs_5_, ...), custom_call_target="tpu_custom_call" | custom-call | tf_op jit(solution)/shard_map/step/pallas_call | solution.py:456
  99.8 14.2 %all_to_all.44.refs_5_ = f32[128,1,256]{2,1,0:T(1,128)S(1)} all-to-all(f32[128,1,256]{2,1,0:T(1,128)S(1)} %get-tuple-element.53), channel_id=1, replica_groups=mesh['gx'=8,'gy'=4,'af'=4] {'gx','gy','af'}, dimensions={0} | all-to-all | bytes 262144 | tf_op jit(solution)/shard_map/all_to_all | solution.py:468
  114.0 2.3 %step.11 = (f32[128,1,256]{2,1,0:T(1,128)S(1)}, f32[8,24,128]{2,1,0:T(8,128)S(1)}, f32[8,128]{1,0:T(8,128)S(1)}) custom-call(s32[1]{0:T(128)} %bitcast.me_ref.refs_0_, s32[4]{0:T(128)S(1)} %copy-done.4, s32[4]{0:T(128)S(1)} %copy-done.5, s32[4]{0:T(128)S(1)} %copy-done.6, f32[4]{0:T(128)S(1)} %copy-done.7, f32[128,1,256]{2,1,0:T(1,128)S(1)} %all_to_all.44.refs_5_, ...), custom_call_target="tpu_custom_call" | custom-call | tf_op jit(solution)/shard_map/step/pallas_call | solution.py:456
  116.3 14.2 %all_to_all.45.refs_5_ = f32[128,1,256]{2,1,0:T(1,128)S(1)} all-to-all(f32[128,1,256]{2,1,0:T(1,128)S(1)} %get-tuple-element.56), channel_id=1, replica_groups=mesh['gx'=8,'gy'=4,'af'=4] {'gx','gy','af'}, dimensions={0} | all-to-all | bytes 262144 | tf_op jit(solution)/shard_map/all_to_all | solution.py:468
  130.5 2.3 %step.12 = (f32[128,1,256]{2,1,0:T(1,128)S(1)}, f32[8,24,128]{2,1,0:T(8,128)S(1)}, f32[8,128]{1,0:T(8,128)S(1)}) custom-call(s32[1]{0:T(128)} %bitcast.me_ref.refs_0_, s32[4]{0:T(128)S(1)} %copy-done.4, s32[4]{0:T(128)S(1)} %copy-done.5, s32[4]{0:T(128)S(1)} %copy-done.6, f32[4]{0:T(128)S(1)} %copy-done.7, f32[128,1,256]{2,1,0:T(1,128)S(1)} %all_to_all.45.refs_5_, ...), custom_call_target="tpu_custom_call" | custom-call | tf_op jit(solution)/shard_map/step/pallas_call | solution.py:456
  132.8 14.2 %all_to_all.46.refs_5_ = f32[128,1,256]{2,1,0:T(1,128)S(1)} all-to-all(f32[128,1,256]{2,1,0:T(1,128)S(1)} %get-tuple-element.59), channel_id=1, replica_groups=mesh['gx'=8,'gy'=4,'af'=4] {'gx','gy','af'}, dimensions={0} | all-to-all | bytes 262144 | tf_op jit(solution)/shard_map/all_to_all | solution.py:468
  147.0 1.7 %step.13 = (f32[8,8,128]{2,1,0:T(8,128)}, f32[4,256]{1,0:T(4,128)}) custom-call(s32[1]{0:T(128)} %bitcast.me_ref.refs_0_, s32[4]{0:T(128)S(1)} %copy-done.4, s32[4]{0:T(128)S(1)} %copy-done.5, s32[4]{0:T(128)S(1)} %copy-done.6, f32[4]{0:T(128)S(1)} %copy-done.7, f32[128,1,256]{2,1,0:T(1,128)S(1)} %all_to_all.46.refs_5_, ...), custom_call_target="tpu_custom_call" | custom-call | tf_op jit(solution)/shard_map/step/pallas_call | solution.py:456
  (21 shorter events, 0.1 us)
Async XLA Ops:
  3.8 11.5 %copy-start.1 = (f32[8,8,128]{2,1,0:T(8,128)S(1)}, f32[8,8,128]{2,1,0:T(8,128)}, u32[]{:S(2)}) copy-start(f32[8,8,128]{2,1,0:T(8,128)} %press_ref.1) | copy-start | bytes 98308
  3.8 11.5 %copy-start.2 = (f32[8,8,128]{2,1,0:T(8,128)S(1)}, f32[8,8,128]{2,1,0:T(8,128)}, u32[]{:S(2)}) copy-start(f32[8,8,128]{2,1,0:T(8,128)} %cond_ref.1) | copy-start | bytes 98308
  3.8 11.5 %copy-start.3 = (f32[8,8,128]{2,1,0:T(8,128)S(1)}, f32[8,8,128]{2,1,0:T(8,128)}, u32[]{:S(2)}) copy-start(f32[8,8,128]{2,1,0:T(8,128)} %accum_ref.1) | copy-start | bytes 98308
  3.8 22.3 %all-to-all-start = ((f32[128,1,384]{2,1,0:T(1,128)}), f32[128,1,384]{2,1,0:T(1,128)S(1)}, u32[]{:S(2)}, u32[]{:S(2)}) async-start(f32[128,1,384]{2,1,0:T(1,128)} %get-tuple-element.34), calls=%async_computation | async-start | bytes 393216 | tf_op jit(solution)/shard_map/all_to_all | solution.py:468
  15.4 10.8 %copy-start = (f32[8,8,128]{2,1,0:T(8,128)S(1)}, f32[8,8,128]{2,1,0:T(8,128)}, u32[]{:S(2)}) copy-start(f32[8,8,128]{2,1,0:T(8,128)} %get-tuple-element.35.seg_ref.refs_9_) | copy-start | bytes 98308
  15.4 10.7 %copy-start.8 = (s32[32]{0:T(128)S(1)}, s32[32]{0:T(128)}, u32[]{:S(2)}) copy-start(s32[32]{0:T(128)} %well_tile_ref.1) | copy-start | bytes 388
  15.4 10.7 %copy-start.9 = (s32[32]{0:T(128)S(1)}, s32[32]{0:T(128)}, u32[]{:S(2)}) copy-start(s32[32]{0:T(128)} %well_cell_ref.1) | copy-start | bytes 388
  15.4 10.7 %copy-start.10 = (f32[32]{0:T(128)S(1)}, f32[32]{0:T(128)}, u32[]{:S(2)}) copy-start(f32[32]{0:T(128)} %well_rate_ref.1) | copy-start | bytes 388
  15.4 6.8 %collective-permute-start.1 = (f32[3,8,8,128]{3,2,1,0:T(8,128)S(1)}, f32[3,8,8,128]{3,2,1,0:T(8,128)S(1)}, u32[]{:S(2)}, u32[]{:S(2)}) collective-permute-start(f32[3,8,8,128]{3,2,1,0:T(8,128)S(1)} %pad_maximum_fusion), channel_id=1, source_target_pairs={{16,0},{32,16},{48,32},{64,48},{80,64},{96,80},{112,96},{17,1},{33... | collective-permute-start | bytes 294920 | tf_op jit(solution)/shard_map/ppermute | solution.py:473
  18.6 4.2 %collective-permute-start = (f32[3,8,8,128]{3,2,1,0:T(8,128)S(1)}, f32[3,8,8,128]{3,2,1,0:T(8,128)S(1)}, u32[]{:S(2)}, u32[]{:S(2)}) collective-permute-start(f32[3,8,8,128]{3,2,1,0:T(8,128)S(1)} %pad_maximum_fusion), channel_id=1, source_target_pairs={{0,16},{16,32},{32,48},{48,64},{64,80},{80,96},{96,112},{1,17},{17... | collective-permute-start | bytes 294920 | tf_op jit(solution)/shard_map/ppermute | solution.py:473
  29.2 18.0 %copy-start.7 = (f32[4]{0:T(128)S(1)}, f32[4]{0:T(128)}, u32[]{:S(2)}) copy-start(f32[4]{0:T(128)} %refs_4_.15) | copy-start | bytes 52
  47.2 0.7 copy-start.4
  47.2 0.7 copy-start.5
  47.2 0.7 copy-start.6

commit v2 on v1

--- a/solution.py
+++ b/solution.py
@@ -92,40 +92,37 @@
     return dot_nt(both, jnp.concatenate([hot, hot], axis=1))
 
 
-def from_slots(table, hot, mask):
-    high, low = parts(table)
-    rows = dot_nn(jnp.concatenate([high, low], axis=1), jnp.concatenate([hot, hot], axis=0))
-    return as_rows(jnp.sum(jnp.where(mask, rows, 0.0), axis=0, keepdims=True))
+def look_up(table, row, lane):
+    out = jnp.zeros(row.shape, f32)
+    for r in range(table.shape[0]):
+        picked = jnp.take_along_axis(jnp.broadcast_to(table[r : r + 1], row.shape), lane, axis=1, mode="promise_in_bounds")
+        out = jnp.where(row == r, picked, out)
+    return out
+
+
+def find(table, index):
+    return look_up(table, index >> 7, index & 127)
 
 
 def cell_hot(index_row):
     count = index_row.shape[1]
-    columns = (iota((128, count), 0) == (index_row & 127)).astype(bf16)
-    return columns, iota((ROWS, count), 0) == (index_row >> 7)
-
-
-def scatter(tables, columns, mask):
+    columns = iota((128, count), 0) == (index_row & 127)
+    rows = iota((ROWS, count), 0) == (index_row >> 7)
+    return columns.astype(bf16), rows.astype(bf16)
+
+
+def scatter(tables, columns, rows):
     stacked = []
     for table in tables:
-        for part in parts(as_row(table)):
-            stacked.append(jnp.where(mask, part.astype(f32), 0.0).astype(bf16))
+        for part in parts(table):
+            row = as_row(part.astype(f32))
+            tall = jnp.broadcast_to(row, (16, row.shape[1])).astype(bf16)
+            stacked.append(rows * jnp.concatenate([tall] * (ROWS // 16), axis=0))
     sums = dot_nt(jnp.concatenate(stacked, axis=0), columns)
     return [
         (sums[2 * i * ROWS : (2 * i + 1) * ROWS] + sums[(2 * i + 1) * ROWS : (2 * i + 2) * ROWS]).reshape(LAYERS, 8, 128)
         for i in range(len(tables))
     ]
-
-
-def gather(fields, columns, mask):
-    stacked = []
-    for field in fields:
-        stacked.extend(parts(field.reshape(ROWS, 128)))
-    rows = dot_nn(jnp.concatenate(stacked, axis=0), columns)
-    out = []
-    for i in range(len(fields)):
-        both = rows[2 * i * ROWS : (2 * i + 1) * ROWS] + rows[(2 * i + 1) * ROWS : (2 * i + 2) * ROWS]
-        out.append(as_rows(jnp.sum(jnp.where(mask, both, 0.0), axis=0, keepdims=True)))
-    return out
 
 
 def faces_of(field):
@@ -218,7 +215,9 @@
     return jnp.concatenate([got_ref[:, 0, i : i + 128].T for i in range(0, count, 128)], axis=0)
 
 
-def begin_kernel(me_ref, delta_ref, from_ref, to_ref, trans_ref, *refs):
+def begin_kernel(
+    me_ref, delta_ref, from_ref, to_ref, trans_ref, well_tile_ref, well_cell_ref, well_rate_ref, *refs
+):
     given, (out_ref, seg_ref), held, sems = refs[:10], refs[10:12], refs[12:22], refs[22]
     copies = [pltpu.make_async_copy(a, b, sems.at[i]) for i, (a, b) in enumerate(zip(given, held))]
     for copy in copies:
@@ -259,7 +258,9 @@
         at = code == b * 256 + from_ref[b]
         partial = partial - jnp.where(at, trans_ref[b] * total(jnp.where(code == here, press, 0.0)), 0.0)
     where_cell = (fold(layer_ref[...]) * 1024 + fold(cell_ref[...]) + 1).astype(f32)
-    slots = to_slots([where_cell, mf * press, fm * inverse * fm], hot, mask)
+    position = (iota((8, 128), 0) * 128 + iota((8, 128), 1) + 1).astype(f32)
+    slots = to_slots([where_cell, mf * press, fm * inverse * fm, position], hot, mask)
+    inverse_index, slots = slots[48:64], slots[:48]
     place = (owner * CAP + rank).astype(f32)
     edges = []
     for b in range(4):
@@ -278,6 +279,26 @@
         put_faces(me, out_ref, 256, first_face, last_face, across)
     for i, value in enumerate((tnext, inverse, partial, fm, mf, owner.astype(f32), rank.astype(f32), press)):
         seg_ref[i] = value
+    for i in range(2):
+        seg_ref[8 + i] = inverse_index[8 * i : 8 * i + 8] - 1.0
+    lane = iota((8, 128), 1)
+    own = jnp.zeros((8, 128), f32)
+    for b in range(4):
+        here, there = edge_codes(delta_ref, to_ref, b)
+        for i, value in enumerate((b * 256 + from_ref[b], here, there)):
+            own = jnp.where(lane == 8 * b + i, value.astype(f32), own)
+        own = jnp.where(lane == 8 * b + 3, trans_ref[b], own)
+    seg_ref[10] = own
+    plane_x = iota((EXT, 128), 0) + ((me >> 4) - 1) * 8
+    plane_y = iota((EXT, 128), 1) + (me & 15) * 128
+    source = jnp.zeros((EXT, 128), f32)
+    for w in range(well_tile_ref.shape[0]):
+        tile = well_tile_ref[w]
+        cell = well_cell_ref[w]
+        at = (plane_x == (tile >> 4) * 8 + (cell >> 7)) & (plane_y == (tile & 15) * 128 + (cell & 127))
+        source = source + jnp.where(at, well_rate_ref[w], 0.0)
+    for i in range(3):
+        seg_ref[11 + i] = source[8 * i : 8 * i + 8]
 
 
 def edge_in(row, k, i):
@@ -286,25 +307,28 @@
 
 
 def cells_kernel(
-    me_ref, well_tile_ref, well_cell_ref, well_rate_ref,
-    got_ref, press_ref, cond_ref, accum_ref, left_ref, right_ref, seg_ref,
-    out_ref, cells_ref, field_ref, index_ref, edge_ref, res_ref,
+    me_ref,
+    got_ref, middle_ref, inside_ref, across_ref, seg_ref,
+    out_ref, cells_ref, field_ref, index_ref, columns_ref, rows_ref, edge_ref, res_ref,
 ):
     me = me_ref[0]
     slots = load_slots(got_ref, 256)
+    even = ((me >> 4) & 1) == 0
     press, cond, accum = (
-        jnp.concatenate([left_ref[i], ref[...], right_ref[i]], axis=1)
-        for i, ref in enumerate((press_ref, cond_ref, accum_ref))
+        jnp.concatenate([jnp.where(even, b, a), middle_ref[i], jnp.where(even, a, b)], axis=1)
+        for i, a, b in ((i, inside_ref[i], across_ref[i]) for i in range(3))
     )
     sums = []
     for side in range(3):
         table = slots[side * 48 : side * 48 + 48]
         index = table[:CAP].astype(i32) - 1
-        index_ref[side * CAP : side * CAP + CAP] = index
-        columns, mask = cell_hot(as_row(index))
-        sums.append(scatter([table[16:32], table[32:48]], columns, mask))
         if side == 1:
-            own_columns, own_mask = columns, mask
+            index_ref[...] = index
+            own = index
+        columns, rows = cell_hot(as_row(index))
+        columns_ref[side] = columns
+        rows_ref[side] = rows
+        sums.append(scatter([table[16:32], table[32:48]], columns, rows))
     flow, weight = (jnp.concatenate([sums[side][i] for side in range(3)], axis=1) for i in range(2))
 
     halos = [columns_of(*read_faces(me, got_ref, 256, 2 * ROWS, across)) for across in (-16, 0, 16)]
@@ -318,17 +342,7 @@
     diag = accum + tx + down_x(tx) + ty + down_y(ty, ty_first) + tz + down_z(tz)
     inverse = jnp.where(diag > 0.0, 1.0 / jnp.where(diag > 0.0, diag, 1.0), 0.0)
 
-    x0 = ((me >> 4) - 1) * 8
-    y0 = (me & 15) * 128
-    plane_x = iota((EXT, 128), 0) + x0
-    plane_y = iota((EXT, 128), 1) + y0
-    source = jnp.zeros((EXT, 128), f32)
-    for w in range(well_tile_ref.shape[0]):
-        tile = well_tile_ref[w]
-        cell = well_cell_ref[w]
-        at = (plane_x == (tile >> 4) * 8 + (cell >> 7)) & (plane_y == (tile & 15) * 128 + (cell & 127))
-        source = source + jnp.where(at, well_rate_ref[w], 0.0)
-
+    source = jnp.concatenate([seg_ref[11 + i] for i in range(3)], axis=0)
     res = diag * press - stencil(tx, ty, tz, ty_first, press, press_halo) - flow - source[None]
     field = inverse * res
     for i, value in enumerate((tx, ty, tz, ty_first, inverse, res, weight * press)):
@@ -337,7 +351,7 @@
     res_ref[...] = res[:, 8:16]
 
     code = seg_code().astype(f32)
-    _, inverse_f, partial, fm, _, owner, rank, press_f = (seg_ref[i] for i in range(8))
+    _, inverse_f, partial, fm, _, _, _, press_f = (seg_ref[i] for i in range(8))
     edge = jnp.where(me > 0, got_ref[jnp.maximum(me - 1, 0), :, 128:256], -1.0)
     lane = iota((1, 128), 1)
     cells, terms, picks = [], [], []
@@ -351,10 +365,10 @@
         edge = jnp.where(lane == 16 + 8 * k + 4, edge - edge_in(edge, k, 5) * picked, edge)
     edge_ref[...] = jnp.broadcast_to(edge, (8, 128))
     late = jnp.concatenate(cells + terms, axis=0)
-    hot = owner_hot(as_row(owner.astype(i32)))
-    first = to_slots([fm * inverse_f * partial], hot, rank_mask(as_row(rank.astype(i32))))
-
-    taken = gather([press_ref[...], field[:, 8:16]], own_columns, own_mask)
+    position = jnp.concatenate([seg_ref[8], seg_ref[9]], axis=0).astype(i32)
+    first = find(fm * inverse_f * partial, position)
+
+    taken = [find(middle_ref[0].reshape(ROWS, 128), own), find(field[:, 8:16].reshape(ROWS, 128), own)]
     rows = taken + [spread(taken[0], 1)]
     rows += [spread(first, 16), first, spread(first, -16), spread(late, 16), late, spread(late, -16)]
     store_slots(out_ref, jnp.concatenate(rows + picks + [jnp.zeros((4, 128), f32)], axis=0))
@@ -363,64 +377,60 @@
 
 def step_kernel(
     first, final,
-    me_ref, delta_ref, from_ref, to_ref, trans_ref,
-    got_ref, cells_ref, field_ref, index_ref, seg_ref, edge_ref, *rest,
+    me_ref,
+    got_ref, cells_ref, field_ref, index_ref, columns_ref, rows_ref, seg_ref, edge_ref, *rest,
 ):
     me = me_ref[0]
     if not first:
         frac_ref, resf_ref, *rest = rest
     slots = load_slots(got_ref, 128)
-    code = seg_code()
-    code_f = code.astype(f32)
+    code = seg_code().astype(f32)
     tnext, inverse_f, partial, fm, mf, owner, rank = (seg_ref[i] for i in range(7))
-    hot = owner_hot(as_row(owner.astype(i32)))
-    mask = rank_mask(as_row(rank.astype(i32)))
+    owner = owner.astype(i32)
+    rank = rank.astype(i32)
     edge = edge_ref[0:1]
+    own = seg_ref[10][0:1]
+    starts, targets, nexts, factors = ([own[:, 8 * b + i : 8 * b + i + 1] for b in range(4)] for i in range(4))
 
     if first:
-        resf = partial - fm * from_slots(slots[0:16], hot, mask)
+        resf = partial - fm * look_up(slots[0:16], rank, owner)
         after = got_ref[jnp.minimum(me + 1, TILES - 1), :, 0:128]
         for b in range(4):
-            _, there = edge_codes(delta_ref, to_ref, b)
-            at = (code == b * 256 + from_ref[b]) & (there >= 0)
-            resf = resf - jnp.where(at, trans_ref[b] * after[:, 120 + b : 121 + b], 0.0)
+            at = (code == starts[b]) & (nexts[b] >= 0.0)
+            resf = resf - jnp.where(at, factors[b] * after[:, 120 + b : 121 + b], 0.0)
         frac = inverse_f * resf
-        here = from_slots(slots[16:32], hot, mask)
+        here = look_up(slots[16:32], rank, owner)
     else:
         resf = resf_ref[...]
         frac = frac_ref[...]
-        here = from_slots(slots[0:16], hot, mask)
+        here = look_up(slots[0:16], rank, owner)
     gain = resf + chain(tnext, frac) + mf * here
     before = got_ref[jnp.maximum(me - 1, 0), :, 64:256]
     for b in range(4):
-        target, _ = edge_codes(delta_ref, to_ref, b)
-        at = code == b * 256 + from_ref[b]
-        term = trans_ref[b] * total(jnp.where(at, frac, 0.0))
-        gain = gain + jnp.where(code == target, term, 0.0)
+        term = factors[b] * total(jnp.where(code == starts[b], frac, 0.0))
+        gain = gain + jnp.where(code == targets[b], term, 0.0)
         if first:
             place = (iota((CAP, 128), 1) * CAP + iota((CAP, 128), 0)).astype(f32)
             there = total(jnp.where(place == edge_in(edge, b, 1), slots[32:48], 0.0))
             term = edge_in(edge, b, 4) - edge_in(edge, b, 3) * there
         else:
             term = before[:, EXT * b : EXT * b + 1]
-        gain = gain + jnp.where(code_f == edge_in(edge, b, 0), term, 0.0)
+        gain = gain + jnp.where(code == edge_in(edge, b, 0), term, 0.0)
     frac = inverse_f * gain
 
     tx, ty, tz, ty_first, inverse, res = (cells_ref[i] for i in range(6))
     field = field_ref[...]
     flow = []
     for side in range(3):
-        index = index_ref[side * CAP : side * CAP + CAP]
+        if final and side != 1:
+            flow.append(jnp.zeros((LAYERS, 8, 128), f32))
+            continue
+        start = (48 if first else 16) + side * CAP
+        flow.extend(scatter([slots[start : start + CAP]], columns_ref[side], rows_ref[side]))
         if first:
             late = slots[96 + 8 * side : 104 + 8 * side]
-            index = jnp.concatenate([index, late[:4].astype(i32) - 1], axis=0)
-            table = jnp.concatenate([slots[48 + side * CAP : 64 + side * CAP], late[4:]], axis=0)
-        else:
-            table = slots[16 + side * CAP : 32 + side * CAP]
-        columns, rows = cell_hot(as_row(index))
-        flow.extend(scatter([table], columns, rows))
-        if side == 1:
-            own_columns, own_mask = columns[:, :SLOTS], rows[:, :SLOTS]
+            more = scatter([late[4:]], *cell_hot(as_row(late[:4].astype(i32) - 1)))
+            flow[side] = flow[side] + more[0]
     flow = jnp.concatenate(flow, axis=1)
     if first:
         flow = flow - cells_ref[6]
@@ -439,18 +449,17 @@
         res_fracture_ref[...] = unfold(resf)
     new_field_ref[...] = field
     new_frac_ref[...] = frac
-    taken = gather([field[:, 8:16]], own_columns, own_mask)
-    terms = to_slots([fm * frac], hot, mask)
+    taken = [find(field[:, 8:16].reshape(ROWS, 128), index_ref[...])]
+    terms = find(fm * frac, jnp.concatenate([seg_ref[8], seg_ref[9]], axis=0).astype(i32))
     store_slots(out_ref, jnp.concatenate(taken + [spread(terms, 16), terms, spread(terms, -16)], axis=0))
     begin, end = faces_of(field.reshape(LAYERS * EXT, 128))
     lane = iota(end.shape, 1)
     for b in range(4):
-        at = code == b * 256 + from_ref[b]
-        end = jnp.where(lane == EXT * b, trans_ref[b] * total(jnp.where(at, frac, 0.0)), end)
+        end = jnp.where(lane == EXT * b, factors[b] * total(jnp.where(code == starts[b], frac, 0.0)), end)
     put_faces(me, out_ref, 64, begin, end)
 
 
-def call(kernel, name, scalars, arrays, outs, space=pltpu.VMEM, scratch=(), limit=48 * 1024 * 1024):
+def call(kernel, name, scalars, arrays, outs, space=pltpu.VMEM, scratch=(), limit=20 * 1024 * 1024):
     spec = [pl.BlockSpec(memory_space=pltpu.SMEM)] * len(scalars)
     spec += [pl.BlockSpec(memory_space=space)] * len(arrays)
     return pl.pallas_call(
@@ -468,9 +477,9 @@
     return lax.all_to_all(message, ALL, split_axis=0, concat_axis=0, tiled=True)
 
 
-def passed(block, axis, distance):
-    count = lax.axis_size(axis)
-    return lax.ppermute(block, axis, [(i - distance, i) for i in range(count) if 0 <= i - distance < count])
+def swapped(block, first):
+    pairs = [(i, i + 1) for i in range(first, lax.axis_size("gx") - 1, 2)]
+    return lax.ppermute(block, "gx", pairs + [(j, i) for i, j in pairs])
 
 
 def body(
@@ -479,9 +488,8 @@
 ):
     me = lax.axis_index(ALL).astype(i32).reshape(1)
     stacked = jnp.stack([press_matrix, cond_matrix, accum_matrix])
-    left = passed(stacked, "gx", 1)
-    right = passed(stacked, "gx", -1)
-    edges = (inter_delta, inter_from, inter_to, inter_trans)
+    inside = swapped(stacked, 0)
+    across = swapped(stacked, 1)
     wide = (LAYERS, EXT, 128)
     tile = (LAYERS, 8, 128)
     seg = (8, 128)
@@ -490,20 +498,21 @@
     message, segs = call(
         begin_kernel,
         "begin",
-        (me, *edges),
+        (me, inter_delta, inter_from, inter_to, inter_trans, well_tile, well_cell, well_rate),
         given,
-        [((TILES, 1, 384), f32), ((8, *seg), f32)],
+        [((TILES, 1, 384), f32), ((14, *seg), f32)],
         pl.ANY,
         [pltpu.VMEM(a.shape, a.dtype) for a in given] + [pltpu.SemaphoreType.DMA((len(given),))],
         64 * 1024 * 1024,
     )
     got = exchange(message)
-    message, cells, field, index, edge, res_matrix = call(
+    message, cells, field, index, columns, rows, edge, res_matrix = call(
         cells_kernel,
         "cells",
-        (me, well_tile, well_cell, well_rate),
-        (got, press_matrix, cond_matrix, accum_matrix, left, right, segs),
-        [((TILES, 1, 384), f32), ((7, *wide), f32), (wide, f32), ((48, 128), i32), (seg, f32), (tile, f32)],
+        (me,),
+        (got, stacked, inside, across, segs),
+        [((TILES, 1, 384), f32), ((7, *wide), f32), (wide, f32), ((CAP, 128), i32), ((3, 128, SLOTS), bf16),
+         ((3, ROWS, SLOTS), bf16), (seg, f32), (tile, f32)],
     )
     got = exchange(message)
 
@@ -511,7 +520,7 @@
         def kernel(*refs):
             step_kernel(first, final, *refs)
 
-        return call(kernel, "step", (me, *edges), (got, cells, field, index, segs, edge, *more), outs)
+        return call(kernel, "step", (me,), (got, cells, field, index, columns, rows, segs, edge, *more), outs)
 
     going = [((TILES, 1, 256), f32), (wide, f32), (seg, f32)]
     message, field, frac, resf, res_fracture = step(

time: 149 us -> 141 us (0.946)
  Pallas kernels: 21.8 us -> 15.7 us
  starting transfers between devices: 17.2 us -> 15.1 us
  blocking collectives: 103 us -> 101 us
    pallas_call x9, Pallas kernels: 21.8 us -> 15.7 us  [call(): pl.pallas_call(kernel, name=name, out_shape=[jax.ShapeDtypeStruct(shape,...]
    ppermute x2, starting transfers between devices: 5.69 us -> 3.62 us  [swapped(): return lax.ppermute(block, 'gx', pairs + [(j, i) for i, j in pairs])]
    all_to_all x7, blocking collectives: 103 us -> 101 us  [exchange(): return lax.all_to_all(message, ALL, split_axis=0, concat_axis=0, tiled=True)]
  transfers between devices with their start and end apart: 3 -> 3, of which waited for: 3 -> 2; matrix products, arithmetic and copies ran while one was open for 0% -> 1% of each run, Pallas kernels for 0% -> 0%
where the time goes in v2:
time: 141 us
  blocking collectives  101 us (72%)
  Pallas kernels  15.7 us (11%)
  starting transfers between devices  15.1 us (11%)
  waiting for transfers between devices  6.37 us (5%)
    all_to_all x7, blocking collectives, exchange(): return lax.all_to_all(message, ALL, split_axis=0, concat_axis=0, tiled=True)  101 us
    pallas_call x9, Pallas kernels, call(): pl.pallas_call(kernel, name=name, out_shape=[jax.ShapeDtypeStruct(shape,...  15.7 us
    all_to_all x1, starting transfers between devices, exchange(): return lax.all_to_all(message, ALL, split_axis=0, concat_axis=0, tiled=True)  11.5 us
    all_to_all x1, waiting for transfers between devices, exchange(): return lax.all_to_all(message, ALL, split_axis=0, concat_axis=0, tiled=True)  3.65 us
    ppermute x2, starting transfers between devices, swapped(): return lax.ppermute(block, 'gx', pairs + [(j, i) for i, j in pairs])  3.62 us
  transfers between devices with their start and end apart: 3, of which 2 were waited for; matrix products, arithmetic and copies ran while one was open for 1% of the time, Pallas kernels for 0%

profile of v2, /device:TPU:1, one launch (start us, length us, event | category | flops | bytes accessed | tf_op | source)
XLA Modules:
  0.0 140.9 jit_solution(14713267813418365261)
XLA Ops:
  0.6 3.2 %begin.1 = (f32[128,1,384]{2,1,0:T(1,128)}, f32[14,8,128]{2,1,0:T(8,128)}) custom-call(s32[1]{0:T(128)} %bitcast.me_ref.refs_0_, s32[4]{0:T(128)} %delta_ref.1, s32[4]{0:T(128)} %from_ref.1, s32[4]{0:T(128)} %to_ref.1, f32[4]{0:T(128)} %trans_ref.1, s32[32]{0:T(128)} %well_tile_ref.1, s32[32]{0:T(128)} %well_cell_ref.1, f32[32]{0:T(128)} %well_rate_ref.1, ...), custom_call_target="tpu_custom_call" | custom-call | tf_op jit(solution)/shard_map/begin/pallas_call | solution.py:465
  3.9 11.5 %all-to-all-start = ((f32[128,1,384]{2,1,0:T(1,128)}), f32[128,1,384]{2,1,0:T(1,128)S(1)}, u32[]{:S(2)}, u32[]{:S(2)}) async-start(f32[128,1,384]{2,1,0:T(1,128)} %get-tuple-element.36), calls=%async_computation | async-start | bytes 393216 | tf_op jit(solution)/shard_map/all_to_all | solution.py:477
  15.4 0.8 pad_maximum_fusion.middle_ref
  16.2 3.5 %collective-permute-start.1 = (f32[3,8,8,128]{3,2,1,0:T(8,128)S(1)}, f32[3,8,8,128]{3,2,1,0:T(8,128)S(1)}, u32[]{:S(2)}, u32[]{:S(2)}) collective-permute-start(f32[3,8,8,128]{3,2,1,0:T(8,128)S(1)} %pad_maximum_fusion.middle_ref), channel_id=1, source_target_pairs={{16,32},{48,64},{80,96},{32,16},{64,48},{96,80},{17,33},{49,65},{8... | collective-permute-start | bytes 294920 | tf_op jit(solution)/shard_map/ppermute | solution.py:482
  19.7 0.1 collective-permute-start
  19.8 2.7 %collective-permute-done.1.across_ref = f32[3,8,8,128]{3,2,1,0:T(8,128)S(1)} collective-permute-done((f32[3,8,8,128]{3,2,1,0:T(8,128)S(1)}, f32[3,8,8,128]{3,2,1,0:T(8,128)S(1)}, u32[]{:S(2)}, u32[]{:S(2)}) %collective-permute-start.1) | collective-permute-done | bytes 98336 | tf_op jit(solution)/shard_map/ppermute | solution.py:482
  22.5 0.0 collective-permute-done.inside_ref
  22.5 3.6 %all-to-all-done.got_ref = f32[128,1,384]{2,1,0:T(1,128)S(1)} async-done(((f32[128,1,384]{2,1,0:T(1,128)}), f32[128,1,384]{2,1,0:T(1,128)S(1)}, u32[]{:S(2)}, u32[]{:S(2)}) %all-to-all-start) | async-done | bytes 196640 | tf_op jit(solution)/shard_map/all_to_all | solution.py:477
  26.2 0.8 copy-done
  27.0 2.4 %cells.1 = (f32[128,1,384]{2,1,0:T(1,128)S(1)}, f32[7,8,24,128]{3,2,1,0:T(8,128)S(1)}, f32[8,24,128]{2,1,0:T(8,128)S(1)}, s32[16,128]{1,0:T(8,128)S(1)}, bf16[3,...) custom-call(s32[1]{0:T(128)} %bitcast.me_ref.refs_0_, ...), custom_call_target="tpu_custom_call" | custom-call | tf_op jit(solution)/shard_map/cells/pallas_call | solution.py:465
  29.4 16.3 %all_to_all.40.refs_1_ = f32[128,1,384]{2,1,0:T(1,128)S(1)} all-to-all(f32[128,1,384]{2,1,0:T(1,128)S(1)} %get-tuple-element.39), channel_id=1, replica_groups=mesh['gx'=8,'gy'=4,'af'=4] {'gx','gy','af'}, dimensions={0} | all-to-all | bytes 393216 | tf_op jit(solution)/shard_map/all_to_all | solution.py:477
  45.7 2.3 %step.7 = (f32[128,1,256]{2,1,0:T(1,128)S(1)}, f32[8,24,128]{2,1,0:T(8,128)S(1)}, f32[8,128]{1,0:T(8,128)S(1)}, f32[8,128]{1,0:T(8,128)S(1)}, f32[4,256]{1,0:T(4,128)}) custom-call(s32[1]{0:T(128)} %bitcast.me_ref.refs_0_, f32[128,1,384]{2,1,0:T(1,128)S(1)} %all_to_all.40.refs_1_, f32[7,8,24,128]{3,2,1,0:T(8,128)S(1)} %get-tuple-element.40.refs_2_, ...), custom_call_target="tpu_custom_call" | custom-call | tf_op jit(solution)/shard_map/step/pallas_call | solution.py:465
  48.0 14.2 %all_to_all.41.refs_1_ = f32[128,1,256]{2,1,0:T(1,128)S(1)} all-to-all(f32[128,1,256]{2,1,0:T(1,128)S(1)} %get-tuple-element.47), channel_id=1, replica_groups=mesh['gx'=8,'gy'=4,'af'=4] {'gx','gy','af'}, dimensions={0} | all-to-all | bytes 262144 | tf_op jit(solution)/shard_map/all_to_all | solution.py:477
  62.2 1.3 step.8
  63.5 14.2 %all_to_all.42.refs_1_ = f32[128,1,256]{2,1,0:T(1,128)S(1)} all-to-all(f32[128,1,256]{2,1,0:T(1,128)S(1)} %get-tuple-element.51), channel_id=1, replica_groups=mesh['gx'=8,'gy'=4,'af'=4] {'gx','gy','af'}, dimensions={0} | all-to-all | bytes 262144 | tf_op jit(solution)/shard_map/all_to_all | solution.py:477
  77.7 1.3 step.9
  78.9 14.2 %all_to_all.43.refs_1_ = f32[128,1,256]{2,1,0:T(1,128)S(1)} all-to-all(f32[128,1,256]{2,1,0:T(1,128)S(1)} %get-tuple-element.54), channel_id=1, replica_groups=mesh['gx'=8,'gy'=4,'af'=4] {'gx','gy','af'}, dimensions={0} | all-to-all | bytes 262144 | tf_op jit(solution)/shard_map/all_to_all | solution.py:477
  93.1 1.3 step.10
  94.4 14.2 %all_to_all.44.refs_1_ = f32[128,1,256]{2,1,0:T(1,128)S(1)} all-to-all(f32[128,1,256]{2,1,0:T(1,128)S(1)} %get-tuple-element.57), channel_id=1, replica_groups=mesh['gx'=8,'gy'=4,'af'=4] {'gx','gy','af'}, dimensions={0} | all-to-all | bytes 262144 | tf_op jit(solution)/shard_map/all_to_all | solution.py:477
  108.6 1.3 step.11
  109.9 14.2 %all_to_all.45.refs_1_ = f32[128,1,256]{2,1,0:T(1,128)S(1)} all-to-all(f32[128,1,256]{2,1,0:T(1,128)S(1)} %get-tuple-element.60), channel_id=1, replica_groups=mesh['gx'=8,'gy'=4,'af'=4] {'gx','gy','af'}, dimensions={0} | all-to-all | bytes 262144 | tf_op jit(solution)/shard_map/all_to_all | solution.py:477
  124.0 1.3 step.12
  125.3 14.2 %all_to_all.46.refs_1_ = f32[128,1,256]{2,1,0:T(1,128)S(1)} all-to-all(f32[128,1,256]{2,1,0:T(1,128)S(1)} %get-tuple-element.63), channel_id=1, replica_groups=mesh['gx'=8,'gy'=4,'af'=4] {'gx','gy','af'}, dimensions={0} | all-to-all | bytes 262144 | tf_op jit(solution)/shard_map/all_to_all | solution.py:477
  139.5 1.4 %step.13 = (f32[8,8,128]{2,1,0:T(8,128)}, f32[4,256]{1,0:T(4,128)}) custom-call(s32[1]{0:T(128)} %bitcast.me_ref.refs_0_, f32[128,1,256]{2,1,0:T(1,128)S(1)} %all_to_all.46.refs_1_, f32[7,8,24,128]{3,2,1,0:T(8,128)S(1)} %get-tuple-element.40.refs_2_, f32[8,24,128]{2,1,0:T(8,128)S(1)} %get-tuple-element.64.refs_3_, s32[16,128]{1,0:T(8,128)S(1)} %get-tuple-element.42.refs_4_, ...), custom_call_target="tpu_custom_call" | custom-call | tf_op jit(solution)/shard_map/step/pallas_call | solution.py:465
  (1 shorter events, 0.0 us)
Async XLA Ops:
  3.9 22.3 %all-to-all-start = ((f32[128,1,384]{2,1,0:T(1,128)}), f32[128,1,384]{2,1,0:T(1,128)S(1)}, u32[]{:S(2)}, u32[]{:S(2)}) async-start(f32[128,1,384]{2,1,0:T(1,128)} %get-tuple-element.36), calls=%async_computation | async-start | bytes 393216 | tf_op jit(solution)/shard_map/all_to_all | solution.py:477
  16.2 6.3 %collective-permute-start.1 = (f32[3,8,8,128]{3,2,1,0:T(8,128)S(1)}, f32[3,8,8,128]{3,2,1,0:T(8,128)S(1)}, u32[]{:S(2)}, u32[]{:S(2)}) collective-permute-start(f32[3,8,8,128]{3,2,1,0:T(8,128)S(1)} %pad_maximum_fusion.middle_ref), channel_id=1, source_target_pairs={{16,32},{48,64},{80,96},{32,16},{64,48},{96,80},{17,33},{49,65},{8... | collective-permute-start | bytes 294920 | tf_op jit(solution)/shard_map/ppermute | solution.py:482
  19.7 2.8 %collective-permute-start = (f32[3,8,8,128]{3,2,1,0:T(8,128)S(1)}, f32[3,8,8,128]{3,2,1,0:T(8,128)S(1)}, u32[]{:S(2)}, u32[]{:S(2)}) collective-permute-start(f32[3,8,8,128]{3,2,1,0:T(8,128)S(1)} %pad_maximum_fusion.middle_ref), channel_id=1, source_target_pairs={{0,16},{32,48},{64,80},{96,112},{16,0},{48,32},{80,64},{112,96},{1... | collective-permute-start | bytes 294920 | tf_op jit(solution)/shard_map/ppermute | solution.py:482
  26.2 0.8 copy-start

commit v3 on v2

--- a/solution.py
+++ b/solution.py
@@ -14,6 +14,7 @@
 SLOTS = CAP * TILES
 ALL = ("gx", "gy", "af")
 YA = ("gy", "af")
+BESIDE = (17, 1, -15, 15, -1, -17)
 f32 = jnp.float32
 bf16 = jnp.bfloat16
 i32 = jnp.int32
@@ -259,8 +260,8 @@
         partial = partial - jnp.where(at, trans_ref[b] * total(jnp.where(code == here, press, 0.0)), 0.0)
     where_cell = (fold(layer_ref[...]) * 1024 + fold(cell_ref[...]) + 1).astype(f32)
     position = (iota((8, 128), 0) * 128 + iota((8, 128), 1) + 1).astype(f32)
-    slots = to_slots([where_cell, mf * press, fm * inverse * fm, position], hot, mask)
-    inverse_index, slots = slots[48:64], slots[:48]
+    slots = to_slots([where_cell, mf * press, fm * inverse * fm, fm * inverse * mf, position], hot, mask)
+    inverse_index, slots = slots[64:80], slots[:64]
     place = (owner * CAP + rank).astype(f32)
     edges = []
     for b in range(4):
@@ -268,15 +269,15 @@
         at = code == b * 256 + from_ref[b]
         gain = trans_ref[b] * inverse
         edges.append(jnp.full((1, 128), there.astype(f32)))
-        for value in (place, where_cell, gain * fm, gain * partial, gain * trans_ref[b]):
+        for value in (place, where_cell, gain * fm, gain * partial, gain * trans_ref[b], gain * mf, code.astype(f32), gain):
             edges.append(jnp.broadcast_to(total(jnp.where(at, value, 0.0)), (1, 128)))
-        edges.append(jnp.full((1, 128), trans_ref[b]))
-        edges.append(jnp.zeros((1, 128), f32))
-    rows = [spread(slots, 16), slots, spread(slots, -16)] + edges + [jnp.zeros((80, 128), f32)]
+        edges.append(jnp.zeros((3, 128), f32))
+    rows = [spread(slots, 16), slots, spread(slots, -16)] + edges
+    rows += [spread(slots[:CAP], shift) for shift in BESIDE] + [jnp.zeros((48, 128), f32)]
     store_slots(out_ref, jnp.concatenate(rows, axis=0))
     first_face, last_face = faces_of(jnp.concatenate([press_ref[...].reshape(ROWS, 128), cond_ref[...].reshape(ROWS, 128)], axis=0))
     for across in (-16, 0, 16):
-        put_faces(me, out_ref, 256, first_face, last_face, across)
+        put_faces(me, out_ref, 384, first_face, last_face, across)
     for i, value in enumerate((tnext, inverse, partial, fm, mf, owner.astype(f32), rank.astype(f32), press)):
         seg_ref[i] = value
     for i in range(2):
@@ -299,20 +300,21 @@
         source = source + jnp.where(at, well_rate_ref[w], 0.0)
     for i in range(3):
         seg_ref[11 + i] = source[8 * i : 8 * i + 8]
+    seg_ref[14] = where_cell
 
 
 def edge_in(row, k, i):
-    at = 16 + 8 * k + i
+    at = 64 + 12 * k + i
     return row[:, at : at + 1]
 
 
 def cells_kernel(
     me_ref,
     got_ref, middle_ref, inside_ref, across_ref, seg_ref,
-    out_ref, cells_ref, field_ref, index_ref, columns_ref, rows_ref, edge_ref, res_ref,
+    out_ref, cells_ref, field_ref, index_ref, columns_ref, rows_ref, edge_ref, beside_ref, res_ref,
 ):
     me = me_ref[0]
-    slots = load_slots(got_ref, 256)
+    slots = load_slots(got_ref, 384)
     even = ((me >> 4) & 1) == 0
     press, cond, accum = (
         jnp.concatenate([jnp.where(even, b, a), middle_ref[i], jnp.where(even, a, b)], axis=1)
@@ -320,7 +322,7 @@
     )
     sums = []
     for side in range(3):
-        table = slots[side * 48 : side * 48 + 48]
+        table = slots[side * 64 : side * 64 + 64]
         index = table[:CAP].astype(i32) - 1
         if side == 1:
             index_ref[...] = index
@@ -328,10 +330,15 @@
         columns, rows = cell_hot(as_row(index))
         columns_ref[side] = columns
         rows_ref[side] = rows
-        sums.append(scatter([table[16:32], table[32:48]], columns, rows))
-    flow, weight = (jnp.concatenate([sums[side][i] for side in range(3)], axis=1) for i in range(2))
-
-    halos = [columns_of(*read_faces(me, got_ref, 256, 2 * ROWS, across)) for across in (-16, 0, 16)]
+        sums.append(scatter([table[16:32], table[32:48], table[48:64]], columns, rows))
+    flow, weight, mirror = (jnp.concatenate([sums[side][i] for side in range(3)], axis=1) for i in range(3))
+    beside = slots[240:336].astype(i32) - 1
+    along = me & 15
+    for i, (there, column) in enumerate(((along > 0, 127), (along < 15, 0))):
+        part = beside[48 * i : 48 * i + 48]
+        beside_ref[48 * i : 48 * i + 48] = jnp.where(there & (part >= 0) & ((part & 127) == column), part >> 7, -1)
+
+    halos = [columns_of(*read_faces(me, got_ref, 384, 2 * ROWS, across)) for across in (-16, 0, 16)]
     press_halo = jnp.concatenate([halo[:ROWS].reshape(LAYERS, 8, 128) for halo in halos], axis=1)
     cond_halo = jnp.concatenate([halo[ROWS:].reshape(LAYERS, 8, 128) for halo in halos], axis=1)
     lane = iota((LAYERS, EXT, 128), 2)
@@ -345,16 +352,16 @@
     source = jnp.concatenate([seg_ref[11 + i] for i in range(3)], axis=0)
     res = diag * press - stencil(tx, ty, tz, ty_first, press, press_halo) - flow - source[None]
     field = inverse * res
-    for i, value in enumerate((tx, ty, tz, ty_first, inverse, res, weight * press)):
+    for i, value in enumerate((tx, ty, tz, ty_first, inverse, res, weight * press, mirror)):
         cells_ref[i] = value
     field_ref[...] = field
     res_ref[...] = res[:, 8:16]
 
     code = seg_code().astype(f32)
-    _, inverse_f, partial, fm, _, _, _, press_f = (seg_ref[i] for i in range(8))
+    _, inverse_f, partial, fm, _, owner, _, press_f = (seg_ref[i] for i in range(8))
     edge = jnp.where(me > 0, got_ref[jnp.maximum(me - 1, 0), :, 128:256], -1.0)
     lane = iota((1, 128), 1)
-    cells, terms, picks = [], [], []
+    cells, terms, picks, found = [], [], [], []
     for k in range(4):
         there = edge_in(edge, k, 0)
         picked = total(jnp.where(code == there, press_f, 0.0))
@@ -362,7 +369,8 @@
         cells.append(jnp.where(at, edge_in(edge, k, 2), 0.0))
         terms.append(jnp.where(at, -edge_in(edge, k, 3) * picked, 0.0))
         picks.append(jnp.broadcast_to(picked, (1, 128)))
-        edge = jnp.where(lane == 16 + 8 * k + 4, edge - edge_in(edge, k, 5) * picked, edge)
+        found.append([total(jnp.where(code == there, value, 0.0)) for value in (owner, seg_ref[14], fm * inverse_f)])
+        edge = jnp.where(lane == 64 + 12 * k + 4, edge - edge_in(edge, k, 5) * picked, edge)
     edge_ref[...] = jnp.broadcast_to(edge, (8, 128))
     late = jnp.concatenate(cells + terms, axis=0)
     position = jnp.concatenate([seg_ref[8], seg_ref[9]], axis=0).astype(i32)
@@ -372,91 +380,264 @@
     rows = taken + [spread(taken[0], 1)]
     rows += [spread(first, 16), first, spread(first, -16), spread(late, 16), late, spread(late, -16)]
     store_slots(out_ref, jnp.concatenate(rows + picks + [jnp.zeros((4, 128), f32)], axis=0))
-    put_faces(me, out_ref, 128, *faces_of(field.reshape(LAYERS * EXT, 128)))
-
-
-def step_kernel(
-    first, final,
-    me_ref,
-    got_ref, cells_ref, field_ref, index_ref, columns_ref, rows_ref, seg_ref, edge_ref, *rest,
+    begin, end = faces_of(field.reshape(LAYERS * EXT, 128))
+    begin_inverse, end_inverse = faces_of(inverse.reshape(LAYERS * EXT, 128))
+    for k, (tile, cell, weight_there) in enumerate(found):
+        begin = put_entry(begin, k, tile)
+        begin = put_entry(begin, 4 + k, cell)
+        begin_inverse = put_entry(begin_inverse, k, weight_there)
+    put_faces(me, out_ref, 128, begin, end)
+    put_faces(me, out_ref, 320, begin_inverse, end_inverse)
+
+
+def put_entry(face, k, value):
+    return jnp.where(iota(face.shape, 1) == EXT * k, value, face)
+
+
+def get_entry(face, k):
+    return face[:, EXT * k : EXT * k + 1]
+
+
+def own_edges(seg_ref):
+    own = seg_ref[10][0:1]
+    return [[own[:, 8 * b + i : 8 * b + i + 1] for b in range(4)] for i in range(4)]
+
+
+def edge_terms(code, edges, frac):
+    starts, _, _, factors = edges
+    return [factor * total(jnp.where(code == start, frac, 0.0)) for start, factor in zip(starts, factors)]
+
+
+def arrive(code, targets, terms):
+    gain = jnp.zeros(code.shape, f32)
+    for target, term in zip(targets, terms):
+        gain = gain + jnp.where(code == target, term, 0.0)
+    return gain
+
+
+def late_rows(edges, ends, terms):
+    lane = iota((1, 128), 1)
+    cells, values = [], []
+    for there, (tile, cell, weight), term in zip(edges[2], ends, terms):
+        at = (lane == tile.astype(i32)) & (there >= 0.0)
+        cells.append(jnp.where(at, cell, 0.0))
+        values.append(jnp.where(at, weight * term, 0.0))
+    return jnp.concatenate(cells + values, axis=0)
+
+
+def to_three(rows):
+    return [spread(rows, 16), rows, spread(rows, -16)]
+
+
+def scatter_late(late):
+    return scatter([late[4:]], *cell_hot(as_row(late[:4].astype(i32) - 1)))[0]
+
+
+def own_tile(field):
+    return field[:, 8:16].reshape(ROWS, 128)
+
+
+def start_of(edge, k, table):
+    place = (iota((CAP, 128), 1) * CAP + iota((CAP, 128), 0)).astype(f32)
+    return total(jnp.where(place == edge_in(edge, k, 1), table, 0.0))
+
+
+def advance(cells_ref, field, halo, flow):
+    tx, ty, tz, ty_first, inverse, res = (cells_ref[i] for i in range(6))
+    return inverse * (res + stencil(tx, ty, tz, ty_first, field, halo) + flow)
+
+
+def wide_halo(me, got_ref, start):
+    return columns_of(*read_faces(me, got_ref, start, LAYERS * EXT)).reshape(LAYERS, EXT, 128)
+
+
+def ends_of(ends_ref):
+    held = ends_ref[0:1]
+    return [[held[:, 3 * k + i : 3 * k + i + 1] for i in range(3)] for k in range(4)]
+
+
+def send_wide(me, out_ref, code, edges, ends, seg_ref, cells_ref, index_ref, field, frac, resf):
+    tnext, inverse_f, fm = seg_ref[0], seg_ref[1], seg_ref[3]
+    terms = edge_terms(code, edges, frac)
+    ahead = inverse_f * (resf + chain(tnext, frac) + arrive(code, edges[1], terms))
+    part = advance(cells_ref, field, jnp.zeros((LAYERS, EXT, 128), f32), 0.0)
+    position = jnp.concatenate([seg_ref[8], seg_ref[9]], axis=0).astype(i32)
+    now = find(fm * frac, position)
+    rows = [find(own_tile(field), index_ref[...])] + to_three(now) + to_three(find(fm * ahead, position))
+    rows += to_three(late_rows(edges, ends, terms)) + [spread(now, shift) for shift in BESIDE]
+    store_slots(out_ref, jnp.concatenate(rows + [jnp.zeros((24, 128), f32)], axis=0))
+    begin, end = faces_of(field.reshape(LAYERS * EXT, 128))
+    for b in range(4):
+        end = put_entry(end, b, terms[b])
+    put_faces(me, out_ref, 256, begin, end)
+    put_faces(me, out_ref, 448, *faces_of(part.reshape(LAYERS * EXT, 128)))
+
+
+def first_kernel(
+    me_ref, got_ref, cells_ref, field_ref, index_ref, columns_ref, rows_ref, seg_ref, edge_ref,
+    out_ref, new_field_ref, new_frac_ref, resf_ref, ends_ref, halo_inverse_ref, res_fracture_ref,
 ):
     me = me_ref[0]
-    if not first:
-        frac_ref, resf_ref, *rest = rest
     slots = load_slots(got_ref, 128)
     code = seg_code().astype(f32)
     tnext, inverse_f, partial, fm, mf, owner, rank = (seg_ref[i] for i in range(7))
     owner = owner.astype(i32)
     rank = rank.astype(i32)
     edge = edge_ref[0:1]
-    own = seg_ref[10][0:1]
-    starts, targets, nexts, factors = ([own[:, 8 * b + i : 8 * b + i + 1] for b in range(4)] for i in range(4))
-
-    if first:
-        resf = partial - fm * look_up(slots[0:16], rank, owner)
-        after = got_ref[jnp.minimum(me + 1, TILES - 1), :, 0:128]
-        for b in range(4):
-            at = (code == starts[b]) & (nexts[b] >= 0.0)
-            resf = resf - jnp.where(at, factors[b] * after[:, 120 + b : 121 + b], 0.0)
-        frac = inverse_f * resf
-        here = look_up(slots[16:32], rank, owner)
-    else:
-        resf = resf_ref[...]
-        frac = frac_ref[...]
-        here = look_up(slots[0:16], rank, owner)
-    gain = resf + chain(tnext, frac) + mf * here
-    before = got_ref[jnp.maximum(me - 1, 0), :, 64:256]
+    edges = own_edges(seg_ref)
+    starts, targets, nexts, factors = edges
+
+    resf = partial - fm * look_up(slots[0:16], rank, owner)
+    after = got_ref[jnp.minimum(me + 1, TILES - 1), :, :]
     for b in range(4):
-        term = factors[b] * total(jnp.where(code == starts[b], frac, 0.0))
-        gain = gain + jnp.where(code == targets[b], term, 0.0)
-        if first:
-            place = (iota((CAP, 128), 1) * CAP + iota((CAP, 128), 0)).astype(f32)
-            there = total(jnp.where(place == edge_in(edge, b, 1), slots[32:48], 0.0))
-            term = edge_in(edge, b, 4) - edge_in(edge, b, 3) * there
-        else:
-            term = before[:, EXT * b : EXT * b + 1]
-        gain = gain + jnp.where(code == edge_in(edge, b, 0), term, 0.0)
+        at = (code == starts[b]) & (nexts[b] >= 0.0)
+        resf = resf - jnp.where(at, factors[b] * after[:, 120 + b : 121 + b], 0.0)
+    frac = inverse_f * resf
+    terms = edge_terms(code, edges, frac)
+    before = [edge_in(edge, k, 4) - edge_in(edge, k, 3) * start_of(edge, k, slots[32:48]) for k in range(4)]
+    gain = resf + chain(tnext, frac) + mf * look_up(slots[16:32], rank, owner)
+    gain = gain + arrive(code, targets, terms) + arrive(code, [edge_in(edge, k, 0) for k in range(4)], before)
     frac = inverse_f * gain
-
-    tx, ty, tz, ty_first, inverse, res = (cells_ref[i] for i in range(6))
-    field = field_ref[...]
+    flow = []
+    for side in range(3):
+        sums = scatter([slots[48 + side * CAP : 64 + side * CAP]], columns_ref[side], rows_ref[side])
+        flow.append(sums[0] + scatter_late(slots[96 + 8 * side : 104 + 8 * side]))
+    flow = jnp.concatenate(flow, axis=1) - cells_ref[6]
+    field = advance(cells_ref, field_ref[...], wide_halo(me, got_ref, 128), flow)
+    new_field_ref[...] = field
+    new_frac_ref[...] = frac
+    resf_ref[...] = resf
+    res_fracture_ref[...] = unfold(resf)
+    halo_inverse_ref[...] = wide_halo(me, got_ref, 320)
+    face, weights = after[:, 128:320], after[:, 320:512]
+    ends = [(get_entry(face, k), get_entry(face, 4 + k), get_entry(weights, k)) for k in range(4)]
+    lane = iota((8, 128), 1)
+    held = jnp.zeros((8, 128), f32)
+    for k in range(4):
+        for i in range(3):
+            held = jnp.where(lane == 3 * k + i, ends[k][i], held)
+    ends_ref[...] = held
+
+    send_wide(me, out_ref, code, edges, ends, seg_ref, cells_ref, index_ref, field, frac, resf)
+
+
+def even_kernel(
+    me_ref, got_ref, cells_ref, field_ref, index_ref, columns_ref, rows_ref, seg_ref, edge_ref,
+    frac_ref, resf_ref, ends_ref, halo_inverse_ref, beside_ref,
+    out_ref, third_ref, new_field_ref, new_frac_ref,
+):
+    me = me_ref[0]
+    slots = load_slots(got_ref, 256)
+    code = seg_code().astype(f32)
+    tnext, inverse_f, _, fm, mf, owner, rank = (seg_ref[i] for i in range(7))
+    edge = edge_ref[0:1]
+    edges = own_edges(seg_ref)
+    targets = edges[1]
+    resf = resf_ref[...]
+    frac = frac_ref[...]
+    before = got_ref[jnp.maximum(me - 1, 0), :, 256:448]
+    gain = resf + chain(tnext, frac) + mf * look_up(slots[0:16], rank.astype(i32), owner.astype(i32))
+    gain = gain + arrive(code, targets, edge_terms(code, edges, frac))
+    gain = gain + arrive(code, [edge_in(edge, k, 0) for k in range(4)], [get_entry(before, k) for k in range(4)])
+    frac = inverse_f * gain
+    terms = edge_terms(code, edges, frac)
+    ahead = inverse_f * (resf + chain(tnext, frac) + arrive(code, targets, terms))
+    new_frac_ref[...] = frac
+
+    flow, later, beside = [], [], []
+    lane = iota((ROWS, 128), 1)
+    level = iota((ROWS, 128), 0)
+    for side in range(3):
+        start = 16 + side * CAP
+        sums = scatter([slots[start : start + CAP], slots[start + 48 : start + 48 + CAP]], columns_ref[side], rows_ref[side])
+        flow.append(sums[0])
+        later.append(sums[1] + scatter_late(slots[112 + 8 * side : 120 + 8 * side]))
+        column = jnp.zeros((ROWS, 128), f32)
+        for i, at in enumerate((0, 127)):
+            first = 48 * i + CAP * side
+            held = jnp.zeros((ROWS, 128), f32)
+            for r in range(first, first + CAP):
+                held = held + jnp.where(level == beside_ref[r : r + 1], slots[136 + r : 137 + r], 0.0)
+            column = jnp.where(lane == at, jnp.sum(held, axis=1, keepdims=True), column)
+        beside.append(column.reshape(LAYERS, 8, 128))
+    flow, later, beside = (jnp.concatenate(parts_x, axis=1) for parts_x in (flow, later, beside))
+    second = field_ref[...]
+    third = advance(cells_ref, second, wide_halo(me, got_ref, 256), flow)
+    lane = iota((LAYERS, EXT, 128), 2)
+    joint = jnp.where(lane == 0, cells_ref[3], jnp.where(lane == 127, cells_ref[1], 0.0))
+    halo = wide_halo(me, got_ref, 448) + halo_inverse_ref[...] * (joint * second + beside)
+    field = advance(cells_ref, third, halo, later + cells_ref[7] * second)
+    third_ref[...] = third
+    new_field_ref[...] = field
+
+    position = jnp.concatenate([seg_ref[8], seg_ref[9]], axis=0).astype(i32)
+    ends = ends_of(ends_ref)
+    own_third = find(own_tile(third), index_ref[...])
+    rows = [own_third, find(own_tile(field), index_ref[...]), spread(own_third, 1)] + to_three(find(fm * ahead, position))
+    rows += to_three(late_rows(edges, ends, terms))
+    store_slots(out_ref, jnp.concatenate(rows + [jnp.zeros((8, 128), f32)], axis=0))
+    begin, end = faces_of(field.reshape(LAYERS * EXT, 128))
+    for b, term in enumerate(terms + edge_terms(code, edges, ahead)):
+        end = put_entry(end, b, term)
+    put_faces(me, out_ref, 128, begin, end)
+    lane = iota((1, 64), 1)
+    two = jnp.zeros((1, 64), f32)
+    for b in range(4):
+        two = jnp.where(lane == b, terms[b], jnp.where(lane == 4 + b, edges[2][b], two))
+    out_ref[jnp.where(me + 2 < TILES, me + 2, me), :, 320:384] = two
+
+
+def odd_kernel(
+    final, me_ref, got_ref, cells_ref, field_ref, index_ref, columns_ref, rows_ref, seg_ref, edge_ref,
+    frac_ref, resf_ref, ends_ref, third_ref, *outs,
+):
+    me = me_ref[0]
+    slots = load_slots(got_ref, 128)
+    code = seg_code().astype(f32)
+    tnext, inverse_f, _, _, mf, owner, rank = (seg_ref[i] for i in range(7))
+    owner = owner.astype(i32)
+    rank = rank.astype(i32)
+    edge = edge_ref[0:1]
+    edges = own_edges(seg_ref)
+    targets = edges[1]
+    resf = resf_ref[...]
+    frac = frac_ref[...]
+    before = got_ref[jnp.maximum(me - 1, 0), :, 128:320]
+    two = jnp.where(me > 1, got_ref[jnp.maximum(me - 2, 0), :, 320:384], -1.0)
+    heres = [edge_in(edge, k, 0) for k in range(4)]
+    gain = resf + chain(tnext, frac) + mf * look_up(slots[0:16], rank, owner)
+    gain = gain + arrive(code, targets, edge_terms(code, edges, frac))
+    frac = inverse_f * (gain + arrive(code, heres, [get_entry(before, k) for k in range(4)]))
+    terms = []
+    for k in range(4):
+        term = get_entry(before, 4 + k) + edge_in(edge, k, 6) * start_of(edge, k, slots[32:48])
+        for j in range(4):
+            meets = two[:, 4 + j : 5 + j] == edge_in(edge, k, 7)
+            term = term + jnp.where(meets, edge_in(edge, k, 8) * two[:, j : j + 1], 0.0)
+        terms.append(term)
+    gain = resf + chain(tnext, frac) + mf * look_up(slots[16:32], rank, owner)
+    gain = gain + arrive(code, targets, edge_terms(code, edges, frac))
+    frac = inverse_f * (gain + arrive(code, heres, terms))
+
     flow = []
     for side in range(3):
         if final and side != 1:
             flow.append(jnp.zeros((LAYERS, 8, 128), f32))
             continue
-        start = (48 if first else 16) + side * CAP
-        flow.extend(scatter([slots[start : start + CAP]], columns_ref[side], rows_ref[side]))
-        if first:
-            late = slots[96 + 8 * side : 104 + 8 * side]
-            more = scatter([late[4:]], *cell_hot(as_row(late[:4].astype(i32) - 1)))
-            flow[side] = flow[side] + more[0]
-    flow = jnp.concatenate(flow, axis=1)
-    if first:
-        flow = flow - cells_ref[6]
-    halo = columns_of(*read_faces(me, got_ref, 128 if first else 64, LAYERS * EXT)).reshape(LAYERS, EXT, 128)
-    field = inverse * (res + stencil(tx, ty, tz, ty_first, field, halo) + flow)
-
+        start = 48 + side * CAP
+        sums = scatter([slots[start : start + CAP]], columns_ref[side], rows_ref[side])
+        flow.append(sums[0] + scatter_late(slots[96 + 8 * side : 104 + 8 * side]))
+    flow = jnp.concatenate(flow, axis=1) + cells_ref[7] * third_ref[...]
+    field = advance(cells_ref, field_ref[...], wide_halo(me, got_ref, 128), flow)
     if final:
-        adj_matrix_ref, adj_fracture_ref = rest
+        adj_matrix_ref, adj_fracture_ref = outs
         adj_matrix_ref[...] = field[:, 8:16]
         adj_fracture_ref[...] = unfold(frac)
         return
-    out_ref, new_field_ref, new_frac_ref = rest[:3]
-    if first:
-        resf_out_ref, res_fracture_ref = rest[3:]
-        resf_out_ref[...] = resf
-        res_fracture_ref[...] = unfold(resf)
+    out_ref, new_field_ref, new_frac_ref = outs
     new_field_ref[...] = field
     new_frac_ref[...] = frac
-    taken = [find(field[:, 8:16].reshape(ROWS, 128), index_ref[...])]
-    terms = find(fm * frac, jnp.concatenate([seg_ref[8], seg_ref[9]], axis=0).astype(i32))
-    store_slots(out_ref, jnp.concatenate(taken + [spread(terms, 16), terms, spread(terms, -16)], axis=0))
-    begin, end = faces_of(field.reshape(LAYERS * EXT, 128))
-    lane = iota(end.shape, 1)
-    for b in range(4):
-        end = jnp.where(lane == EXT * b, factors[b] * total(jnp.where(code == starts[b], frac, 0.0)), end)
-    put_faces(me, out_ref, 64, begin, end)
+    send_wide(me, out_ref, code, edges, ends_of(ends_ref), seg_ref, cells_ref, index_ref, field, frac, resf)
 
 
 def call(kernel, name, scalars, arrays, outs, space=pltpu.VMEM, scratch=(), limit=20 * 1024 * 1024):
@@ -500,37 +681,49 @@
         "begin",
         (me, inter_delta, inter_from, inter_to, inter_trans, well_tile, well_cell, well_rate),
         given,
-        [((TILES, 1, 384), f32), ((14, *seg), f32)],
+        [((TILES, 1, 512), f32), ((15, *seg), f32)],
         pl.ANY,
         [pltpu.VMEM(a.shape, a.dtype) for a in given] + [pltpu.SemaphoreType.DMA((len(given),))],
         64 * 1024 * 1024,
     )
     got = exchange(message)
-    message, cells, field, index, columns, rows, edge, res_matrix = call(
+    message, cells, field, index, columns, rows, edge, beside, res_matrix = call(
         cells_kernel,
         "cells",
         (me,),
         (got, stacked, inside, across, segs),
-        [((TILES, 1, 384), f32), ((7, *wide), f32), (wide, f32), ((CAP, 128), i32), ((3, 128, SLOTS), bf16),
-         ((3, ROWS, SLOTS), bf16), (seg, f32), (tile, f32)],
+        [((TILES, 1, 512), f32), ((8, *wide), f32), (wide, f32), ((CAP, 128), i32), ((3, 128, SLOTS), bf16),
+         ((3, ROWS, SLOTS), bf16), (seg, f32), ((96, 128), i32), (tile, f32)],
     )
+    kept = (index, columns, rows, segs, edge)
+    going = [(wide, f32), (seg, f32)]
     got = exchange(message)
-
-    def step(first, final, got, field, more, outs):
-        def kernel(*refs):
-            step_kernel(first, final, *refs)
-
-        return call(kernel, "step", (me,), (got, cells, field, index, columns, rows, segs, edge, *more), outs)
-
-    going = [((TILES, 1, 256), f32), (wide, f32), (seg, f32)]
-    message, field, frac, resf, res_fracture = step(
-        True, False, got, field, (), going + [(seg, f32), ((4, 256), f32)]
+    message, field, frac, resf, ends, halo_inverse, res_fracture = call(
+        first_kernel,
+        "first",
+        (me,),
+        (got, cells, field, *kept),
+        [((TILES, 1, 640), f32), *going, (seg, f32), (seg, f32), (wide, f32), ((4, 256), f32)],
     )
-    for _ in range(ITERS - 3):
+    for final in (False, True):
         got = exchange(message)
-        message, field, frac = step(False, False, got, field, (frac, resf), going)
-    got = exchange(message)
-    adj_matrix, adj_fracture = step(False, True, got, field, (frac, resf), [(tile, f32), ((4, 256), f32)])
+        message, third, field, frac = call(
+            even_kernel,
+            "even",
+            (me,),
+            (got, cells, field, *kept, frac, resf, ends, halo_inverse, beside),
+            [((TILES, 1, 384), f32), (wide, f32), *going],
+        )
+        got = exchange(message)
+
+        def kernel(*refs, final=final):
+            odd_kernel(final, *refs)
+
+        outs = [(tile, f32), ((4, 256), f32)] if final else [((TILES, 1, 640), f32), *going]
+        results = call(kernel, "odd", (me,), (got, cells, field, *kept, frac, resf, ends, third), outs)
+        if not final:
+            message, field, frac = results
+    adj_matrix, adj_fracture = results
     return res_matrix, res_fracture, adj_matrix, adj_fracture
 
 

time: 141 us -> 119 us (0.84)
  blocking collectives: 101 us -> 77.3 us
  Pallas kernels: 15.7 us -> 17.2 us
    all_to_all x7 -> x5, blocking collectives: 101 us -> 77.3 us  [exchange(): return lax.all_to_all(message, ALL, split_axis=0, concat_axis=0, tiled=True)]
    pallas_call x9 -> x7, Pallas kernels: 15.7 us -> 17.2 us  [call(): pl.pallas_call(kernel, name=name, out_shape=[jax.ShapeDtypeStruct(shape,...]
where the time goes in v3:
time: 119 us
  blocking collectives  77.3 us (65%)
  Pallas kernels  17.2 us (14%)
  starting transfers between devices  15.1 us (13%)
  waiting for transfers between devices  7.03 us (6%)
    all_to_all x5, blocking collectives, exchange(): return lax.all_to_all(message, ALL, split_axis=0, concat_axis=0, tiled=True)  77.3 us
    pallas_call x7, Pallas kernels, call(): pl.pallas_call(kernel, name=name, out_shape=[jax.ShapeDtypeStruct(shape,...  17.2 us
    all_to_all x1, starting transfers between devices, exchange(): return lax.all_to_all(message, ALL, split_axis=0, concat_axis=0, tiled=True)  11.5 us
    all_to_all x1, waiting for transfers between devices, exchange(): return lax.all_to_all(message, ALL, split_axis=0, concat_axis=0, tiled=True)  3.99 us
    ppermute x2, starting transfers between devices, swapped(): return lax.ppermute(block, 'gx', pairs + [(j, i) for i, j in pairs])  3.62 us
    ppermute x2, waiting for transfers between devices, swapped(): return lax.ppermute(block, 'gx', pairs + [(j, i) for i, j in pairs])  3.04 us
  transfers between devices with their start and end apart: 3, of which 2 were waited for; matrix products, arithmetic and copies ran while one was open for 1% of the time, Pallas kernels for 0%

profile of v3, /device:TPU:1, one launch (start us, length us, event | category | flops | bytes accessed | tf_op | source)
XLA Modules:
  0.0 119.0 jit_solution(11523738635231080768)
XLA Ops:
  0.6 3.3 %begin.1 = (f32[128,1,512]{2,1,0:T(1,128)}, f32[15,8,128]{2,1,0:T(8,128)}) custom-call(s32[1]{0:T(128)} %bitcast.me_ref.refs_0_, s32[4]{0:T(128)} %delta_ref.1, s32[4]{0:T(128)} %from_ref.1, s32[4]{0:T(128)} %to_ref.1, f32[4]{0:T(128)} %trans_ref.1, s32[32]{0:T(128)} %well_tile_ref.1, s32[32]{0:T(128)} %well_cell_ref.1, f32[32]{0:T(128)} %well_rate_ref.1, ...), custom_call_target="tpu_custom_call" | custom-call | tf_op jit(solution)/shard_map/begin/pallas_call | solution.py:646
  3.9 11.5 %all-to-all-start = ((f32[128,1,512]{2,1,0:T(1,128)}), f32[128,1,512]{2,1,0:T(1,128)S(1)}, u32[]{:S(2)}, u32[]{:S(2)}) async-start(f32[128,1,512]{2,1,0:T(1,128)} %get-tuple-element.35), calls=%async_computation | async-start | bytes 524288 | tf_op jit(solution)/shard_map/all_to_all | solution.py:658
  15.4 0.8 pad_maximum_fusion.middle_ref
  16.2 3.5 %collective-permute-start.1 = (f32[3,8,8,128]{3,2,1,0:T(8,128)S(1)}, f32[3,8,8,128]{3,2,1,0:T(8,128)S(1)}, u32[]{:S(2)}, u32[]{:S(2)}) collective-permute-start(f32[3,8,8,128]{3,2,1,0:T(8,128)S(1)} %pad_maximum_fusion.middle_ref), channel_id=1, source_target_pairs={{16,32},{48,64},{80,96},{32,16},{64,48},{96,80},{17,33},{49,65},{8... | collective-permute-start | bytes 294920 | tf_op jit(solution)/shard_map/ppermute | solution.py:663
  19.8 0.1 collective-permute-start
  19.9 3.0 %collective-permute-done.1.across_ref = f32[3,8,8,128]{3,2,1,0:T(8,128)S(1)} collective-permute-done((f32[3,8,8,128]{3,2,1,0:T(8,128)S(1)}, f32[3,8,8,128]{3,2,1,0:T(8,128)S(1)}, u32[]{:S(2)}, u32[]{:S(2)}) %collective-permute-start.1) | collective-permute-done | bytes 98336 | tf_op jit(solution)/shard_map/ppermute | solution.py:663
  22.9 0.0 collective-permute-done.inside_ref
  22.9 4.0 %all-to-all-done.got_ref = f32[128,1,512]{2,1,0:T(1,128)S(1)} async-done(((f32[128,1,512]{2,1,0:T(1,128)}), f32[128,1,512]{2,1,0:T(1,128)S(1)}, u32[]{:S(2)}, u32[]{:S(2)}) %all-to-all-start) | async-done | bytes 262176 | tf_op jit(solution)/shard_map/all_to_all | solution.py:658
  26.9 0.0 copy-start
  26.9 0.8 copy-done
  27.7 3.0 %cells.1 = (f32[128,1,512]{2,1,0:T(1,128)S(1)}, f32[8,8,24,128]{3,2,1,0:T(8,128)S(1)}, f32[8,24,128]{2,1,0:T(8,128)S(1)}, s32[16,128]{1,0:T(8,128)S(1)}, bf16[3,...) custom-call(s32[1]{0:T(128)} %bitcast.me_ref.refs_0_, ...), custom_call_target="tpu_custom_call" | custom-call | tf_op jit(solution)/shard_map/cells/pallas_call | solution.py:646
  30.7 16.3 %all_to_all.30.got_ref = f32[128,1,512]{2,1,0:T(1,128)S(1)} all-to-all(f32[128,1,512]{2,1,0:T(1,128)S(1)} %get-tuple-element.38), channel_id=1, replica_groups=mesh['gx'=8,'gy'=4,'af'=4] {'gx','gy','af'}, dimensions={0} | all-to-all | bytes 524288 | tf_op jit(solution)/shard_map/all_to_all | solution.py:658
  47.0 1.8 %first.1 = (f32[128,1,640]{2,1,0:T(1,128)S(1)}, f32[8,24,128]{2,1,0:T(8,128)S(1)}, f32[8,128]{1,0:T(8,128)S(1)}, f32[8,128]{1,0:T(8,128)S(1)}, f32[8,128]{1,0:T(...) custom-call(s32[1]{0:T(128)} %bitcast.me_ref.refs_0_, f32[128,1,512]{2,1,0:T(1,128)S(1)} %all_to_all.30.got_ref, ...), custom_call_target="tpu_custom_call" | custom-call | tf_op jit(solution)/shard_map/first/pallas_call | solution.py:646
  48.8 15.9 %all_to_all.31.got_ref = f32[128,1,640]{2,1,0:T(1,128)S(1)} all-to-all(f32[128,1,640]{2,1,0:T(1,128)S(1)} %get-tuple-element.46), channel_id=1, replica_groups=mesh['gx'=8,'gy'=4,'af'=4] {'gx','gy','af'}, dimensions={0} | all-to-all | bytes 655360 | tf_op jit(solution)/shard_map/all_to_all | solution.py:658
  64.8 2.5 %even.2 = (f32[128,1,384]{2,1,0:T(1,128)S(1)}, f32[8,24,128]{2,1,0:T(8,128)S(1)}, f32[8,24,128]{2,1,0:T(8,128)S(1)}, f32[8,128]{1,0:T(8,128)S(1)}) custom-call(s32[1]{0:T(128)} %bitcast.me_ref.refs_0_, f32[128,1,640]{2,1,0:T(1,128)S(1)} %all_to_all.31.got_ref, f32[8,8,24,128]{3,2,1,0:T(8,128)S(1)} %get-tuple-element.39.cells_ref.refs_2_, ...), custom_call_target="tpu_custom_call" | custom-call | tf_op jit(solution)/shard_map/even/pallas_call | solution.py:646
  67.2 14.6 %all_to_all.32.refs_1_ = f32[128,1,384]{2,1,0:T(1,128)S(1)} all-to-all(f32[128,1,384]{2,1,0:T(1,128)S(1)} %get-tuple-element.53), channel_id=1, replica_groups=mesh['gx'=8,'gy'=4,'af'=4] {'gx','gy','af'}, dimensions={0} | all-to-all | bytes 393216 | tf_op jit(solution)/shard_map/all_to_all | solution.py:658
  81.8 2.7 %odd.2 = (f32[128,1,640]{2,1,0:T(1,128)S(1)}, f32[8,24,128]{2,1,0:T(8,128)S(1)}, f32[8,128]{1,0:T(8,128)S(1)}) custom-call(s32[1]{0:T(128)} %bitcast.me_ref.refs_0_, f32[128,1,384]{2,1,0:T(1,128)S(1)} %all_to_all.32.refs_1_, f32[8,8,24,128]{3,2,1,0:T(8,128)S(1)} %get-tuple-element.39.cells_ref.refs_2_, f32[8,24,128]{2,1,0:T(8,128)S(1)} %get-tuple-element.54.refs_3_, ...), custom_call_target="tpu_custom_call" | custom-call | tf_op jit(solution)/shard_map/odd/pallas_call | solution.py:646
  84.5 15.9 %all_to_all.33.got_ref = f32[128,1,640]{2,1,0:T(1,128)S(1)} all-to-all(f32[128,1,640]{2,1,0:T(1,128)S(1)} %get-tuple-element.57), channel_id=1, replica_groups=mesh['gx'=8,'gy'=4,'af'=4] {'gx','gy','af'}, dimensions={0} | all-to-all | bytes 655360 | tf_op jit(solution)/shard_map/all_to_all | solution.py:658
  100.5 2.5 %even.3 = (f32[128,1,384]{2,1,0:T(1,128)S(1)}, f32[8,24,128]{2,1,0:T(8,128)S(1)}, f32[8,24,128]{2,1,0:T(8,128)S(1)}, f32[8,128]{1,0:T(8,128)S(1)}) custom-call(s32[1]{0:T(128)} %bitcast.me_ref.refs_0_, f32[128,1,640]{2,1,0:T(1,128)S(1)} %all_to_all.33.got_ref, f32[8,8,24,128]{3,2,1,0:T(8,128)S(1)} %get-tuple-element.39.cells_ref.refs_2_, ...), custom_call_target="tpu_custom_call" | custom-call | tf_op jit(solution)/shard_map/even/pallas_call | solution.py:646
  102.9 14.6 %all_to_all.34.refs_1_ = f32[128,1,384]{2,1,0:T(1,128)S(1)} all-to-all(f32[128,1,384]{2,1,0:T(1,128)S(1)} %get-tuple-element.60), channel_id=1, replica_groups=mesh['gx'=8,'gy'=4,'af'=4] {'gx','gy','af'}, dimensions={0} | all-to-all | bytes 393216 | tf_op jit(solution)/shard_map/all_to_all | solution.py:658
  117.5 1.5 %odd.3 = (f32[8,8,128]{2,1,0:T(8,128)}, f32[4,256]{1,0:T(4,128)}) custom-call(s32[1]{0:T(128)} %bitcast.me_ref.refs_0_, f32[128,1,384]{2,1,0:T(1,128)S(1)} %all_to_all.34.refs_1_, f32[8,8,24,128]{3,2,1,0:T(8,128)S(1)} %get-tuple-element.39.cells_ref.refs_2_, f32[8,24,128]{2,1,0:T(8,128)S(1)} %get-tuple-element.61.refs_3_, ...), custom_call_target="tpu_custom_call" | custom-call | tf_op jit(solution)/shard_map/odd/pallas_call | solution.py:646
Async XLA Ops:
  3.9 23.0 %all-to-all-start = ((f32[128,1,512]{2,1,0:T(1,128)}), f32[128,1,512]{2,1,0:T(1,128)S(1)}, u32[]{:S(2)}, u32[]{:S(2)}) async-start(f32[128,1,512]{2,1,0:T(1,128)} %get-tuple-element.35), calls=%async_computation | async-start | bytes 524288 | tf_op jit(solution)/shard_map/all_to_all | solution.py:658
  16.2 6.7 %collective-permute-start.1 = (f32[3,8,8,128]{3,2,1,0:T(8,128)S(1)}, f32[3,8,8,128]{3,2,1,0:T(8,128)S(1)}, u32[]{:S(2)}, u32[]{:S(2)}) collective-permute-start(f32[3,8,8,128]{3,2,1,0:T(8,128)S(1)} %pad_maximum_fusion.middle_ref), channel_id=1, source_target_pairs={{16,32},{48,64},{80,96},{32,16},{64,48},{96,80},{17,33},{49,65},{8... | collective-permute-start | bytes 294920 | tf_op jit(solution)/shard_map/ppermute | solution.py:663
  19.8 3.1 %collective-permute-start = (f32[3,8,8,128]{3,2,1,0:T(8,128)S(1)}, f32[3,8,8,128]{3,2,1,0:T(8,128)S(1)}, u32[]{:S(2)}, u32[]{:S(2)}) collective-permute-start(f32[3,8,8,128]{3,2,1,0:T(8,128)S(1)} %pad_maximum_fusion.middle_ref), channel_id=1, source_target_pairs={{0,16},{32,48},{64,80},{96,112},{16,0},{48,32},{80,64},{112,96},{1... | collective-permute-start | bytes 294920 | tf_op jit(solution)/shard_map/ppermute | solution.py:663
  26.9 0.8 copy-start

commit v4 on v3

--- a/solution.py
+++ b/solution.py
@@ -1,3 +1,5 @@
+import functools
+
 import jax
 import jax.numpy as jnp
 from jax import lax
@@ -49,8 +51,10 @@
     return jnp.concatenate([row[:, i : i + 128] for i in range(0, row.shape[1], 128)], axis=0)
 
 
-def total(value):
-    return jnp.sum(jnp.sum(value, axis=1, keepdims=True), axis=0, keepdims=True)
+def totals(values):
+    rows = jnp.concatenate([jnp.sum(value, axis=0, keepdims=True) for value in values], axis=0)
+    sums = jnp.sum(rows, axis=1, keepdims=True)
+    return [sums[i : i + 1] for i in range(len(values))]
 
 
 def fold(value):
@@ -105,25 +109,56 @@
     return look_up(table, index >> 7, index & 127)
 
 
-def cell_hot(index_row):
+def swap_x(block):
+    return jnp.swapaxes(block, 0, 1)
+
+
+def cell_hot(index_row, low=0, high=ROWS):
     count = index_row.shape[1]
     columns = iota((128, count), 0) == (index_row & 127)
-    rows = iota((ROWS, count), 0) == (index_row >> 7)
+    rows = iota((high - low, count), 0) == (index_row >> 7) - low
     return columns.astype(bf16), rows.astype(bf16)
 
 
 def scatter(tables, columns, rows):
+    height = rows.shape[0]
     stacked = []
     for table in tables:
         for part in parts(table):
             row = as_row(part.astype(f32))
             tall = jnp.broadcast_to(row, (16, row.shape[1])).astype(bf16)
-            stacked.append(rows * jnp.concatenate([tall] * (ROWS // 16), axis=0))
+            stacked.append(rows * jnp.concatenate([tall] * (height // 16), axis=0))
     sums = dot_nt(jnp.concatenate(stacked, axis=0), columns)
     return [
-        (sums[2 * i * ROWS : (2 * i + 1) * ROWS] + sums[(2 * i + 1) * ROWS : (2 * i + 2) * ROWS]).reshape(LAYERS, 8, 128)
+        (sums[2 * i * height : (2 * i + 1) * height] + sums[(2 * i + 1) * height : (2 * i + 2) * height]).reshape(-1, 8, 128)
         for i in range(len(tables))
     ]
+
+
+def side_rows(side, count):
+    height = (count + 1) // 2 * 16
+    return ((0, ROWS), (ROWS - height, ROWS), (0, height))[0 if side == 1 else 1 + side // 2]
+
+
+def gather_wide(sums, count):
+    left, middle, right = sums
+    if count == 0:
+        return middle
+    return jnp.concatenate([left[left.shape[0] - count :], middle, right[:count]], axis=0)
+
+
+def scatter_wide(tables, late, columns_ref, rows_ref, count):
+    found = []
+    for side in range(3):
+        if side != 1 and count == 0:
+            found.append([None] * len(tables))
+            continue
+        low, high = side_rows(side, count)
+        sums = scatter([table[side] for table in tables], columns_ref[side], rows_ref[side, low:high])
+        index = as_row(late[side][:4].astype(i32) - 1)
+        sums[-1] = sums[-1] + scatter([late[side][4:]], *cell_hot(index, low, high))[0]
+        found.append(sums)
+    return [gather_wide([found[side][i] for side in range(3)], count) for i in range(len(tables))]
 
 
 def faces_of(field):
@@ -144,22 +179,6 @@
     return dot_tn(held, place)
 
 
-def up_x(v):
-    return jnp.concatenate([v[:, 1:], jnp.zeros_like(v[:, :1])], axis=1)
-
-
-def down_x(v):
-    return jnp.concatenate([jnp.zeros_like(v[:, :1]), v[:, :-1]], axis=1)
-
-
-def up_z(v):
-    return jnp.concatenate([v[1:], jnp.zeros_like(v[:1])], axis=0)
-
-
-def down_z(v):
-    return jnp.concatenate([jnp.zeros_like(v[:1]), v[:-1]], axis=0)
-
-
 def up_y(v, halo):
     return jnp.where(iota(v.shape, 2) == 127, halo, pltpu.roll(v, 127, 2))
 
@@ -168,10 +187,11 @@
     return jnp.where(iota(v.shape, 2) == 0, first, pltpu.roll(v, 1, 2))
 
 
-def stencil(tx, ty, tz, ty_first, field, halo):
-    out = tx * up_x(field) + down_x(tx * field)
-    out = out + ty * up_y(field, halo) + down_y(ty * field, ty_first * halo)
-    return out + tz * up_z(field) + down_z(tz * field)
+def stencil(tx_up, tx_down, ty, tz, ty_first, field, halo):
+    middle = field[1:-1]
+    out = tx_up * field[2:] + tx_down * field[:-2]
+    out = out + ty * up_y(middle, halo) + down_y(ty * middle, ty_first * halo)
+    return out + tz * pltpu.roll(middle, 7, 1) + pltpu.roll(tz * middle, 1, 1)
 
 
 def harmonic(first, second):
@@ -254,28 +274,30 @@
     diag = fold(accum_ref[...]) + tnext + tprev + fm
     inverse = 1.0 / diag
     partial = diag * press - chain(tnext, press)
-    for b in range(4):
-        here, _ = edge_codes(delta_ref, to_ref, b)
+    heres = [edge_codes(delta_ref, to_ref, b)[0] for b in range(4)]
+    for b, picked in enumerate(totals([jnp.where(code == here, press, 0.0) for here in heres])):
         at = code == b * 256 + from_ref[b]
-        partial = partial - jnp.where(at, trans_ref[b] * total(jnp.where(code == here, press, 0.0)), 0.0)
-    where_cell = (fold(layer_ref[...]) * 1024 + fold(cell_ref[...]) + 1).astype(f32)
+        partial = partial - jnp.where(at, trans_ref[b] * picked, 0.0)
+    cell = fold(cell_ref[...])
+    where_cell = ((((cell >> 7) * 8 + fold(layer_ref[...])) << 7) + (cell & 127) + 1).astype(f32)
     position = (iota((8, 128), 0) * 128 + iota((8, 128), 1) + 1).astype(f32)
     slots = to_slots([where_cell, mf * press, fm * inverse * fm, fm * inverse * mf, position], hot, mask)
     inverse_index, slots = slots[64:80], slots[:64]
     place = (owner * CAP + rank).astype(f32)
-    edges = []
+    rows = []
     for b in range(4):
         _, there = edge_codes(delta_ref, to_ref, b)
         at = code == b * 256 + from_ref[b]
         gain = trans_ref[b] * inverse
-        edges.append(jnp.full((1, 128), there.astype(f32)))
+        rows.append(jnp.where(iota((1, 128), 1) == 0, there.astype(f32), 0.0))
         for value in (place, where_cell, gain * fm, gain * partial, gain * trans_ref[b], gain * mf, code.astype(f32), gain):
-            edges.append(jnp.broadcast_to(total(jnp.where(at, value, 0.0)), (1, 128)))
-        edges.append(jnp.zeros((3, 128), f32))
+            rows.append(jnp.sum(jnp.where(at, value, 0.0), axis=0, keepdims=True))
+        rows.append(jnp.zeros((3, 128), f32))
+    edges = [jnp.broadcast_to(jnp.sum(jnp.concatenate(rows, axis=0), axis=1, keepdims=True), (48, 128))]
     rows = [spread(slots, 16), slots, spread(slots, -16)] + edges
     rows += [spread(slots[:CAP], shift) for shift in BESIDE] + [jnp.zeros((48, 128), f32)]
     store_slots(out_ref, jnp.concatenate(rows, axis=0))
-    first_face, last_face = faces_of(jnp.concatenate([press_ref[...].reshape(ROWS, 128), cond_ref[...].reshape(ROWS, 128)], axis=0))
+    first_face, last_face = faces_of(jnp.concatenate([swap_x(ref[...]).reshape(ROWS, 128) for ref in (press_ref, cond_ref)], axis=0))
     for across in (-16, 0, 16):
         put_faces(me, out_ref, 384, first_face, last_face, across)
     for i, value in enumerate((tnext, inverse, partial, fm, mf, owner.astype(f32), rank.astype(f32), press)):
@@ -317,7 +339,7 @@
     slots = load_slots(got_ref, 384)
     even = ((me >> 4) & 1) == 0
     press, cond, accum = (
-        jnp.concatenate([jnp.where(even, b, a), middle_ref[i], jnp.where(even, a, b)], axis=1)
+        jnp.concatenate([swap_x(part) for part in (jnp.where(even, b, a), middle_ref[i], jnp.where(even, a, b))], axis=0)
         for i, a, b in ((i, inside_ref[i], across_ref[i]) for i in range(3))
     )
     sums = []
@@ -331,7 +353,7 @@
         columns_ref[side] = columns
         rows_ref[side] = rows
         sums.append(scatter([table[16:32], table[32:48], table[48:64]], columns, rows))
-    flow, weight, mirror = (jnp.concatenate([sums[side][i] for side in range(3)], axis=1) for i in range(3))
+    flow, weight, mirror = (jnp.concatenate([sums[side][i] for side in range(3)], axis=0) for i in range(3))
     beside = slots[240:336].astype(i32) - 1
     along = me & 15
     for i, (there, column) in enumerate(((along > 0, 127), (along < 15, 0))):
@@ -339,63 +361,92 @@
         beside_ref[48 * i : 48 * i + 48] = jnp.where(there & (part >= 0) & ((part & 127) == column), part >> 7, -1)
 
     halos = [columns_of(*read_faces(me, got_ref, 384, 2 * ROWS, across)) for across in (-16, 0, 16)]
-    press_halo = jnp.concatenate([halo[:ROWS].reshape(LAYERS, 8, 128) for halo in halos], axis=1)
-    cond_halo = jnp.concatenate([halo[ROWS:].reshape(LAYERS, 8, 128) for halo in halos], axis=1)
-    lane = iota((LAYERS, EXT, 128), 2)
-    tx = harmonic(cond, up_x(cond))
+    press_halo = jnp.concatenate([halo[:ROWS].reshape(8, 8, 128) for halo in halos], axis=0)
+    cond_halo = jnp.concatenate([halo[ROWS:].reshape(8, 8, 128) for halo in halos], axis=0)
+    wide = (EXT, 8, 128)
+    tx = harmonic(cond[:-1], cond[1:])
     ty = harmonic(cond, up_y(cond, cond_halo))
-    tz = 0.5 * harmonic(cond, up_z(cond))
-    ty_first = jnp.where(lane == 0, harmonic(cond, cond_halo), 0.0)
-    diag = accum + tx + down_x(tx) + ty + down_y(ty, ty_first) + tz + down_z(tz)
+    tz = 0.5 * harmonic(cond, jnp.where(iota(wide, 1) == 7, 0.0, pltpu.roll(cond, 7, 1)))
+    ty_first = jnp.where(iota(wide, 2) == 0, harmonic(cond, cond_halo), 0.0)
+    diag = accum + ty + down_y(ty, ty_first) + tz + pltpu.roll(tz, 1, 1)
+    diag = diag[1:-1] + tx[1:] + tx[:-1]
     inverse = jnp.where(diag > 0.0, 1.0 / jnp.where(diag > 0.0, diag, 1.0), 0.0)
-
     source = jnp.concatenate([seg_ref[11 + i] for i in range(3)], axis=0)
-    res = diag * press - stencil(tx, ty, tz, ty_first, press, press_halo) - flow - source[None]
+
+    res = diag * press[1:-1] - flow[1:-1] - source.reshape(EXT, 1, 128)[1:-1]
+    res = res - stencil(tx[1:], tx[:-1], ty[1:-1], tz[1:-1], ty_first[1:-1], press, press_halo[1:-1])
     field = inverse * res
-    for i, value in enumerate((tx, ty, tz, ty_first, inverse, res, weight * press, mirror)):
+    cells_ref[0, : EXT - 1] = tx
+    for i, value in ((1, ty), (2, tz), (3, ty_first), (6, weight * press), (7, mirror)):
         cells_ref[i] = value
+    cells_ref[4, 1 : EXT - 1] = inverse
+    cells_ref[5, 1 : EXT - 1] = res
     field_ref[...] = field
-    res_ref[...] = res[:, 8:16]
+    res_ref[...] = swap_x(res[7:15])
 
     code = seg_code().astype(f32)
     _, inverse_f, partial, fm, _, owner, _, press_f = (seg_ref[i] for i in range(8))
-    edge = jnp.where(me > 0, got_ref[jnp.maximum(me - 1, 0), :, 128:256], -1.0)
+    edge = jnp.where(me > 0, got_ref[before(me), :, 128:256], -1.0)
     lane = iota((1, 128), 1)
     cells, terms, picks, found = [], [], [], []
+    ends = [code == edge_in(edge, k, 0) for k in range(4)]
+    wanted = (press_f, owner, seg_ref[14], fm * inverse_f)
+    sums = totals([jnp.where(at, value, 0.0) for at in ends for value in wanted])
     for k in range(4):
-        there = edge_in(edge, k, 0)
-        picked = total(jnp.where(code == there, press_f, 0.0))
-        at = (lane == (edge_in(edge, k, 1).astype(i32) >> 4)) & (there >= 0.0)
+        picked = sums[4 * k]
+        at = (lane == (edge_in(edge, k, 1).astype(i32) >> 4)) & (edge_in(edge, k, 0) >= 0.0)
         cells.append(jnp.where(at, edge_in(edge, k, 2), 0.0))
         terms.append(jnp.where(at, -edge_in(edge, k, 3) * picked, 0.0))
         picks.append(jnp.broadcast_to(picked, (1, 128)))
-        found.append([total(jnp.where(code == there, value, 0.0)) for value in (owner, seg_ref[14], fm * inverse_f)])
-        edge = jnp.where(lane == 64 + 12 * k + 4, edge - edge_in(edge, k, 5) * picked, edge)
+        found.append(sums[4 * k + 1 : 4 * k + 4])
+    for k in range(4):
+        edge = jnp.where(lane == 64 + 12 * k + 4, edge - edge_in(edge, k, 5) * sums[4 * k], edge)
     edge_ref[...] = jnp.broadcast_to(edge, (8, 128))
     late = jnp.concatenate(cells + terms, axis=0)
     position = jnp.concatenate([seg_ref[8], seg_ref[9]], axis=0).astype(i32)
     first = find(fm * inverse_f * partial, position)
 
-    taken = [find(middle_ref[0].reshape(ROWS, 128), own), find(field[:, 8:16].reshape(ROWS, 128), own)]
+    taken = [find(press[8:16].reshape(ROWS, 128), own), find(own_tile(field, 1), own)]
     rows = taken + [spread(taken[0], 1)]
     rows += [spread(first, 16), first, spread(first, -16), spread(late, 16), late, spread(late, -16)]
     store_slots(out_ref, jnp.concatenate(rows + picks + [jnp.zeros((4, 128), f32)], axis=0))
-    begin, end = faces_of(field.reshape(LAYERS * EXT, 128))
-    begin_inverse, end_inverse = faces_of(inverse.reshape(LAYERS * EXT, 128))
-    for k, (tile, cell, weight_there) in enumerate(found):
-        begin = put_entry(begin, k, tile)
-        begin = put_entry(begin, 4 + k, cell)
-        begin_inverse = put_entry(begin_inverse, k, weight_there)
-    put_faces(me, out_ref, 128, begin, end)
-    put_faces(me, out_ref, 320, begin_inverse, end_inverse)
-
-
-def put_entry(face, k, value):
-    return jnp.where(iota(face.shape, 1) == EXT * k, value, face)
-
-
-def get_entry(face, k):
-    return face[:, EXT * k : EXT * k + 1]
+    put_faces(me, out_ref, FIRST, *faces_of(field[1:-1].reshape(-1, 128)))
+    put_faces(me, out_ref, FIRST_INVERSE, *faces_of(inverse[3:19].reshape(-1, 128)))
+    put_entries(out_ref, before(me), FIRST_ENDS, [end for ends in found for end in ends])
+
+
+def put_entries(out_ref, at, start, entries):
+    lane = iota((1, len(entries)), 1)
+    row = jnp.zeros(lane.shape, f32)
+    for i, entry in enumerate(entries):
+        row = jnp.where(lane == i, entry, row)
+    out_ref[at, :, start : start + len(entries)] = row
+
+
+def get_entries(got_ref, at, start, count):
+    row = got_ref[at, :, start : start + count]
+    return [row[:, i : i + 1] for i in range(count)]
+
+
+def before(me):
+    return jnp.maximum(me - 1, 0)
+
+
+def after(me):
+    return jnp.minimum(me + 1, TILES - 1)
+
+
+FIRST = 128
+FIRST_ENDS = FIRST + 160
+FIRST_INVERSE = FIRST_ENDS + 16
+WIDE = 232
+SLIM = 128
+SLIM_TWO = 248
+
+
+def wide_lanes(k):
+    entries = WIDE + 8 * (22 - 2 * k)
+    return entries, entries + 4
 
 
 def own_edges(seg_ref):
@@ -405,7 +456,8 @@
 
 def edge_terms(code, edges, frac):
     starts, _, _, factors = edges
-    return [factor * total(jnp.where(code == start, frac, 0.0)) for start, factor in zip(starts, factors)]
+    sums = totals([jnp.where(code == start, frac, 0.0) for start in starts])
+    return [factor * picked for factor, picked in zip(factors, sums)]
 
 
 def arrive(code, targets, terms):
@@ -429,26 +481,24 @@
     return [spread(rows, 16), rows, spread(rows, -16)]
 
 
-def scatter_late(late):
-    return scatter([late[4:]], *cell_hot(as_row(late[:4].astype(i32) - 1)))[0]
-
-
-def own_tile(field):
-    return field[:, 8:16].reshape(ROWS, 128)
-
-
-def start_of(edge, k, table):
+def own_tile(field, k):
+    return field[8 - k : 16 - k].reshape(ROWS, 128)
+
+
+def starts_of(edge, table):
     place = (iota((CAP, 128), 1) * CAP + iota((CAP, 128), 0)).astype(f32)
-    return total(jnp.where(place == edge_in(edge, k, 1), table, 0.0))
-
-
-def advance(cells_ref, field, halo, flow):
-    tx, ty, tz, ty_first, inverse, res = (cells_ref[i] for i in range(6))
-    return inverse * (res + stencil(tx, ty, tz, ty_first, field, halo) + flow)
-
-
-def wide_halo(me, got_ref, start):
-    return columns_of(*read_faces(me, got_ref, start, LAYERS * EXT)).reshape(LAYERS, EXT, 128)
+    return totals([jnp.where(place == edge_in(edge, k, 1), table, 0.0) for k in range(4)])
+
+
+def advance(cells_ref, k, field, halo, flow):
+    low, high = k + 1, EXT - 1 - k
+    ty, tz, ty_first, inverse, res = (cells_ref[i, low:high] for i in range(1, 6))
+    tx_up, tx_down = cells_ref[0, low:high], cells_ref[0, low - 1 : high - 1]
+    return inverse * (res + stencil(tx_up, tx_down, ty, tz, ty_first, field, halo) + flow)
+
+
+def wide_halo(me, got_ref, start, count):
+    return columns_of(*read_faces(me, got_ref, start, 8 * count)).reshape(count, 8, 128)
 
 
 def ends_of(ends_ref):
@@ -456,21 +506,20 @@
     return [[held[:, 3 * k + i : 3 * k + i + 1] for i in range(3)] for k in range(4)]
 
 
-def send_wide(me, out_ref, code, edges, ends, seg_ref, cells_ref, index_ref, field, frac, resf):
+def send_wide(me, out_ref, k, code, edges, ends, seg_ref, cells_ref, index_ref, field, frac, resf):
     tnext, inverse_f, fm = seg_ref[0], seg_ref[1], seg_ref[3]
     terms = edge_terms(code, edges, frac)
     ahead = inverse_f * (resf + chain(tnext, frac) + arrive(code, edges[1], terms))
-    part = advance(cells_ref, field, jnp.zeros((LAYERS, EXT, 128), f32), 0.0)
+    part = advance(cells_ref, k, field, jnp.zeros((22 - 2 * k, 8, 128), f32), 0.0)
     position = jnp.concatenate([seg_ref[8], seg_ref[9]], axis=0).astype(i32)
     now = find(fm * frac, position)
-    rows = [find(own_tile(field), index_ref[...])] + to_three(now) + to_three(find(fm * ahead, position))
+    rows = [find(own_tile(field, k), index_ref[...])] + to_three(now) + to_three(find(fm * ahead, position))
     rows += to_three(late_rows(edges, ends, terms)) + [spread(now, shift) for shift in BESIDE]
     store_slots(out_ref, jnp.concatenate(rows + [jnp.zeros((24, 128), f32)], axis=0))
-    begin, end = faces_of(field.reshape(LAYERS * EXT, 128))
-    for b in range(4):
-        end = put_entry(end, b, terms[b])
-    put_faces(me, out_ref, 256, begin, end)
-    put_faces(me, out_ref, 448, *faces_of(part.reshape(LAYERS * EXT, 128)))
+    entries, further = wide_lanes(k)
+    put_faces(me, out_ref, WIDE, *faces_of(field[1:-1].reshape(-1, 128)))
+    put_faces(me, out_ref, further, *faces_of(part[1:-1].reshape(-1, 128)))
+    put_entries(out_ref, jnp.where(me + 1 < TILES, me + 1, me), entries, terms)
 
 
 def first_kernel(
@@ -488,29 +537,28 @@
     starts, targets, nexts, factors = edges
 
     resf = partial - fm * look_up(slots[0:16], rank, owner)
-    after = got_ref[jnp.minimum(me + 1, TILES - 1), :, :]
+    picks = get_entries(got_ref, after(me), 120, 4)
     for b in range(4):
         at = (code == starts[b]) & (nexts[b] >= 0.0)
-        resf = resf - jnp.where(at, factors[b] * after[:, 120 + b : 121 + b], 0.0)
+        resf = resf - jnp.where(at, factors[b] * picks[b], 0.0)
     frac = inverse_f * resf
     terms = edge_terms(code, edges, frac)
-    before = [edge_in(edge, k, 4) - edge_in(edge, k, 3) * start_of(edge, k, slots[32:48]) for k in range(4)]
+    begun = starts_of(edge, slots[32:48])
+    coming = [edge_in(edge, k, 4) - edge_in(edge, k, 3) * begun[k] for k in range(4)]
     gain = resf + chain(tnext, frac) + mf * look_up(slots[16:32], rank, owner)
-    gain = gain + arrive(code, targets, terms) + arrive(code, [edge_in(edge, k, 0) for k in range(4)], before)
+    gain = gain + arrive(code, targets, terms) + arrive(code, [edge_in(edge, k, 0) for k in range(4)], coming)
     frac = inverse_f * gain
-    flow = []
-    for side in range(3):
-        sums = scatter([slots[48 + side * CAP : 64 + side * CAP]], columns_ref[side], rows_ref[side])
-        flow.append(sums[0] + scatter_late(slots[96 + 8 * side : 104 + 8 * side]))
-    flow = jnp.concatenate(flow, axis=1) - cells_ref[6]
-    field = advance(cells_ref, field_ref[...], wide_halo(me, got_ref, 128), flow)
+    late = [slots[96 + 8 * side : 104 + 8 * side] for side in range(3)]
+    first = [slots[48 + side * CAP : 64 + side * CAP] for side in range(3)]
+    (flow,) = scatter_wide([first], late, columns_ref, rows_ref, 6)
+    field = advance(cells_ref, 1, field_ref[...], wide_halo(me, got_ref, FIRST, 20), flow - cells_ref[6, 2:22])
     new_field_ref[...] = field
     new_frac_ref[...] = frac
     resf_ref[...] = resf
     res_fracture_ref[...] = unfold(resf)
-    halo_inverse_ref[...] = wide_halo(me, got_ref, 320)
-    face, weights = after[:, 128:320], after[:, 320:512]
-    ends = [(get_entry(face, k), get_entry(face, 4 + k), get_entry(weights, k)) for k in range(4)]
+    halo_inverse_ref[...] = wide_halo(me, got_ref, FIRST_INVERSE, 16)
+    ends = get_entries(got_ref, after(me), FIRST_ENDS, 12)
+    ends = [ends[3 * k : 3 * k + 3] for k in range(4)]
     lane = iota((8, 128), 1)
     held = jnp.zeros((8, 128), f32)
     for k in range(4):
@@ -518,11 +566,11 @@
             held = jnp.where(lane == 3 * k + i, ends[k][i], held)
     ends_ref[...] = held
 
-    send_wide(me, out_ref, code, edges, ends, seg_ref, cells_ref, index_ref, field, frac, resf)
+    send_wide(me, out_ref, 2, code, edges, ends, seg_ref, cells_ref, index_ref, field, frac, resf)
 
 
 def even_kernel(
-    me_ref, got_ref, cells_ref, field_ref, index_ref, columns_ref, rows_ref, seg_ref, edge_ref,
+    k, me_ref, got_ref, cells_ref, field_ref, index_ref, columns_ref, rows_ref, seg_ref, edge_ref,
     frac_ref, resf_ref, ends_ref, halo_inverse_ref, beside_ref,
     out_ref, third_ref, new_field_ref, new_frac_ref,
 ):
@@ -535,23 +583,23 @@
     targets = edges[1]
     resf = resf_ref[...]
     frac = frac_ref[...]
-    before = got_ref[jnp.maximum(me - 1, 0), :, 256:448]
+    entries, further = wide_lanes(k)
+    coming = get_entries(got_ref, before(me), entries, 4)
     gain = resf + chain(tnext, frac) + mf * look_up(slots[0:16], rank.astype(i32), owner.astype(i32))
     gain = gain + arrive(code, targets, edge_terms(code, edges, frac))
-    gain = gain + arrive(code, [edge_in(edge, k, 0) for k in range(4)], [get_entry(before, k) for k in range(4)])
+    gain = gain + arrive(code, [edge_in(edge, b, 0) for b in range(4)], coming)
     frac = inverse_f * gain
     terms = edge_terms(code, edges, frac)
     ahead = inverse_f * (resf + chain(tnext, frac) + arrive(code, targets, terms))
     new_frac_ref[...] = frac
 
-    flow, later, beside = [], [], []
+    tables = [[slots[first + side * CAP : first + CAP + side * CAP] for side in range(3)] for first in (16, 64)]
+    late = [slots[112 + 8 * side : 120 + 8 * side] for side in range(3)]
+    flow, later = scatter_wide(tables, late, columns_ref, rows_ref, 7 - k)
+    beside = []
     lane = iota((ROWS, 128), 1)
     level = iota((ROWS, 128), 0)
     for side in range(3):
-        start = 16 + side * CAP
-        sums = scatter([slots[start : start + CAP], slots[start + 48 : start + 48 + CAP]], columns_ref[side], rows_ref[side])
-        flow.append(sums[0])
-        later.append(sums[1] + scatter_late(slots[112 + 8 * side : 120 + 8 * side]))
         column = jnp.zeros((ROWS, 128), f32)
         for i, at in enumerate((0, 127)):
             first = 48 * i + CAP * side
@@ -559,36 +607,32 @@
             for r in range(first, first + CAP):
                 held = held + jnp.where(level == beside_ref[r : r + 1], slots[136 + r : 137 + r], 0.0)
             column = jnp.where(lane == at, jnp.sum(held, axis=1, keepdims=True), column)
-        beside.append(column.reshape(LAYERS, 8, 128))
-    flow, later, beside = (jnp.concatenate(parts_x, axis=1) for parts_x in (flow, later, beside))
+        beside.append(column.reshape(8, 8, 128))
+    beside = jnp.concatenate(beside, axis=0)[k + 2 : 22 - k]
     second = field_ref[...]
-    third = advance(cells_ref, second, wide_halo(me, got_ref, 256), flow)
-    lane = iota((LAYERS, EXT, 128), 2)
-    joint = jnp.where(lane == 0, cells_ref[3], jnp.where(lane == 127, cells_ref[1], 0.0))
-    halo = wide_halo(me, got_ref, 448) + halo_inverse_ref[...] * (joint * second + beside)
-    field = advance(cells_ref, third, halo, later + cells_ref[7] * second)
+    third = advance(cells_ref, k, second, wide_halo(me, got_ref, WIDE, 22 - 2 * k), flow)
+    inner = second[2:-2]
+    lane = iota(inner.shape, 2)
+    joint = jnp.where(lane == 0, cells_ref[3, k + 2 : 22 - k], jnp.where(lane == 127, cells_ref[1, k + 2 : 22 - k], 0.0))
+    halo = wide_halo(me, got_ref, further, 20 - 2 * k) + halo_inverse_ref[k - 2 : 18 - k] * (joint * inner + beside)
+    field = advance(cells_ref, k + 1, third, halo, later[1:-1] + cells_ref[7, k + 2 : 22 - k] * inner)
     third_ref[...] = third
     new_field_ref[...] = field
 
     position = jnp.concatenate([seg_ref[8], seg_ref[9]], axis=0).astype(i32)
     ends = ends_of(ends_ref)
-    own_third = find(own_tile(third), index_ref[...])
-    rows = [own_third, find(own_tile(field), index_ref[...]), spread(own_third, 1)] + to_three(find(fm * ahead, position))
+    own_third = find(own_tile(third, k + 1), index_ref[...])
+    rows = [own_third, find(own_tile(field, k + 2), index_ref[...]), spread(own_third, 1)] + to_three(find(fm * ahead, position))
     rows += to_three(late_rows(edges, ends, terms))
     store_slots(out_ref, jnp.concatenate(rows + [jnp.zeros((8, 128), f32)], axis=0))
-    begin, end = faces_of(field.reshape(LAYERS * EXT, 128))
-    for b, term in enumerate(terms + edge_terms(code, edges, ahead)):
-        end = put_entry(end, b, term)
-    put_faces(me, out_ref, 128, begin, end)
-    lane = iota((1, 64), 1)
-    two = jnp.zeros((1, 64), f32)
-    for b in range(4):
-        two = jnp.where(lane == b, terms[b], jnp.where(lane == 4 + b, edges[2][b], two))
-    out_ref[jnp.where(me + 2 < TILES, me + 2, me), :, 320:384] = two
+    put_faces(me, out_ref, SLIM, *faces_of(field[1:-1].reshape(-1, 128)))
+    to_next = jnp.where(me + 1 < TILES, me + 1, me)
+    put_entries(out_ref, to_next, SLIM + 8 * (18 - 2 * k), terms + edge_terms(code, edges, ahead))
+    put_entries(out_ref, jnp.where(me + 2 < TILES, me + 2, me), SLIM_TWO, terms + edges[2])
 
 
 def odd_kernel(
-    final, me_ref, got_ref, cells_ref, field_ref, index_ref, columns_ref, rows_ref, seg_ref, edge_ref,
+    k, final, me_ref, got_ref, cells_ref, field_ref, index_ref, columns_ref, rows_ref, seg_ref, edge_ref,
     frac_ref, resf_ref, ends_ref, third_ref, *outs,
 ):
     me = me_ref[0]
@@ -602,42 +646,38 @@
     targets = edges[1]
     resf = resf_ref[...]
     frac = frac_ref[...]
-    before = got_ref[jnp.maximum(me - 1, 0), :, 128:320]
-    two = jnp.where(me > 1, got_ref[jnp.maximum(me - 2, 0), :, 320:384], -1.0)
-    heres = [edge_in(edge, k, 0) for k in range(4)]
+    coming = get_entries(got_ref, before(me), SLIM + 8 * (22 - 2 * k), 8)
+    two = jnp.where(me > 1, got_ref[jnp.maximum(me - 2, 0), :, 128:256], -1.0)
+    lane = iota((1, 128), 1)
+    codes = jnp.where((lane >= SLIM_TWO - 128) & (lane < SLIM_TWO - 124), pltpu.roll(two, 124, 1), -2.0)
+    meets = jnp.concatenate([jnp.where(codes == edge_in(edge, b, 7), two, 0.0) for b in range(4)], axis=0)
+    meets = jnp.sum(meets, axis=1, keepdims=True)
+    begun = starts_of(edge, slots[32:48])
+    heres = [edge_in(edge, b, 0) for b in range(4)]
     gain = resf + chain(tnext, frac) + mf * look_up(slots[0:16], rank, owner)
     gain = gain + arrive(code, targets, edge_terms(code, edges, frac))
-    frac = inverse_f * (gain + arrive(code, heres, [get_entry(before, k) for k in range(4)]))
-    terms = []
-    for k in range(4):
-        term = get_entry(before, 4 + k) + edge_in(edge, k, 6) * start_of(edge, k, slots[32:48])
-        for j in range(4):
-            meets = two[:, 4 + j : 5 + j] == edge_in(edge, k, 7)
-            term = term + jnp.where(meets, edge_in(edge, k, 8) * two[:, j : j + 1], 0.0)
-        terms.append(term)
+    frac = inverse_f * (gain + arrive(code, heres, coming[:4]))
+    terms = [
+        coming[4 + b] + edge_in(edge, b, 6) * begun[b] + edge_in(edge, b, 8) * meets[b : b + 1] for b in range(4)
+    ]
     gain = resf + chain(tnext, frac) + mf * look_up(slots[16:32], rank, owner)
     gain = gain + arrive(code, targets, edge_terms(code, edges, frac))
     frac = inverse_f * (gain + arrive(code, heres, terms))
 
-    flow = []
-    for side in range(3):
-        if final and side != 1:
-            flow.append(jnp.zeros((LAYERS, 8, 128), f32))
-            continue
-        start = 48 + side * CAP
-        sums = scatter([slots[start : start + CAP]], columns_ref[side], rows_ref[side])
-        flow.append(sums[0] + scatter_late(slots[96 + 8 * side : 104 + 8 * side]))
-    flow = jnp.concatenate(flow, axis=1) + cells_ref[7] * third_ref[...]
-    field = advance(cells_ref, field_ref[...], wide_halo(me, got_ref, 128), flow)
+    late = [slots[96 + 8 * side : 104 + 8 * side] for side in range(3)]
+    tables = [[slots[48 + side * CAP : 64 + side * CAP] for side in range(3)]]
+    (flow,) = scatter_wide(tables, late, columns_ref, rows_ref, 7 - k)
+    flow = flow + cells_ref[7, k + 1 : 23 - k] * third_ref[2:-2]
+    field = advance(cells_ref, k, field_ref[...], wide_halo(me, got_ref, SLIM, 22 - 2 * k), flow)
     if final:
         adj_matrix_ref, adj_fracture_ref = outs
-        adj_matrix_ref[...] = field[:, 8:16]
+        adj_matrix_ref[...] = swap_x(field)
         adj_fracture_ref[...] = unfold(frac)
         return
     out_ref, new_field_ref, new_frac_ref = outs
     new_field_ref[...] = field
     new_frac_ref[...] = frac
-    send_wide(me, out_ref, code, edges, ends_of(ends_ref), seg_ref, cells_ref, index_ref, field, frac, resf)
+    send_wide(me, out_ref, k + 1, code, edges, ends_of(ends_ref), seg_ref, cells_ref, index_ref, field, frac, resf)
 
 
 def call(kernel, name, scalars, arrays, outs, space=pltpu.VMEM, scratch=(), limit=20 * 1024 * 1024):
@@ -671,7 +711,7 @@
     stacked = jnp.stack([press_matrix, cond_matrix, accum_matrix])
     inside = swapped(stacked, 0)
     across = swapped(stacked, 1)
-    wide = (LAYERS, EXT, 128)
+    wide = (EXT, 8, 128)
     tile = (LAYERS, 8, 128)
     seg = (8, 128)
 
@@ -692,35 +732,42 @@
         "cells",
         (me,),
         (got, stacked, inside, across, segs),
-        [((TILES, 1, 512), f32), ((8, *wide), f32), (wide, f32), ((CAP, 128), i32), ((3, 128, SLOTS), bf16),
+        [((TILES, 1, 512), f32), ((8, *wide), f32), ((22, 8, 128), f32), ((CAP, 128), i32), ((3, 128, SLOTS), bf16),
          ((3, ROWS, SLOTS), bf16), (seg, f32), ((96, 128), i32), (tile, f32)],
     )
     kept = (index, columns, rows, segs, edge)
-    going = [(wide, f32), (seg, f32)]
+
+    def after_sweeps(k):
+        return ((EXT - 2 * k, 8, 128), f32)
+
+    wide_message = ((TILES, 1, 512), f32)
+    slim_message = ((TILES, 1, 256), f32)
     got = exchange(message)
     message, field, frac, resf, ends, halo_inverse, res_fracture = call(
         first_kernel,
         "first",
         (me,),
         (got, cells, field, *kept),
-        [((TILES, 1, 640), f32), *going, (seg, f32), (seg, f32), (wide, f32), ((4, 256), f32)],
+        [wide_message, after_sweeps(2), (seg, f32), (seg, f32), (seg, f32), ((16, 8, 128), f32), ((4, 256), f32)],
     )
-    for final in (False, True):
+    for k, final in ((2, False), (5, True)):
         got = exchange(message)
         message, third, field, frac = call(
-            even_kernel,
+            functools.partial(even_kernel, k),
             "even",
             (me,),
             (got, cells, field, *kept, frac, resf, ends, halo_inverse, beside),
-            [((TILES, 1, 384), f32), (wide, f32), *going],
+            [slim_message, after_sweeps(k + 1), after_sweeps(k + 2), (seg, f32)],
         )
         got = exchange(message)
-
-        def kernel(*refs, final=final):
-            odd_kernel(final, *refs)
-
-        outs = [(tile, f32), ((4, 256), f32)] if final else [((TILES, 1, 640), f32), *going]
-        results = call(kernel, "odd", (me,), (got, cells, field, *kept, frac, resf, ends, third), outs)
+        outs = [(tile, f32), ((4, 256), f32)] if final else [wide_message, after_sweeps(k + 3), (seg, f32)]
+        results = call(
+            functools.partial(odd_kernel, k + 2, final),
+            "odd",
+            (me,),
+            (got, cells, field, *kept, frac, resf, ends, third),
+            outs,
+        )
         if not final:
             message, field, frac = results
     adj_matrix, adj_fracture = results

time: 119 us -> 115 us (0.966)
  Pallas kernels: 17.2 us -> 14.5 us
  blocking collectives: 77.3 us -> 75.2 us
    pallas_call x7, Pallas kernels: 17.2 us -> 14.5 us  [call(): pl.pallas_call(kernel, name=name, out_shape=[jax.ShapeDtypeStruct(shape,...]
    all_to_all x5, blocking collectives: 77.3 us -> 75.2 us  [exchange(): return lax.all_to_all(message, ALL, split_axis=0, concat_axis=0, tiled=True)]
where the time goes in v4:
time: 115 us; the launch traced here: 114 us
  blocking collectives  75.2 us (65%)
  starting transfers between devices  15.1 us (13%)
  Pallas kernels  14.5 us (13%)
  waiting for transfers between devices  7.03 us (6%)
    all_to_all x5, blocking collectives, exchange(): return lax.all_to_all(message, ALL, split_axis=0, concat_axis=0, tiled=True)  75.2 us
    pallas_call x7, Pallas kernels, call(): pl.pallas_call(kernel, name=name, out_shape=[jax.ShapeDtypeStruct(shape,...  14.5 us
    all_to_all x1, starting transfers between devices, exchange(): return lax.all_to_all(message, ALL, split_axis=0, concat_axis=0, tiled=True)  11.5 us
    all_to_all x1, waiting for transfers between devices, exchange(): return lax.all_to_all(message, ALL, split_axis=0, concat_axis=0, tiled=True)  3.99 us
    ppermute x2, starting transfers between devices, swapped(): return lax.ppermute(block, 'gx', pairs + [(j, i) for i, j in pairs])  3.62 us
    ppermute x2, waiting for transfers between devices, swapped(): return lax.ppermute(block, 'gx', pairs + [(j, i) for i, j in pairs])  3.04 us
  transfers between devices with their start and end apart: 3, of which 2 were waited for; matrix products, arithmetic and copies ran while one was open for 1% of the time, Pallas kernels for 0%

profile of v4, /device:TPU:1, one launch (start us, length us, event | category | flops | bytes accessed | tf_op | source)
XLA Modules:
  0.0 114.2 jit_solution(3253128399344982335)
XLA Ops:
  0.6 3.3 %begin.1 = (f32[128,1,512]{2,1,0:T(1,128)}, f32[15,8,128]{2,1,0:T(8,128)}) custom-call(s32[1]{0:T(128)} %bitcast.me_ref, s32[4]{0:T(128)} %delta_ref.1, s32[4]{0:T(128)} %from_ref.1, s32[4]{0:T(128)} %to_ref.1, f32[4]{0:T(128)} %trans_ref.1, s32[32]{0:T(128)} %well_tile_ref.1, s32[32]{0:T(128)} %well_cell_ref.1, f32[32]{0:T(128)} %well_rate_ref.1, ...), custom_call_target="tpu_custom_call" | custom-call | tf_op jit(solution)/shard_map/begin/pallas_call | solution.py:686
  4.0 11.5 %all-to-all-start = ((f32[128,1,512]{2,1,0:T(1,128)}), f32[128,1,512]{2,1,0:T(1,128)S(1)}, u32[]{:S(2)}, u32[]{:S(2)}) async-start(f32[128,1,512]{2,1,0:T(1,128)} %get-tuple-element.35), calls=%async_computation | async-start | bytes 524288 | tf_op jit(solution)/shard_map/all_to_all | solution.py:698
  15.5 0.8 pad_maximum_fusion.middle_ref
  16.3 3.5 %collective-permute-start.1 = (f32[3,8,8,128]{3,2,1,0:T(8,128)S(1)}, f32[3,8,8,128]{3,2,1,0:T(8,128)S(1)}, u32[]{:S(2)}, u32[]{:S(2)}) collective-permute-start(f32[3,8,8,128]{3,2,1,0:T(8,128)S(1)} %pad_maximum_fusion.middle_ref), channel_id=1, source_target_pairs={{16,32},{48,64},{80,96},{32,16},{64,48},{96,80},{17,33},{49,65},{8... | collective-permute-start | bytes 294920 | tf_op jit(solution)/shard_map/ppermute | solution.py:703
  19.8 0.1 collective-permute-start
  19.9 3.0 %collective-permute-done.1.across_ref = f32[3,8,8,128]{3,2,1,0:T(8,128)S(1)} collective-permute-done((f32[3,8,8,128]{3,2,1,0:T(8,128)S(1)}, f32[3,8,8,128]{3,2,1,0:T(8,128)S(1)}, u32[]{:S(2)}, u32[]{:S(2)}) %collective-permute-start.1) | collective-permute-done | bytes 98336 | tf_op jit(solution)/shard_map/ppermute | solution.py:703
  22.9 0.0 collective-permute-done.inside_ref
  22.9 4.0 %all-to-all-done.got_ref = f32[128,1,512]{2,1,0:T(1,128)S(1)} async-done(((f32[128,1,512]{2,1,0:T(1,128)}), f32[128,1,512]{2,1,0:T(1,128)S(1)}, u32[]{:S(2)}, u32[]{:S(2)}) %all-to-all-start) | async-done | bytes 262176 | tf_op jit(solution)/shard_map/all_to_all | solution.py:698
  26.9 0.0 copy-start
  26.9 0.8 copy-done
  27.8 2.8 %cells.1 = (f32[128,1,512]{2,1,0:T(1,128)S(1)}, f32[8,24,8,128]{3,2,1,0:T(8,128)S(1)}, f32[22,8,128]{2,1,0:T(8,128)S(1)}, s32[16,128]{1,0:T(8,128)S(1)}, bf16[3,...) custom-call(s32[1]{0:T(128)} %bitcast.me_ref, ...), custom_call_target="tpu_custom_call" | custom-call | tf_op jit(solution)/shard_map/cells/pallas_call | solution.py:686
  30.6 16.3 %all_to_all.30.got_ref = f32[128,1,512]{2,1,0:T(1,128)S(1)} all-to-all(f32[128,1,512]{2,1,0:T(1,128)S(1)} %get-tuple-element.38), channel_id=1, replica_groups=mesh['gx'=8,'gy'=4,'af'=4] {'gx','gy','af'}, dimensions={0} | all-to-all | bytes 524288 | tf_op jit(solution)/shard_map/all_to_all | solution.py:698
  46.9 1.6 %first.1 = (f32[128,1,512]{2,1,0:T(1,128)S(1)}, f32[20,8,128]{2,1,0:T(8,128)S(1)}, f32[8,128]{1,0:T(8,128)S(1)}, f32[8,128]{1,0:T(8,128)S(1)}, f32[8,128]{1,0:T(...) custom-call(s32[1]{0:T(128)} %bitcast.me_ref, f32[128,1,512]{2,1,0:T(1,128)S(1)} %all_to_all.30.got_ref, ...), custom_call_target="tpu_custom_call" | custom-call | tf_op jit(solution)/shard_map/first/pallas_call | solution.py:686
  48.5 15.3 %all_to_all.31.got_ref = f32[128,1,512]{2,1,0:T(1,128)S(1)} all-to-all(f32[128,1,512]{2,1,0:T(1,128)S(1)} %get-tuple-element.46), channel_id=1, replica_groups=mesh['gx'=8,'gy'=4,'af'=4] {'gx','gy','af'}, dimensions={0} | all-to-all | bytes 524288 | tf_op jit(solution)/shard_map/all_to_all | solution.py:698
  63.7 2.2 %even.2 = (f32[128,1,256]{2,1,0:T(1,128)S(1)}, f32[18,8,128]{2,1,0:T(8,128)S(1)}, f32[16,8,128]{2,1,0:T(8,128)S(1)}, f32[8,128]{1,0:T(8,128)S(1)}) custom-call(s32[1]{0:T(128)} %bitcast.me_ref, f32[128,1,512]{2,1,0:T(1,128)S(1)} %all_to_all.31.got_ref, f32[8,24,8,128]{3,2,1,0:T(8,128)S(1)} %get-tuple-element.39.cells_ref, ...), custom_call_target="tpu_custom_call" | custom-call | tf_op jit(solution)/shard_map/even/pallas_call | solution.py:686
  66.0 14.2 %all_to_all.32.got_ref = f32[128,1,256]{2,1,0:T(1,128)S(1)} all-to-all(f32[128,1,256]{2,1,0:T(1,128)S(1)} %get-tuple-element.53), channel_id=1, replica_groups=mesh['gx'=8,'gy'=4,'af'=4] {'gx','gy','af'}, dimensions={0} | all-to-all | bytes 262144 | tf_op jit(solution)/shard_map/all_to_all | solution.py:698
  80.2 1.5 %odd.2 = (f32[128,1,512]{2,1,0:T(1,128)S(1)}, f32[14,8,128]{2,1,0:T(8,128)S(1)}, f32[8,128]{1,0:T(8,128)S(1)}) custom-call(s32[1]{0:T(128)} %bitcast.me_ref, f32[128,1,256]{2,1,0:T(1,128)S(1)} %all_to_all.32.got_ref, f32[8,24,8,128]{3,2,1,0:T(8,128)S(1)} %get-tuple-element.39.cells_ref, f32[16,8,128]{2,1,0:T(8,128)S(1)} %get-tuple-element.54.field_ref, ...), custom_call_target="tpu_custom_call" | custom-call | tf_op jit(solution)/shard_map/odd/pallas_call | solution.py:686
  81.7 15.2 %all_to_all.33.got_ref = f32[128,1,512]{2,1,0:T(1,128)S(1)} all-to-all(f32[128,1,512]{2,1,0:T(1,128)S(1)} %get-tuple-element.57), channel_id=1, replica_groups=mesh['gx'=8,'gy'=4,'af'=4] {'gx','gy','af'}, dimensions={0} | all-to-all | bytes 524288 | tf_op jit(solution)/shard_map/all_to_all | solution.py:698
  96.9 1.9 %even.3 = (f32[128,1,256]{2,1,0:T(1,128)S(1)}, f32[12,8,128]{2,1,0:T(8,128)S(1)}, f32[10,8,128]{2,1,0:T(8,128)S(1)}, f32[8,128]{1,0:T(8,128)S(1)}) custom-call(s32[1]{0:T(128)} %bitcast.me_ref, f32[128,1,512]{2,1,0:T(1,128)S(1)} %all_to_all.33.got_ref, f32[8,24,8,128]{3,2,1,0:T(8,128)S(1)} %get-tuple-element.39.cells_ref, ...), custom_call_target="tpu_custom_call" | custom-call | tf_op jit(solution)/shard_map/even/pallas_call | solution.py:686
  98.8 14.2 %all_to_all.34.got_ref = f32[128,1,256]{2,1,0:T(1,128)S(1)} all-to-all(f32[128,1,256]{2,1,0:T(1,128)S(1)} %get-tuple-element.60), channel_id=1, replica_groups=mesh['gx'=8,'gy'=4,'af'=4] {'gx','gy','af'}, dimensions={0} | all-to-all | bytes 262144 | tf_op jit(solution)/shard_map/all_to_all | solution.py:698
  113.0 1.2 %odd.3 = (f32[8,8,128]{2,1,0:T(8,128)}, f32[4,256]{1,0:T(4,128)}) custom-call(s32[1]{0:T(128)} %bitcast.me_ref, f32[128,1,256]{2,1,0:T(1,128)S(1)} %all_to_all.34.got_ref, f32[8,24,8,128]{3,2,1,0:T(8,128)S(1)} %get-tuple-element.39.cells_ref, f32[10,8,128]{2,1,0:T(8,128)S(1)} %get-tuple-element.61.field_ref, s32[16,128]{1,0:T(8,128)S(1)} %get-tuple-element.41.index_ref, ...), custom_call_target="tpu_custom_call" | custom-call | tf_op jit(solution)/shard_map/odd/pallas_call | solution.py:686
Async XLA Ops:
  4.0 23.0 %all-to-all-start = ((f32[128,1,512]{2,1,0:T(1,128)}), f32[128,1,512]{2,1,0:T(1,128)S(1)}, u32[]{:S(2)}, u32[]{:S(2)}) async-start(f32[128,1,512]{2,1,0:T(1,128)} %get-tuple-element.35), calls=%async_computation | async-start | bytes 524288 | tf_op jit(solution)/shard_map/all_to_all | solution.py:698
  16.3 6.7 %collective-permute-start.1 = (f32[3,8,8,128]{3,2,1,0:T(8,128)S(1)}, f32[3,8,8,128]{3,2,1,0:T(8,128)S(1)}, u32[]{:S(2)}, u32[]{:S(2)}) collective-permute-start(f32[3,8,8,128]{3,2,1,0:T(8,128)S(1)} %pad_maximum_fusion.middle_ref), channel_id=1, source_target_pairs={{16,32},{48,64},{80,96},{32,16},{64,48},{96,80},{17,33},{49,65},{8... | collective-permute-start | bytes 294920 | tf_op jit(solution)/shard_map/ppermute | solution.py:703
  19.8 3.1 %collective-permute-start = (f32[3,8,8,128]{3,2,1,0:T(8,128)S(1)}, f32[3,8,8,128]{3,2,1,0:T(8,128)S(1)}, u32[]{:S(2)}, u32[]{:S(2)}) collective-permute-start(f32[3,8,8,128]{3,2,1,0:T(8,128)S(1)} %pad_maximum_fusion.middle_ref), channel_id=1, source_target_pairs={{0,16},{32,48},{64,80},{96,112},{16,0},{48,32},{80,64},{112,96},{1... | collective-permute-start | bytes 294920 | tf_op jit(solution)/shard_map/ppermute | solution.py:703
  26.9 0.8 copy-start

commit v5 on v4

--- a/solution.py
+++ b/solution.py
@@ -148,35 +148,32 @@
 
 
 def scatter_wide(tables, late, columns_ref, rows_ref, count):
+    fields = max(len(tables), 1)
     found = []
     for side in range(3):
         if side != 1 and count == 0:
-            found.append([None] * len(tables))
+            found.append([None] * fields)
             continue
         low, high = side_rows(side, count)
-        sums = scatter([table[side] for table in tables], columns_ref[side], rows_ref[side, low:high])
         index = as_row(late[side][:4].astype(i32) - 1)
-        sums[-1] = sums[-1] + scatter([late[side][4:]], *cell_hot(index, low, high))[0]
-        found.append(sums)
-    return [gather_wide([found[side][i] for side in range(3)], count) for i in range(len(tables))]
+        (sums,) = scatter([late[side][4:]], *cell_hot(index, low, high))
+        if tables:
+            *others, last = scatter([table[side] for table in tables], columns_ref[side], rows_ref[side, low:high])
+            found.append([*others, last + sums])
+        else:
+            found.append([sums])
+    return [gather_wide([found[side][i] for side in range(3)], count) for i in range(fields)]
 
 
 def faces_of(field):
-    rows = iota((16, 128), 0)
-    lanes = iota((16, 128), 1)
-    pick = (((rows == 0) & (lanes == 0)) | ((rows == 1) & (lanes == 127))).astype(bf16)
-    both = dot_nt(jnp.concatenate([pick, pick], axis=1), jnp.concatenate(parts(field), axis=1))
-    return both[0:1], both[1:2]
+    turned = field.T
+    return turned[0:1], turned[127:128]
 
 
 def columns_of(left, right):
     width = left.shape[1]
-    held = [part.astype(f32) for row in (left, right) for part in parts(row)]
-    held = jnp.concatenate(held + [jnp.zeros((12, width), f32)], axis=0).astype(bf16)
-    rows = iota((16, 128), 0)
-    lanes = iota((16, 128), 1)
-    place = (((rows < 2) & (lanes == 0)) | ((rows >= 2) & (rows < 4) & (lanes == 127))).astype(bf16)
-    return dot_tn(held, place)
+    row = iota((128, width), 0)
+    return jnp.where(row == 0, left, jnp.where(row == 127, right, 0.0)).T
 
 
 def up_y(v, halo):
@@ -236,16 +233,20 @@
     return jnp.concatenate([got_ref[:, 0, i : i + 128].T for i in range(0, count, 128)], axis=0)
 
 
-def begin_kernel(
-    me_ref, delta_ref, from_ref, to_ref, trans_ref, well_tile_ref, well_cell_ref, well_rate_ref, *refs
-):
-    given, (out_ref, seg_ref), held, sems = refs[:10], refs[10:12], refs[12:22], refs[22]
+def begin_kernel(me_ref, *refs):
+    count = len(refs) // 2 - 2
+    given, (out_ref, seg_ref, tile_out_ref), held, sems = refs[:count], refs[count : count + 3], refs[count + 3 : -1], refs[-1]
     copies = [pltpu.make_async_copy(a, b, sems.at[i]) for i, (a, b) in enumerate(zip(given, held))]
+    passing = [pltpu.make_async_copy(held[8 + i], tile_out_ref.at[i], sems.at[count + i]) for i in range(3)]
     for copy in copies:
         copy.start()
     for copy in copies:
         copy.wait()
-    tile_ref, layer_ref, cell_ref, press_frac_ref, accum_ref, chain_ref, mf_ref, fm_ref, press_ref, cond_ref = held
+    for copy in passing:
+        copy.start()
+    tile_ref, layer_ref, cell_ref, press_frac_ref, accum_ref, chain_ref, mf_ref, fm_ref = held[:8]
+    press_ref, cond_ref, accum_matrix_ref = held[8:11]
+    delta_ref, from_ref, to_ref, trans_ref, well_tile_ref, well_cell_ref, well_rate_ref = held[11:]
     me = me_ref[0]
     code = seg_code()
     owner = fold(tile_ref[...])
@@ -281,8 +282,9 @@
     cell = fold(cell_ref[...])
     where_cell = ((((cell >> 7) * 8 + fold(layer_ref[...])) << 7) + (cell & 127) + 1).astype(f32)
     position = (iota((8, 128), 0) * 128 + iota((8, 128), 1) + 1).astype(f32)
-    slots = to_slots([where_cell, mf * press, fm * inverse * fm, fm * inverse * mf, position], hot, mask)
-    inverse_index, slots = slots[64:80], slots[:64]
+    weight = fm * inverse
+    slots = to_slots([where_cell, mf * press, weight * fm, weight * mf, weight * partial, position], hot, mask)
+    inverse_index, slots = slots[80:96], slots[:80]
     place = (owner * CAP + rank).astype(f32)
     rows = []
     for b in range(4):
@@ -294,8 +296,7 @@
             rows.append(jnp.sum(jnp.where(at, value, 0.0), axis=0, keepdims=True))
         rows.append(jnp.zeros((3, 128), f32))
     edges = [jnp.broadcast_to(jnp.sum(jnp.concatenate(rows, axis=0), axis=1, keepdims=True), (48, 128))]
-    rows = [spread(slots, 16), slots, spread(slots, -16)] + edges
-    rows += [spread(slots[:CAP], shift) for shift in BESIDE] + [jnp.zeros((48, 128), f32)]
+    rows = edges + to_three(slots) + [spread(slots[:CAP], shift) for shift in BESIDE]
     store_slots(out_ref, jnp.concatenate(rows, axis=0))
     first_face, last_face = faces_of(jnp.concatenate([swap_x(ref[...]).reshape(ROWS, 128) for ref in (press_ref, cond_ref)], axis=0))
     for across in (-16, 0, 16):
@@ -323,28 +324,34 @@
     for i in range(3):
         seg_ref[11 + i] = source[8 * i : 8 * i + 8]
     seg_ref[14] = where_cell
+    for i, ref in enumerate((press_ref, cond_ref, accum_matrix_ref)):
+        seg_ref[15 + 8 * i : 23 + 8 * i] = swap_x(ref[...])
+    for copy in passing:
+        copy.wait()
 
 
 def edge_in(row, k, i):
-    at = 64 + 12 * k + i
+    at = 12 * k + i
     return row[:, at : at + 1]
 
 
 def cells_kernel(
     me_ref,
-    got_ref, middle_ref, inside_ref, across_ref, seg_ref,
+    got_ref, inside_ref, across_ref, seg_ref,
     out_ref, cells_ref, field_ref, index_ref, columns_ref, rows_ref, edge_ref, beside_ref, res_ref,
 ):
     me = me_ref[0]
     slots = load_slots(got_ref, 384)
     even = ((me >> 4) & 1) == 0
     press, cond, accum = (
-        jnp.concatenate([swap_x(part) for part in (jnp.where(even, b, a), middle_ref[i], jnp.where(even, a, b))], axis=0)
+        jnp.concatenate(
+            [swap_x(jnp.where(even, b, a)), seg_ref[15 + 8 * i : 23 + 8 * i], swap_x(jnp.where(even, a, b))], axis=0
+        )
         for i, a, b in ((i, inside_ref[i], across_ref[i]) for i in range(3))
     )
     sums = []
     for side in range(3):
-        table = slots[side * 64 : side * 64 + 64]
+        table = slots[48 + side * 80 : 128 + side * 80]
         index = table[:CAP].astype(i32) - 1
         if side == 1:
             index_ref[...] = index
@@ -352,9 +359,9 @@
         columns, rows = cell_hot(as_row(index))
         columns_ref[side] = columns
         rows_ref[side] = rows
-        sums.append(scatter([table[16:32], table[32:48], table[48:64]], columns, rows))
-    flow, weight, mirror = (jnp.concatenate([sums[side][i] for side in range(3)], axis=0) for i in range(3))
-    beside = slots[240:336].astype(i32) - 1
+        sums.append(scatter([table[i : i + CAP] for i in range(CAP, 5 * CAP, CAP)], columns, rows))
+    flow, weight, mirror, first = (jnp.concatenate([sums[side][i] for side in range(3)], axis=0) for i in range(4))
+    beside = slots[288:384].astype(i32) - 1
     along = me & 15
     for i, (there, column) in enumerate(((along > 0, 127), (along < 15, 0))):
         part = beside[48 * i : 48 * i + 48]
@@ -377,7 +384,7 @@
     res = res - stencil(tx[1:], tx[:-1], ty[1:-1], tz[1:-1], ty_first[1:-1], press, press_halo[1:-1])
     field = inverse * res
     cells_ref[0, : EXT - 1] = tx
-    for i, value in ((1, ty), (2, tz), (3, ty_first), (6, weight * press), (7, mirror)):
+    for i, value in ((1, ty), (2, tz), (3, ty_first), (6, first - weight * press), (7, mirror)):
         cells_ref[i] = value
     cells_ref[4, 1 : EXT - 1] = inverse
     cells_ref[5, 1 : EXT - 1] = res
@@ -386,7 +393,7 @@
 
     code = seg_code().astype(f32)
     _, inverse_f, partial, fm, _, owner, _, press_f = (seg_ref[i] for i in range(8))
-    edge = jnp.where(me > 0, got_ref[before(me), :, 128:256], -1.0)
+    edge = jnp.where(me > 0, got_ref[before(me), :, 0:128], -1.0)
     lane = iota((1, 128), 1)
     cells, terms, picks, found = [], [], [], []
     ends = [code == edge_in(edge, k, 0) for k in range(4)]
@@ -400,16 +407,13 @@
         picks.append(jnp.broadcast_to(picked, (1, 128)))
         found.append(sums[4 * k + 1 : 4 * k + 4])
     for k in range(4):
-        edge = jnp.where(lane == 64 + 12 * k + 4, edge - edge_in(edge, k, 5) * sums[4 * k], edge)
+        edge = jnp.where(lane == 12 * k + 4, edge - edge_in(edge, k, 5) * sums[4 * k], edge)
     edge_ref[...] = jnp.broadcast_to(edge, (8, 128))
     late = jnp.concatenate(cells + terms, axis=0)
-    position = jnp.concatenate([seg_ref[8], seg_ref[9]], axis=0).astype(i32)
-    first = find(fm * inverse_f * partial, position)
 
     taken = [find(press[8:16].reshape(ROWS, 128), own), find(own_tile(field, 1), own)]
     rows = taken + [spread(taken[0], 1)]
-    rows += [spread(first, 16), first, spread(first, -16), spread(late, 16), late, spread(late, -16)]
-    store_slots(out_ref, jnp.concatenate(rows + picks + [jnp.zeros((4, 128), f32)], axis=0))
+    store_slots(out_ref, jnp.concatenate(rows + to_three(late) + picks + [jnp.zeros((52, 128), f32)], axis=0))
     put_faces(me, out_ref, FIRST, *faces_of(field[1:-1].reshape(-1, 128)))
     put_faces(me, out_ref, FIRST_INVERSE, *faces_of(inverse[3:19].reshape(-1, 128)))
     put_entries(out_ref, before(me), FIRST_ENDS, [end for ends in found for end in ends])
@@ -436,9 +440,9 @@
     return jnp.minimum(me + 1, TILES - 1)
 
 
-FIRST = 128
+FIRST = 76
 FIRST_ENDS = FIRST + 160
-FIRST_INVERSE = FIRST_ENDS + 16
+FIRST_INVERSE = FIRST_ENDS + 12
 WIDE = 232
 SLIM = 128
 SLIM_TWO = 248
@@ -537,7 +541,7 @@
     starts, targets, nexts, factors = edges
 
     resf = partial - fm * look_up(slots[0:16], rank, owner)
-    picks = get_entries(got_ref, after(me), 120, 4)
+    picks = get_entries(got_ref, after(me), 72, 4)
     for b in range(4):
         at = (code == starts[b]) & (nexts[b] >= 0.0)
         resf = resf - jnp.where(at, factors[b] * picks[b], 0.0)
@@ -548,10 +552,9 @@
     gain = resf + chain(tnext, frac) + mf * look_up(slots[16:32], rank, owner)
     gain = gain + arrive(code, targets, terms) + arrive(code, [edge_in(edge, k, 0) for k in range(4)], coming)
     frac = inverse_f * gain
-    late = [slots[96 + 8 * side : 104 + 8 * side] for side in range(3)]
-    first = [slots[48 + side * CAP : 64 + side * CAP] for side in range(3)]
-    (flow,) = scatter_wide([first], late, columns_ref, rows_ref, 6)
-    field = advance(cells_ref, 1, field_ref[...], wide_halo(me, got_ref, FIRST, 20), flow - cells_ref[6, 2:22])
+    late = [slots[48 + 8 * side : 56 + 8 * side] for side in range(3)]
+    (flow,) = scatter_wide([], late, columns_ref, rows_ref, 6)
+    field = advance(cells_ref, 1, field_ref[...], wide_halo(me, got_ref, FIRST, 20), flow + cells_ref[6, 2:22])
     new_field_ref[...] = field
     new_frac_ref[...] = frac
     resf_ref[...] = resf
@@ -597,18 +600,19 @@
     late = [slots[112 + 8 * side : 120 + 8 * side] for side in range(3)]
     flow, later = scatter_wide(tables, late, columns_ref, rows_ref, 7 - k)
     beside = []
-    lane = iota((ROWS, 128), 1)
-    level = iota((ROWS, 128), 0)
     for side in range(3):
-        column = jnp.zeros((ROWS, 128), f32)
+        height = ROWS if side == 1 else 8 * (6 - k)
+        level = iota((height, 128), 0) + (ROWS - height if side == 0 else 0)
+        lane = iota((height, 128), 1)
+        column = jnp.zeros((height, 128), f32)
         for i, at in enumerate((0, 127)):
             first = 48 * i + CAP * side
-            held = jnp.zeros((ROWS, 128), f32)
+            held = jnp.zeros((height, 128), f32)
             for r in range(first, first + CAP):
                 held = held + jnp.where(level == beside_ref[r : r + 1], slots[136 + r : 137 + r], 0.0)
             column = jnp.where(lane == at, jnp.sum(held, axis=1, keepdims=True), column)
-        beside.append(column.reshape(8, 8, 128))
-    beside = jnp.concatenate(beside, axis=0)[k + 2 : 22 - k]
+        beside.append(column.reshape(-1, 8, 128))
+    beside = jnp.concatenate(beside, axis=0)
     second = field_ref[...]
     third = advance(cells_ref, k, second, wide_halo(me, got_ref, WIDE, 22 - 2 * k), flow)
     inner = second[2:-2]
@@ -680,7 +684,7 @@
     send_wide(me, out_ref, k + 1, code, edges, ends_of(ends_ref), seg_ref, cells_ref, index_ref, field, frac, resf)
 
 
-def call(kernel, name, scalars, arrays, outs, space=pltpu.VMEM, scratch=(), limit=20 * 1024 * 1024):
+def call(kernel, name, scalars, arrays, outs, space=pltpu.VMEM, scratch=(), limit=20 * 1024 * 1024, out_spaces=None):
     spec = [pl.BlockSpec(memory_space=pltpu.SMEM)] * len(scalars)
     spec += [pl.BlockSpec(memory_space=space)] * len(arrays)
     return pl.pallas_call(
@@ -688,7 +692,7 @@
         name=name,
         out_shape=[jax.ShapeDtypeStruct(shape, kind) for shape, kind in outs],
         in_specs=spec,
-        out_specs=[pl.BlockSpec(memory_space=pltpu.VMEM)] * len(outs),
+        out_specs=[pl.BlockSpec(memory_space=out) for out in out_spaces or [pltpu.VMEM] * len(outs)],
         scratch_shapes=list(scratch),
         compiler_params=pltpu.CompilerParams(vmem_limit_bytes=limit),
     )(*scalars, *arrays)
@@ -708,31 +712,35 @@
     conn_tile, conn_layer, conn_cell, inter_delta, inter_from, inter_to, inter_trans, well_tile, well_cell, well_rate,
 ):
     me = lax.axis_index(ALL).astype(i32).reshape(1)
-    stacked = jnp.stack([press_matrix, cond_matrix, accum_matrix])
-    inside = swapped(stacked, 0)
-    across = swapped(stacked, 1)
     wide = (EXT, 8, 128)
     tile = (LAYERS, 8, 128)
     seg = (8, 128)
 
-    given = (conn_tile, conn_layer, conn_cell, press_frac, accum_frac, trans_chain, couple_mf, couple_fm, press_matrix, cond_matrix)
-    message, segs = call(
+    given = (
+        conn_tile, conn_layer, conn_cell, press_frac, accum_frac, trans_chain, couple_mf, couple_fm,
+        press_matrix, cond_matrix, accum_matrix,
+        inter_delta, inter_from, inter_to, inter_trans, well_tile, well_cell, well_rate,
+    )
+    message, segs, stacked = call(
         begin_kernel,
         "begin",
-        (me, inter_delta, inter_from, inter_to, inter_trans, well_tile, well_cell, well_rate),
+        (me,),
         given,
-        [((TILES, 1, 512), f32), ((15, *seg), f32)],
+        [((TILES, 1, 512), f32), ((39, *seg), f32), ((3, *tile), f32)],
         pl.ANY,
-        [pltpu.VMEM(a.shape, a.dtype) for a in given] + [pltpu.SemaphoreType.DMA((len(given),))],
+        [(pltpu.VMEM if a.ndim > 1 else pltpu.SMEM)(a.shape, a.dtype) for a in given] + [pltpu.SemaphoreType.DMA((len(given) + 3,))],
         64 * 1024 * 1024,
+        [pltpu.VMEM, pltpu.VMEM, pl.ANY],
     )
+    inside = swapped(stacked, 0)
+    across = swapped(stacked, 1)
     got = exchange(message)
     message, cells, field, index, columns, rows, edge, beside, res_matrix = call(
         cells_kernel,
         "cells",
         (me,),
-        (got, stacked, inside, across, segs),
-        [((TILES, 1, 512), f32), ((8, *wide), f32), ((22, 8, 128), f32), ((CAP, 128), i32), ((3, 128, SLOTS), bf16),
+        (got, inside, across, segs),
+        [((TILES, 1, 384), f32), ((8, *wide), f32), ((22, 8, 128), f32), ((CAP, 128), i32), ((3, 128, SLOTS), bf16),
          ((3, ROWS, SLOTS), bf16), (seg, f32), ((96, 128), i32), (tile, f32)],
     )
     kept = (index, columns, rows, segs, edge)

time: 115 us -> 112 us (0.974)
  Pallas kernels: 14.5 us -> 13.1 us
  blocking collectives: 75.2 us -> 74 us
    pallas_call x7, Pallas kernels: 14.5 us -> 13.1 us  [call(): pl.pallas_call(kernel, name=name, out_shape=[jax.ShapeDtypeStruct(shape,...]
    all_to_all x5, blocking collectives: 75.2 us -> 74 us  [exchange(): return lax.all_to_all(message, ALL, split_axis=0, concat_axis=0, tiled=True)]
  transfers between devices with their start and end apart: 3 -> 3, of which waited for: 2 -> 2; matrix products, arithmetic and copies ran while one was open for 1% -> 0% of each run, Pallas kernels for 0% -> 0%
where the time goes in v5:
time: 112 us
  blocking collectives  74 us (66%)
  starting transfers between devices  15.1 us (13%)
  Pallas kernels  13.1 us (12%)
  waiting for transfers between devices  7.82 us (7%)
    all_to_all x5, blocking collectives, exchange(): return lax.all_to_all(message, ALL, split_axis=0, concat_axis=0, tiled=True)  74 us
    pallas_call x7, Pallas kernels, call(): pl.pallas_call(kernel, name=name, out_shape=[jax.ShapeDtypeStruct(shape,...  13.1 us
    all_to_all x1, starting transfers between devices, exchange(): return lax.all_to_all(message, ALL, split_axis=0, concat_axis=0, tiled=True)  11.5 us
    all_to_all x1, waiting for transfers between devices, exchange(): return lax.all_to_all(message, ALL, split_axis=0, concat_axis=0, tiled=True)  4.21 us
    ppermute x2, starting transfers between devices, swapped(): return lax.ppermute(block, 'gx', pairs + [(j, i) for i, j in pairs])  3.63 us
    ppermute x2, waiting for transfers between devices, swapped(): return lax.ppermute(block, 'gx', pairs + [(j, i) for i, j in pairs])  3.61 us
  transfers between devices with their start and end apart: 3, of which 2 were waited for; matrix products, arithmetic and copies ran while one was open for 0% of the time, Pallas kernels for 0%

profile of v5, /device:TPU:1, one launch (start us, length us, event | category | flops | bytes accessed | tf_op | source)
XLA Modules:
  0.0 111.7 jit_solution(13920312770531866942)
XLA Ops:
  0.6 2.7 %begin.1 = (f32[128,1,512]{2,1,0:T(1,128)}, f32[39,8,128]{2,1,0:T(8,128)}, f32[3,8,8,128]{3,2,1,0:T(8,128)}) custom-call(s32[1]{0:T(128)} %bitcast.me_ref, s32[4,256]{1,0:T(4,128)} %refs_0_.1, s32[4,256]{1,0:T(4,128)} %refs_1_.1, s32[4,256]{1,0:T(4,128)} %refs_2_.1, f32[4,256]{1,0:T(4,128)} %refs_3_.1, f32[4,256]{1,0:T(4,128)} %refs_4_.1, f32[4,256]{1,0:T(4,128)} %refs_5_.1, ...), custom_call_target="tpu_custom_call" | custom-call | tf_op jit(solution)/shard_map/begin/pallas_call | solution.py:690
  3.4 11.5 %all-to-all-start = ((f32[128,1,512]{2,1,0:T(1,128)}), f32[128,1,512]{2,1,0:T(1,128)S(1)}, u32[]{:S(2)}, u32[]{:S(2)}) async-start(f32[128,1,512]{2,1,0:T(1,128)} %get-tuple-element.36), calls=%async_computation | async-start | bytes 524288 | tf_op jit(solution)/shard_map/all_to_all | solution.py:702
  14.9 3.5 %collective-permute-start.1 = (f32[3,8,8,128]{3,2,1,0:T(8,128)}, f32[3,8,8,128]{3,2,1,0:T(8,128)S(1)}, u32[]{:S(2)}, u32[]{:S(2)}) collective-permute-start(f32[3,8,8,128]{3,2,1,0:T(8,128)} %get-tuple-element.37), channel_id=1, source_target_pairs={{16,32},{48,64},{80,96},{32,16},{64,48},{96,80},{17,33},{49,65},{8... | collective-permute-start | bytes 294920 | tf_op jit(solution)/shard_map/ppermute | solution.py:707
  18.4 0.1 collective-permute-start
  18.5 3.6 %collective-permute-done.1.across_ref = f32[3,8,8,128]{3,2,1,0:T(8,128)S(1)} collective-permute-done((f32[3,8,8,128]{3,2,1,0:T(8,128)}, f32[3,8,8,128]{3,2,1,0:T(8,128)S(1)}, u32[]{:S(2)}, u32[]{:S(2)}) %collective-permute-start.1) | collective-permute-done | bytes 98336 | tf_op jit(solution)/shard_map/ppermute | solution.py:707
  22.2 0.0 collective-permute-done.inside_ref
  22.2 4.2 %all-to-all-done.got_ref = f32[128,1,512]{2,1,0:T(1,128)S(1)} async-done(((f32[128,1,512]{2,1,0:T(1,128)}), f32[128,1,512]{2,1,0:T(1,128)S(1)}, u32[]{:S(2)}, u32[]{:S(2)}) %all-to-all-start) | async-done | bytes 262176 | tf_op jit(solution)/shard_map/all_to_all | solution.py:702
  26.4 0.0 copy-start
  26.4 0.9 copy-done
  27.3 2.9 %cells.1 = (f32[128,1,384]{2,1,0:T(1,128)S(1)}, f32[8,24,8,128]{3,2,1,0:T(8,128)S(1)}, f32[22,8,128]{2,1,0:T(8,128)S(1)}, s32[16,128]{1,0:T(8,128)S(1)}, bf16[3,...) custom-call(s32[1]{0:T(128)} %bitcast.me_ref, ...), custom_call_target="tpu_custom_call" | custom-call | tf_op jit(solution)/shard_map/cells/pallas_call | solution.py:690
  30.2 15.1 %all_to_all.30.got_ref = f32[128,1,384]{2,1,0:T(1,128)S(1)} all-to-all(f32[128,1,384]{2,1,0:T(1,128)S(1)} %get-tuple-element.40), channel_id=1, replica_groups=mesh['gx'=8,'gy'=4,'af'=4] {'gx','gy','af'}, dimensions={0} | all-to-all | bytes 393216 | tf_op jit(solution)/shard_map/all_to_all | solution.py:702
  45.2 1.5 %first.1 = (f32[128,1,512]{2,1,0:T(1,128)S(1)}, f32[20,8,128]{2,1,0:T(8,128)S(1)}, f32[8,128]{1,0:T(8,128)S(1)}, f32[8,128]{1,0:T(8,128)S(1)}, f32[8,128]{1,0:T(...) custom-call(s32[1]{0:T(128)} %bitcast.me_ref, f32[128,1,384]{2,1,0:T(1,128)S(1)} %all_to_all.30.got_ref, ...), custom_call_target="tpu_custom_call" | custom-call | tf_op jit(solution)/shard_map/first/pallas_call | solution.py:690
  46.7 15.3 %all_to_all.31.got_ref = f32[128,1,512]{2,1,0:T(1,128)S(1)} all-to-all(f32[128,1,512]{2,1,0:T(1,128)S(1)} %get-tuple-element.48), channel_id=1, replica_groups=mesh['gx'=8,'gy'=4,'af'=4] {'gx','gy','af'}, dimensions={0} | all-to-all | bytes 524288 | tf_op jit(solution)/shard_map/all_to_all | solution.py:702
  62.0 1.7 %even.2 = (f32[128,1,256]{2,1,0:T(1,128)S(1)}, f32[18,8,128]{2,1,0:T(8,128)S(1)}, f32[16,8,128]{2,1,0:T(8,128)S(1)}, f32[8,128]{1,0:T(8,128)S(1)}) custom-call(s32[1]{0:T(128)} %bitcast.me_ref, f32[128,1,512]{2,1,0:T(1,128)S(1)} %all_to_all.31.got_ref, f32[8,24,8,128]{3,2,1,0:T(8,128)S(1)} %get-tuple-element.41.cells_ref, ...), custom_call_target="tpu_custom_call" | custom-call | tf_op jit(solution)/shard_map/even/pallas_call | solution.py:690
  63.7 14.2 %all_to_all.32.got_ref = f32[128,1,256]{2,1,0:T(1,128)S(1)} all-to-all(f32[128,1,256]{2,1,0:T(1,128)S(1)} %get-tuple-element.55), channel_id=1, replica_groups=mesh['gx'=8,'gy'=4,'af'=4] {'gx','gy','af'}, dimensions={0} | all-to-all | bytes 262144 | tf_op jit(solution)/shard_map/all_to_all | solution.py:702
  77.9 1.6 %odd.2 = (f32[128,1,512]{2,1,0:T(1,128)S(1)}, f32[14,8,128]{2,1,0:T(8,128)S(1)}, f32[8,128]{1,0:T(8,128)S(1)}) custom-call(s32[1]{0:T(128)} %bitcast.me_ref, f32[128,1,256]{2,1,0:T(1,128)S(1)} %all_to_all.32.got_ref, f32[8,24,8,128]{3,2,1,0:T(8,128)S(1)} %get-tuple-element.41.cells_ref, f32[16,8,128]{2,1,0:T(8,128)S(1)} %get-tuple-element.56.field_ref, ...), custom_call_target="tpu_custom_call" | custom-call | tf_op jit(solution)/shard_map/odd/pallas_call | solution.py:690
  79.4 15.2 %all_to_all.33.got_ref = f32[128,1,512]{2,1,0:T(1,128)S(1)} all-to-all(f32[128,1,512]{2,1,0:T(1,128)S(1)} %get-tuple-element.59), channel_id=1, replica_groups=mesh['gx'=8,'gy'=4,'af'=4] {'gx','gy','af'}, dimensions={0} | all-to-all | bytes 524288 | tf_op jit(solution)/shard_map/all_to_all | solution.py:702
  94.7 1.6 %even.3 = (f32[128,1,256]{2,1,0:T(1,128)S(1)}, f32[12,8,128]{2,1,0:T(8,128)S(1)}, f32[10,8,128]{2,1,0:T(8,128)S(1)}, f32[8,128]{1,0:T(8,128)S(1)}) custom-call(s32[1]{0:T(128)} %bitcast.me_ref, f32[128,1,512]{2,1,0:T(1,128)S(1)} %all_to_all.33.got_ref, f32[8,24,8,128]{3,2,1,0:T(8,128)S(1)} %get-tuple-element.41.cells_ref, ...), custom_call_target="tpu_custom_call" | custom-call | tf_op jit(solution)/shard_map/even/pallas_call | solution.py:690
  96.3 14.2 %all_to_all.34.got_ref = f32[128,1,256]{2,1,0:T(1,128)S(1)} all-to-all(f32[128,1,256]{2,1,0:T(1,128)S(1)} %get-tuple-element.62), channel_id=1, replica_groups=mesh['gx'=8,'gy'=4,'af'=4] {'gx','gy','af'}, dimensions={0} | all-to-all | bytes 262144 | tf_op jit(solution)/shard_map/all_to_all | solution.py:702
  110.5 1.2 %odd.3 = (f32[8,8,128]{2,1,0:T(8,128)}, f32[4,256]{1,0:T(4,128)}) custom-call(s32[1]{0:T(128)} %bitcast.me_ref, f32[128,1,256]{2,1,0:T(1,128)S(1)} %all_to_all.34.got_ref, f32[8,24,8,128]{3,2,1,0:T(8,128)S(1)} %get-tuple-element.41.cells_ref, f32[10,8,128]{2,1,0:T(8,128)S(1)} %get-tuple-element.63.field_ref, s32[16,128]{1,0:T(8,128)S(1)} %get-tuple-element.43.index_ref, ...), custom_call_target="tpu_custom_call" | custom-call | tf_op jit(solution)/shard_map/odd/pallas_call | solution.py:690
Async XLA Ops:
  3.4 23.0 %all-to-all-start = ((f32[128,1,512]{2,1,0:T(1,128)}), f32[128,1,512]{2,1,0:T(1,128)S(1)}, u32[]{:S(2)}, u32[]{:S(2)}) async-start(f32[128,1,512]{2,1,0:T(1,128)} %get-tuple-element.36), calls=%async_computation | async-start | bytes 524288 | tf_op jit(solution)/shard_map/all_to_all | solution.py:702
  14.9 7.3 %collective-permute-start.1 = (f32[3,8,8,128]{3,2,1,0:T(8,128)}, f32[3,8,8,128]{3,2,1,0:T(8,128)S(1)}, u32[]{:S(2)}, u32[]{:S(2)}) collective-permute-start(f32[3,8,8,128]{3,2,1,0:T(8,128)} %get-tuple-element.37), channel_id=1, source_target_pairs={{16,32},{48,64},{80,96},{32,16},{64,48},{96,80},{17,33},{49,65},{8... | collective-permute-start | bytes 294920 | tf_op jit(solution)/shard_map/ppermute | solution.py:707
  18.4 3.7 %collective-permute-start = (f32[3,8,8,128]{3,2,1,0:T(8,128)}, f32[3,8,8,128]{3,2,1,0:T(8,128)S(1)}, u32[]{:S(2)}, u32[]{:S(2)}) collective-permute-start(f32[3,8,8,128]{3,2,1,0:T(8,128)} %get-tuple-element.37), channel_id=1, source_target_pairs={{0,16},{32,48},{64,80},{96,112},{16,0},{48,32},{80,64},{112,96},{1... | collective-permute-start | bytes 294920 | tf_op jit(solution)/shard_map/ppermute | solution.py:707
  26.4 0.9 copy-start

commit v6 on v5

--- a/solution.py
+++ b/solution.py
@@ -684,6 +684,10 @@
     send_wide(me, out_ref, k + 1, code, edges, ends_of(ends_ref), seg_ref, cells_ref, index_ref, field, frac, resf)
 
 
+def hold_kernel(given_ref, out_ref):
+    out_ref[...] = given_ref[...]
+
+
 def call(kernel, name, scalars, arrays, outs, space=pltpu.VMEM, scratch=(), limit=20 * 1024 * 1024, out_spaces=None):
     spec = [pl.BlockSpec(memory_space=pltpu.SMEM)] * len(scalars)
     spec += [pl.BlockSpec(memory_space=space)] * len(arrays)
@@ -734,6 +738,7 @@
     )
     inside = swapped(stacked, 0)
     across = swapped(stacked, 1)
+    (segs,) = call(hold_kernel, "hold", (), (segs,), [(segs.shape, f32)])
     got = exchange(message)
     message, cells, field, index, columns, rows, edge, beside, res_matrix = call(
         cells_kernel,

time: 112 us -> 111 us (level)
    pallas_call x7 -> x8, Pallas kernels: 13.1 us -> 13.2 us  [call(): pl.pallas_call(kernel, name=name, out_shape=[jax.ShapeDtypeStruct(shape,...]
where the time goes in v6:
time: 111 us
  blocking collectives  74 us (67%)
  starting transfers between devices  15.1 us (14%)
  Pallas kernels  13.2 us (12%)
  waiting for transfers between devices  6.89 us (6%)
    all_to_all x5, blocking collectives, exchange(): return lax.all_to_all(message, ALL, split_axis=0, concat_axis=0, tiled=True)  74 us
    pallas_call x8, Pallas kernels, call(): pl.pallas_call(kernel, name=name, out_shape=[jax.ShapeDtypeStruct(shape,...  13.2 us
    all_to_all x1, starting transfers between devices, exchange(): return lax.all_to_all(message, ALL, split_axis=0, concat_axis=0, tiled=True)  11.5 us
    all_to_all x1, waiting for transfers between devices, exchange(): return lax.all_to_all(message, ALL, split_axis=0, concat_axis=0, tiled=True)  4.21 us
    ppermute x2, starting transfers between devices, swapped(): return lax.ppermute(block, 'gx', pairs + [(j, i) for i, j in pairs])  3.63 us
    ppermute x2, waiting for transfers between devices, swapped(): return lax.ppermute(block, 'gx', pairs + [(j, i) for i, j in pairs])  2.68 us
  transfers between devices with their start and end apart: 3, of which 2 were waited for; matrix products, arithmetic and copies ran while one was open for 0% of the time, Pallas kernels for 0%

profile of v6, /device:TPU:1, one launch (start us, length us, event | category | flops | bytes accessed | tf_op | source)
XLA Modules:
  0.0 110.8 jit_solution(3409615553192007914)
XLA Ops:
  0.6 2.7 %begin.1 = (f32[128,1,512]{2,1,0:T(1,128)}, f32[39,8,128]{2,1,0:T(8,128)}, f32[3,8,8,128]{3,2,1,0:T(8,128)}) custom-call(s32[1]{0:T(128)} %bitcast.me_ref, s32[4,256]{1,0:T(4,128)} %refs_0_.1, s32[4,256]{1,0:T(4,128)} %refs_1_.1, s32[4,256]{1,0:T(4,128)} %refs_2_.1, f32[4,256]{1,0:T(4,128)} %refs_3_.1, f32[4,256]{1,0:T(4,128)} %refs_4_.1, f32[4,256]{1,0:T(4,128)} %refs_5_.1, ...), custom_call_target="tpu_custom_call" | custom-call | tf_op jit(solution)/shard_map/begin/pallas_call | solution.py:694
  3.4 11.5 %all-to-all-start = ((f32[128,1,512]{2,1,0:T(1,128)}), f32[128,1,512]{2,1,0:T(1,128)S(1)}, u32[]{:S(2)}, u32[]{:S(2)}) async-start(f32[128,1,512]{2,1,0:T(1,128)} %get-tuple-element.36), calls=%async_computation | async-start | bytes 524288 | tf_op jit(solution)/shard_map/all_to_all | solution.py:706
  14.9 3.5 %collective-permute-start.1 = (f32[3,8,8,128]{3,2,1,0:T(8,128)}, f32[3,8,8,128]{3,2,1,0:T(8,128)S(1)}, u32[]{:S(2)}, u32[]{:S(2)}) collective-permute-start(f32[3,8,8,128]{3,2,1,0:T(8,128)} %get-tuple-element.37), channel_id=1, source_target_pairs={{16,32},{48,64},{80,96},{32,16},{64,48},{96,80},{17,33},{49,65},{8... | collective-permute-start | bytes 294920 | tf_op jit(solution)/shard_map/ppermute | solution.py:711
  18.4 0.1 collective-permute-start
  18.5 0.0 copy-start
  18.6 0.9 copy-done
  19.5 2.7 %collective-permute-done.1.across_ref = f32[3,8,8,128]{3,2,1,0:T(8,128)S(1)} collective-permute-done((f32[3,8,8,128]{3,2,1,0:T(8,128)}, f32[3,8,8,128]{3,2,1,0:T(8,128)S(1)}, u32[]{:S(2)}, u32[]{:S(2)}) %collective-permute-start.1) | collective-permute-done | bytes 98336 | tf_op jit(solution)/shard_map/ppermute | solution.py:711
  22.2 0.0 collective-permute-done.inside_ref
  22.2 4.2 %all-to-all-done.got_ref = f32[128,1,512]{2,1,0:T(1,128)S(1)} async-done(((f32[128,1,512]{2,1,0:T(1,128)}), f32[128,1,512]{2,1,0:T(1,128)S(1)}, u32[]{:S(2)}, u32[]{:S(2)}) %all-to-all-start) | async-done | bytes 262176 | tf_op jit(solution)/shard_map/all_to_all | solution.py:706
  26.4 2.9 %cells.1 = (f32[128,1,384]{2,1,0:T(1,128)S(1)}, f32[8,24,8,128]{3,2,1,0:T(8,128)S(1)}, f32[22,8,128]{2,1,0:T(8,128)S(1)}, s32[16,128]{1,0:T(8,128)S(1)}, bf16[3,...) custom-call(s32[1]{0:T(128)} %bitcast.me_ref, ...), custom_call_target="tpu_custom_call" | custom-call | tf_op jit(solution)/shard_map/cells/pallas_call | solution.py:694
  29.2 15.1 %all_to_all.30.got_ref = f32[128,1,384]{2,1,0:T(1,128)S(1)} all-to-all(f32[128,1,384]{2,1,0:T(1,128)S(1)} %get-tuple-element.40), channel_id=1, replica_groups=mesh['gx'=8,'gy'=4,'af'=4] {'gx','gy','af'}, dimensions={0} | all-to-all | bytes 393216 | tf_op jit(solution)/shard_map/all_to_all | solution.py:706
  44.3 1.5 %first.1 = (f32[128,1,512]{2,1,0:T(1,128)S(1)}, f32[20,8,128]{2,1,0:T(8,128)S(1)}, f32[8,128]{1,0:T(8,128)S(1)}, f32[8,128]{1,0:T(8,128)S(1)}, f32[8,128]{1,0:T(...) custom-call(s32[1]{0:T(128)} %bitcast.me_ref, f32[128,1,384]{2,1,0:T(1,128)S(1)} %all_to_all.30.got_ref, ...), custom_call_target="tpu_custom_call" | custom-call | tf_op jit(solution)/shard_map/first/pallas_call | solution.py:694
  45.8 15.3 %all_to_all.31.got_ref = f32[128,1,512]{2,1,0:T(1,128)S(1)} all-to-all(f32[128,1,512]{2,1,0:T(1,128)S(1)} %get-tuple-element.48), channel_id=1, replica_groups=mesh['gx'=8,'gy'=4,'af'=4] {'gx','gy','af'}, dimensions={0} | all-to-all | bytes 524288 | tf_op jit(solution)/shard_map/all_to_all | solution.py:706
  61.1 1.7 %even.2 = (f32[128,1,256]{2,1,0:T(1,128)S(1)}, f32[18,8,128]{2,1,0:T(8,128)S(1)}, f32[16,8,128]{2,1,0:T(8,128)S(1)}, f32[8,128]{1,0:T(8,128)S(1)}) custom-call(s32[1]{0:T(128)} %bitcast.me_ref, f32[128,1,512]{2,1,0:T(1,128)S(1)} %all_to_all.31.got_ref, f32[8,24,8,128]{3,2,1,0:T(8,128)S(1)} %get-tuple-element.41.cells_ref, ...), custom_call_target="tpu_custom_call" | custom-call | tf_op jit(solution)/shard_map/even/pallas_call | solution.py:694
  62.8 14.2 %all_to_all.32.got_ref = f32[128,1,256]{2,1,0:T(1,128)S(1)} all-to-all(f32[128,1,256]{2,1,0:T(1,128)S(1)} %get-tuple-element.55), channel_id=1, replica_groups=mesh['gx'=8,'gy'=4,'af'=4] {'gx','gy','af'}, dimensions={0} | all-to-all | bytes 262144 | tf_op jit(solution)/shard_map/all_to_all | solution.py:706
  77.0 1.6 %odd.2 = (f32[128,1,512]{2,1,0:T(1,128)S(1)}, f32[14,8,128]{2,1,0:T(8,128)S(1)}, f32[8,128]{1,0:T(8,128)S(1)}) custom-call(s32[1]{0:T(128)} %bitcast.me_ref, f32[128,1,256]{2,1,0:T(1,128)S(1)} %all_to_all.32.got_ref, f32[8,24,8,128]{3,2,1,0:T(8,128)S(1)} %get-tuple-element.41.cells_ref, f32[16,8,128]{2,1,0:T(8,128)S(1)} %get-tuple-element.56.field_ref, ...), custom_call_target="tpu_custom_call" | custom-call | tf_op jit(solution)/shard_map/odd/pallas_call | solution.py:694
  78.6 15.2 %all_to_all.33.got_ref = f32[128,1,512]{2,1,0:T(1,128)S(1)} all-to-all(f32[128,1,512]{2,1,0:T(1,128)S(1)} %get-tuple-element.59), channel_id=1, replica_groups=mesh['gx'=8,'gy'=4,'af'=4] {'gx','gy','af'}, dimensions={0} | all-to-all | bytes 524288 | tf_op jit(solution)/shard_map/all_to_all | solution.py:706
  93.8 1.6 %even.3 = (f32[128,1,256]{2,1,0:T(1,128)S(1)}, f32[12,8,128]{2,1,0:T(8,128)S(1)}, f32[10,8,128]{2,1,0:T(8,128)S(1)}, f32[8,128]{1,0:T(8,128)S(1)}) custom-call(s32[1]{0:T(128)} %bitcast.me_ref, f32[128,1,512]{2,1,0:T(1,128)S(1)} %all_to_all.33.got_ref, f32[8,24,8,128]{3,2,1,0:T(8,128)S(1)} %get-tuple-element.41.cells_ref, ...), custom_call_target="tpu_custom_call" | custom-call | tf_op jit(solution)/shard_map/even/pallas_call | solution.py:694
  95.4 14.2 %all_to_all.34.got_ref = f32[128,1,256]{2,1,0:T(1,128)S(1)} all-to-all(f32[128,1,256]{2,1,0:T(1,128)S(1)} %get-tuple-element.62), channel_id=1, replica_groups=mesh['gx'=8,'gy'=4,'af'=4] {'gx','gy','af'}, dimensions={0} | all-to-all | bytes 262144 | tf_op jit(solution)/shard_map/all_to_all | solution.py:706
  109.6 1.2 %odd.3 = (f32[8,8,128]{2,1,0:T(8,128)}, f32[4,256]{1,0:T(4,128)}) custom-call(s32[1]{0:T(128)} %bitcast.me_ref, f32[128,1,256]{2,1,0:T(1,128)S(1)} %all_to_all.34.got_ref, f32[8,24,8,128]{3,2,1,0:T(8,128)S(1)} %get-tuple-element.41.cells_ref, f32[10,8,128]{2,1,0:T(8,128)S(1)} %get-tuple-element.63.field_ref, s32[16,128]{1,0:T(8,128)S(1)} %get-tuple-element.43.index_ref, ...), custom_call_target="tpu_custom_call" | custom-call | tf_op jit(solution)/shard_map/odd/pallas_call | solution.py:694
  (1 shorter events, 0.0 us)
Async XLA Ops:
  3.4 23.0 %all-to-all-start = ((f32[128,1,512]{2,1,0:T(1,128)}), f32[128,1,512]{2,1,0:T(1,128)S(1)}, u32[]{:S(2)}, u32[]{:S(2)}) async-start(f32[128,1,512]{2,1,0:T(1,128)} %get-tuple-element.36), calls=%async_computation | async-start | bytes 524288 | tf_op jit(solution)/shard_map/all_to_all | solution.py:706
  14.9 7.3 %collective-permute-start.1 = (f32[3,8,8,128]{3,2,1,0:T(8,128)}, f32[3,8,8,128]{3,2,1,0:T(8,128)S(1)}, u32[]{:S(2)}, u32[]{:S(2)}) collective-permute-start(f32[3,8,8,128]{3,2,1,0:T(8,128)} %get-tuple-element.37), channel_id=1, source_target_pairs={{16,32},{48,64},{80,96},{32,16},{64,48},{96,80},{17,33},{49,65},{8... | collective-permute-start | bytes 294920 | tf_op jit(solution)/shard_map/ppermute | solution.py:711
  18.4 3.7 %collective-permute-start = (f32[3,8,8,128]{3,2,1,0:T(8,128)}, f32[3,8,8,128]{3,2,1,0:T(8,128)S(1)}, u32[]{:S(2)}, u32[]{:S(2)}) collective-permute-start(f32[3,8,8,128]{3,2,1,0:T(8,128)} %get-tuple-element.37), channel_id=1, source_target_pairs={{0,16},{32,48},{64,80},{96,112},{16,0},{48,32},{80,64},{112,96},{1... | collective-permute-start | bytes 294920 | tf_op jit(solution)/shard_map/ppermute | solution.py:711
  18.5 0.9 copy-start

commit v7 on v6

--- a/solution.py
+++ b/solution.py
@@ -166,8 +166,14 @@
 
 
 def faces_of(field):
-    turned = field.T
-    return turned[0:1], turned[127:128]
+    if field.shape[0] >= 128:
+        turned = field.T
+        return turned[0:1], turned[127:128]
+    rows = iota((16, 128), 0)
+    lanes = iota((16, 128), 1)
+    pick = (((rows == 0) & (lanes == 0)) | ((rows == 1) & (lanes == 127))).astype(bf16)
+    both = dot_nt(jnp.concatenate([pick, pick], axis=1), jnp.concatenate(parts(field), axis=1))
+    return both[0:1], both[1:2]
 
 
 def columns_of(left, right):

time: 111 us -> 111 us (level)
  no operation moved by 1% of the time
where the time goes in v7:
time: 111 us
  blocking collectives  74 us (67%)
  starting transfers between devices  15.1 us (14%)
  Pallas kernels  13 us (12%)
  waiting for transfers between devices  6.89 us (6%)
    all_to_all x5, blocking collectives, exchange(): return lax.all_to_all(message, ALL, split_axis=0, concat_axis=0, tiled=True)  74 us
    pallas_call x8, Pallas kernels, call(): pl.pallas_call(kernel, name=name, out_shape=[jax.ShapeDtypeStruct(shape,...  13 us
    all_to_all x1, starting transfers between devices, exchange(): return lax.all_to_all(message, ALL, split_axis=0, concat_axis=0, tiled=True)  11.5 us
    all_to_all x1, waiting for transfers between devices, exchange(): return lax.all_to_all(message, ALL, split_axis=0, concat_axis=0, tiled=True)  4.21 us
    ppermute x2, starting transfers between devices, swapped(): return lax.ppermute(block, 'gx', pairs + [(j, i) for i, j in pairs])  3.63 us
    ppermute x2, waiting for transfers between devices, swapped(): return lax.ppermute(block, 'gx', pairs + [(j, i) for i, j in pairs])  2.68 us
  transfers between devices with their start and end apart: 3, of which 2 were waited for; matrix products, arithmetic and copies ran while one was open for 0% of the time, Pallas kernels for 0%

profile of v7, /device:TPU:1, one launch (start us, length us, event | category | flops | bytes accessed | tf_op | source)
XLA Modules:
  0.0 110.6 jit_solution(1806398143767165433)
XLA Ops:
  0.6 2.7 %begin.1 = (f32[128,1,512]{2,1,0:T(1,128)}, f32[39,8,128]{2,1,0:T(8,128)}, f32[3,8,8,128]{3,2,1,0:T(8,128)}) custom-call(s32[1]{0:T(128)} %bitcast.me_ref, s32[4,256]{1,0:T(4,128)} %refs_0_.1, s32[4,256]{1,0:T(4,128)} %refs_1_.1, s32[4,256]{1,0:T(4,128)} %refs_2_.1, f32[4,256]{1,0:T(4,128)} %refs_3_.1, f32[4,256]{1,0:T(4,128)} %refs_4_.1, f32[4,256]{1,0:T(4,128)} %refs_5_.1, ...), custom_call_target="tpu_custom_call" | custom-call | tf_op jit(solution)/shard_map/begin/pallas_call | solution.py:700
  3.4 11.5 %all-to-all-start = ((f32[128,1,512]{2,1,0:T(1,128)}), f32[128,1,512]{2,1,0:T(1,128)S(1)}, u32[]{:S(2)}, u32[]{:S(2)}) async-start(f32[128,1,512]{2,1,0:T(1,128)} %get-tuple-element.36), calls=%async_computation | async-start | bytes 524288 | tf_op jit(solution)/shard_map/all_to_all | solution.py:712
  14.9 3.5 %collective-permute-start.1 = (f32[3,8,8,128]{3,2,1,0:T(8,128)}, f32[3,8,8,128]{3,2,1,0:T(8,128)S(1)}, u32[]{:S(2)}, u32[]{:S(2)}) collective-permute-start(f32[3,8,8,128]{3,2,1,0:T(8,128)} %get-tuple-element.37), channel_id=1, source_target_pairs={{16,32},{48,64},{80,96},{32,16},{64,48},{96,80},{17,33},{49,65},{8... | collective-permute-start | bytes 294920 | tf_op jit(solution)/shard_map/ppermute | solution.py:717
  18.4 0.1 collective-permute-start
  18.5 0.0 copy-start
  18.5 0.9 copy-done
  19.5 2.7 %collective-permute-done.1.across_ref = f32[3,8,8,128]{3,2,1,0:T(8,128)S(1)} collective-permute-done((f32[3,8,8,128]{3,2,1,0:T(8,128)}, f32[3,8,8,128]{3,2,1,0:T(8,128)S(1)}, u32[]{:S(2)}, u32[]{:S(2)}) %collective-permute-start.1) | collective-permute-done | bytes 98336 | tf_op jit(solution)/shard_map/ppermute | solution.py:717
  22.1 0.0 collective-permute-done.inside_ref
  22.2 4.2 %all-to-all-done.got_ref = f32[128,1,512]{2,1,0:T(1,128)S(1)} async-done(((f32[128,1,512]{2,1,0:T(1,128)}), f32[128,1,512]{2,1,0:T(1,128)S(1)}, u32[]{:S(2)}, u32[]{:S(2)}) %all-to-all-start) | async-done | bytes 262176 | tf_op jit(solution)/shard_map/all_to_all | solution.py:712
  26.4 2.9 %cells.1 = (f32[128,1,384]{2,1,0:T(1,128)S(1)}, f32[8,24,8,128]{3,2,1,0:T(8,128)S(1)}, f32[22,8,128]{2,1,0:T(8,128)S(1)}, s32[16,128]{1,0:T(8,128)S(1)}, bf16[3,...) custom-call(s32[1]{0:T(128)} %bitcast.me_ref, ...), custom_call_target="tpu_custom_call" | custom-call | tf_op jit(solution)/shard_map/cells/pallas_call | solution.py:700
  29.2 15.0 %all_to_all.30.got_ref = f32[128,1,384]{2,1,0:T(1,128)S(1)} all-to-all(f32[128,1,384]{2,1,0:T(1,128)S(1)} %get-tuple-element.40), channel_id=1, replica_groups=mesh['gx'=8,'gy'=4,'af'=4] {'gx','gy','af'}, dimensions={0} | all-to-all | bytes 393216 | tf_op jit(solution)/shard_map/all_to_all | solution.py:712
  44.3 1.5 %first.1 = (f32[128,1,512]{2,1,0:T(1,128)S(1)}, f32[20,8,128]{2,1,0:T(8,128)S(1)}, f32[8,128]{1,0:T(8,128)S(1)}, f32[8,128]{1,0:T(8,128)S(1)}, f32[8,128]{1,0:T(...) custom-call(s32[1]{0:T(128)} %bitcast.me_ref, f32[128,1,384]{2,1,0:T(1,128)S(1)} %all_to_all.30.got_ref, ...), custom_call_target="tpu_custom_call" | custom-call | tf_op jit(solution)/shard_map/first/pallas_call | solution.py:700
  45.8 15.3 %all_to_all.31.got_ref = f32[128,1,512]{2,1,0:T(1,128)S(1)} all-to-all(f32[128,1,512]{2,1,0:T(1,128)S(1)} %get-tuple-element.48), channel_id=1, replica_groups=mesh['gx'=8,'gy'=4,'af'=4] {'gx','gy','af'}, dimensions={0} | all-to-all | bytes 524288 | tf_op jit(solution)/shard_map/all_to_all | solution.py:712
  61.1 1.7 %even.2 = (f32[128,1,256]{2,1,0:T(1,128)S(1)}, f32[18,8,128]{2,1,0:T(8,128)S(1)}, f32[16,8,128]{2,1,0:T(8,128)S(1)}, f32[8,128]{1,0:T(8,128)S(1)}) custom-call(s32[1]{0:T(128)} %bitcast.me_ref, f32[128,1,512]{2,1,0:T(1,128)S(1)} %all_to_all.31.got_ref, f32[8,24,8,128]{3,2,1,0:T(8,128)S(1)} %get-tuple-element.41.cells_ref, ...), custom_call_target="tpu_custom_call" | custom-call | tf_op jit(solution)/shard_map/even/pallas_call | solution.py:700
  62.8 14.2 %all_to_all.32.got_ref = f32[128,1,256]{2,1,0:T(1,128)S(1)} all-to-all(f32[128,1,256]{2,1,0:T(1,128)S(1)} %get-tuple-element.55), channel_id=1, replica_groups=mesh['gx'=8,'gy'=4,'af'=4] {'gx','gy','af'}, dimensions={0} | all-to-all | bytes 262144 | tf_op jit(solution)/shard_map/all_to_all | solution.py:712
  77.0 1.4 %odd.2 = (f32[128,1,512]{2,1,0:T(1,128)S(1)}, f32[14,8,128]{2,1,0:T(8,128)S(1)}, f32[8,128]{1,0:T(8,128)S(1)}) custom-call(s32[1]{0:T(128)} %bitcast.me_ref, f32[128,1,256]{2,1,0:T(1,128)S(1)} %all_to_all.32.got_ref, f32[8,24,8,128]{3,2,1,0:T(8,128)S(1)} %get-tuple-element.41.cells_ref, f32[16,8,128]{2,1,0:T(8,128)S(1)} %get-tuple-element.56.field_ref, ...), custom_call_target="tpu_custom_call" | custom-call | tf_op jit(solution)/shard_map/odd/pallas_call | solution.py:700
  78.4 15.2 %all_to_all.33.got_ref = f32[128,1,512]{2,1,0:T(1,128)S(1)} all-to-all(f32[128,1,512]{2,1,0:T(1,128)S(1)} %get-tuple-element.59), channel_id=1, replica_groups=mesh['gx'=8,'gy'=4,'af'=4] {'gx','gy','af'}, dimensions={0} | all-to-all | bytes 524288 | tf_op jit(solution)/shard_map/all_to_all | solution.py:712
  93.6 1.5 %even.3 = (f32[128,1,256]{2,1,0:T(1,128)S(1)}, f32[12,8,128]{2,1,0:T(8,128)S(1)}, f32[10,8,128]{2,1,0:T(8,128)S(1)}, f32[8,128]{1,0:T(8,128)S(1)}) custom-call(s32[1]{0:T(128)} %bitcast.me_ref, f32[128,1,512]{2,1,0:T(1,128)S(1)} %all_to_all.33.got_ref, f32[8,24,8,128]{3,2,1,0:T(8,128)S(1)} %get-tuple-element.41.cells_ref, ...), custom_call_target="tpu_custom_call" | custom-call | tf_op jit(solution)/shard_map/even/pallas_call | solution.py:700
  95.2 14.2 %all_to_all.34.got_ref = f32[128,1,256]{2,1,0:T(1,128)S(1)} all-to-all(f32[128,1,256]{2,1,0:T(1,128)S(1)} %get-tuple-element.62), channel_id=1, replica_groups=mesh['gx'=8,'gy'=4,'af'=4] {'gx','gy','af'}, dimensions={0} | all-to-all | bytes 262144 | tf_op jit(solution)/shard_map/all_to_all | solution.py:712
  109.4 1.2 %odd.3 = (f32[8,8,128]{2,1,0:T(8,128)}, f32[4,256]{1,0:T(4,128)}) custom-call(s32[1]{0:T(128)} %bitcast.me_ref, f32[128,1,256]{2,1,0:T(1,128)S(1)} %all_to_all.34.got_ref, f32[8,24,8,128]{3,2,1,0:T(8,128)S(1)} %get-tuple-element.41.cells_ref, f32[10,8,128]{2,1,0:T(8,128)S(1)} %get-tuple-element.63.field_ref, s32[16,128]{1,0:T(8,128)S(1)} %get-tuple-element.43.index_ref, ...), custom_call_target="tpu_custom_call" | custom-call | tf_op jit(solution)/shard_map/odd/pallas_call | solution.py:700
  (1 shorter events, 0.0 us)
Async XLA Ops:
  3.4 23.0 %all-to-all-start = ((f32[128,1,512]{2,1,0:T(1,128)}), f32[128,1,512]{2,1,0:T(1,128)S(1)}, u32[]{:S(2)}, u32[]{:S(2)}) async-start(f32[128,1,512]{2,1,0:T(1,128)} %get-tuple-element.36), calls=%async_computation | async-start | bytes 524288 | tf_op jit(solution)/shard_map/all_to_all | solution.py:712
  14.9 7.3 %collective-permute-start.1 = (f32[3,8,8,128]{3,2,1,0:T(8,128)}, f32[3,8,8,128]{3,2,1,0:T(8,128)S(1)}, u32[]{:S(2)}, u32[]{:S(2)}) collective-permute-start(f32[3,8,8,128]{3,2,1,0:T(8,128)} %get-tuple-element.37), channel_id=1, source_target_pairs={{16,32},{48,64},{80,96},{32,16},{64,48},{96,80},{17,33},{49,65},{8... | collective-permute-start | bytes 294920 | tf_op jit(solution)/shard_map/ppermute | solution.py:717
  18.4 3.7 %collective-permute-start = (f32[3,8,8,128]{3,2,1,0:T(8,128)}, f32[3,8,8,128]{3,2,1,0:T(8,128)S(1)}, u32[]{:S(2)}, u32[]{:S(2)}) collective-permute-start(f32[3,8,8,128]{3,2,1,0:T(8,128)} %get-tuple-element.37), channel_id=1, source_target_pairs={{0,16},{32,48},{64,80},{96,112},{16,0},{48,32},{80,64},{112,96},{1... | collective-permute-start | bytes 294920 | tf_op jit(solution)/shard_map/ppermute | solution.py:717
  18.5 0.9 copy-start

commit v8 on v7

--- a/solution.py
+++ b/solution.py
@@ -331,7 +331,7 @@
         seg_ref[11 + i] = source[8 * i : 8 * i + 8]
     seg_ref[14] = where_cell
     for i, ref in enumerate((press_ref, cond_ref, accum_matrix_ref)):
-        seg_ref[15 + 8 * i : 23 + 8 * i] = swap_x(ref[...])
+        seg_ref[15 + 8 * i : 23 + 8 * i] = ref[...]
     for copy in passing:
         copy.wait()
 
@@ -691,7 +691,9 @@
 
 
 def hold_kernel(given_ref, out_ref):
-    out_ref[...] = given_ref[...]
+    out_ref[:15] = given_ref[:15]
+    for i in range(15, 39, 8):
+        out_ref[i : i + 8] = swap_x(given_ref[i : i + 8])
 
 
 def call(kernel, name, scalars, arrays, outs, space=pltpu.VMEM, scratch=(), limit=20 * 1024 * 1024, out_spaces=None):

time: 111 us -> 111 us (level)
  no operation moved by 1% of the time
where the time goes in v8:
time: 111 us
  blocking collectives  74 us (67%)
  starting transfers between devices  15.1 us (14%)
  Pallas kernels  13 us (12%)
  waiting for transfers between devices  6.88 us (6%)
    all_to_all x5, blocking collectives, exchange(): return lax.all_to_all(message, ALL, split_axis=0, concat_axis=0, tiled=True)  74 us
    pallas_call x8, Pallas kernels, call(): pl.pallas_call(kernel, name=name, out_shape=[jax.ShapeDtypeStruct(shape,...  13 us
    all_to_all x1, starting transfers between devices, exchange(): return lax.all_to_all(message, ALL, split_axis=0, concat_axis=0, tiled=True)  11.5 us
    all_to_all x1, waiting for transfers between devices, exchange(): return lax.all_to_all(message, ALL, split_axis=0, concat_axis=0, tiled=True)  4.21 us
    ppermute x2, starting transfers between devices, swapped(): return lax.ppermute(block, 'gx', pairs + [(j, i) for i, j in pairs])  3.63 us
    ppermute x2, waiting for transfers between devices, swapped(): return lax.ppermute(block, 'gx', pairs + [(j, i) for i, j in pairs])  2.67 us
  transfers between devices with their start and end apart: 3, of which 2 were waited for; matrix products, arithmetic and copies ran while one was open for 0% of the time, Pallas kernels for 0%

profile of v8, /device:TPU:1, one launch (start us, length us, event | category | flops | bytes accessed | tf_op | source)
XLA Modules:
  0.0 110.6 jit_solution(9900791356543451112)
XLA Ops:
  0.6 2.7 %begin.1 = (f32[128,1,512]{2,1,0:T(1,128)}, f32[39,8,128]{2,1,0:T(8,128)}, f32[3,8,8,128]{3,2,1,0:T(8,128)}) custom-call(s32[1]{0:T(128)} %bitcast.me_ref, s32[4,256]{1,0:T(4,128)} %refs_0_.1, s32[4,256]{1,0:T(4,128)} %refs_1_.1, s32[4,256]{1,0:T(4,128)} %refs_2_.1, f32[4,256]{1,0:T(4,128)} %refs_3_.1, f32[4,256]{1,0:T(4,128)} %refs_4_.1, f32[4,256]{1,0:T(4,128)} %refs_5_.1, ...), custom_call_target="tpu_custom_call" | custom-call | tf_op jit(solution)/shard_map/begin/pallas_call | solution.py:702
  3.4 11.5 %all-to-all-start = ((f32[128,1,512]{2,1,0:T(1,128)}), f32[128,1,512]{2,1,0:T(1,128)S(1)}, u32[]{:S(2)}, u32[]{:S(2)}) async-start(f32[128,1,512]{2,1,0:T(1,128)} %get-tuple-element.36), calls=%async_computation | async-start | bytes 524288 | tf_op jit(solution)/shard_map/all_to_all | solution.py:714
  14.9 3.5 %collective-permute-start.1 = (f32[3,8,8,128]{3,2,1,0:T(8,128)}, f32[3,8,8,128]{3,2,1,0:T(8,128)S(1)}, u32[]{:S(2)}, u32[]{:S(2)}) collective-permute-start(f32[3,8,8,128]{3,2,1,0:T(8,128)} %get-tuple-element.37), channel_id=1, source_target_pairs={{16,32},{48,64},{80,96},{32,16},{64,48},{96,80},{17,33},{49,65},{8... | collective-permute-start | bytes 294920 | tf_op jit(solution)/shard_map/ppermute | solution.py:719
  18.4 0.1 collective-permute-start
  18.5 0.0 copy-start
  18.6 0.9 copy-done
  19.5 2.7 %collective-permute-done.1.across_ref = f32[3,8,8,128]{3,2,1,0:T(8,128)S(1)} collective-permute-done((f32[3,8,8,128]{3,2,1,0:T(8,128)}, f32[3,8,8,128]{3,2,1,0:T(8,128)S(1)}, u32[]{:S(2)}, u32[]{:S(2)}) %collective-permute-start.1) | collective-permute-done | bytes 98336 | tf_op jit(solution)/shard_map/ppermute | solution.py:719
  22.2 0.0 collective-permute-done.inside_ref
  22.2 4.2 %all-to-all-done.got_ref = f32[128,1,512]{2,1,0:T(1,128)S(1)} async-done(((f32[128,1,512]{2,1,0:T(1,128)}), f32[128,1,512]{2,1,0:T(1,128)S(1)}, u32[]{:S(2)}, u32[]{:S(2)}) %all-to-all-start) | async-done | bytes 262176 | tf_op jit(solution)/shard_map/all_to_all | solution.py:714
  26.4 2.9 %cells.1 = (f32[128,1,384]{2,1,0:T(1,128)S(1)}, f32[8,24,8,128]{3,2,1,0:T(8,128)S(1)}, f32[22,8,128]{2,1,0:T(8,128)S(1)}, s32[16,128]{1,0:T(8,128)S(1)}, bf16[3,...) custom-call(s32[1]{0:T(128)} %bitcast.me_ref, ...), custom_call_target="tpu_custom_call" | custom-call | tf_op jit(solution)/shard_map/cells/pallas_call | solution.py:702
  29.2 15.0 %all_to_all.30.got_ref = f32[128,1,384]{2,1,0:T(1,128)S(1)} all-to-all(f32[128,1,384]{2,1,0:T(1,128)S(1)} %get-tuple-element.40), channel_id=1, replica_groups=mesh['gx'=8,'gy'=4,'af'=4] {'gx','gy','af'}, dimensions={0} | all-to-all | bytes 393216 | tf_op jit(solution)/shard_map/all_to_all | solution.py:714
  44.3 1.5 %first.1 = (f32[128,1,512]{2,1,0:T(1,128)S(1)}, f32[20,8,128]{2,1,0:T(8,128)S(1)}, f32[8,128]{1,0:T(8,128)S(1)}, f32[8,128]{1,0:T(8,128)S(1)}, f32[8,128]{1,0:T(...) custom-call(s32[1]{0:T(128)} %bitcast.me_ref, f32[128,1,384]{2,1,0:T(1,128)S(1)} %all_to_all.30.got_ref, ...), custom_call_target="tpu_custom_call" | custom-call | tf_op jit(solution)/shard_map/first/pallas_call | solution.py:702
  45.8 15.3 %all_to_all.31.got_ref = f32[128,1,512]{2,1,0:T(1,128)S(1)} all-to-all(f32[128,1,512]{2,1,0:T(1,128)S(1)} %get-tuple-element.48), channel_id=1, replica_groups=mesh['gx'=8,'gy'=4,'af'=4] {'gx','gy','af'}, dimensions={0} | all-to-all | bytes 524288 | tf_op jit(solution)/shard_map/all_to_all | solution.py:714
  61.1 1.7 %even.2 = (f32[128,1,256]{2,1,0:T(1,128)S(1)}, f32[18,8,128]{2,1,0:T(8,128)S(1)}, f32[16,8,128]{2,1,0:T(8,128)S(1)}, f32[8,128]{1,0:T(8,128)S(1)}) custom-call(s32[1]{0:T(128)} %bitcast.me_ref, f32[128,1,512]{2,1,0:T(1,128)S(1)} %all_to_all.31.got_ref, f32[8,24,8,128]{3,2,1,0:T(8,128)S(1)} %get-tuple-element.41.cells_ref, ...), custom_call_target="tpu_custom_call" | custom-call | tf_op jit(solution)/shard_map/even/pallas_call | solution.py:702
  62.8 14.2 %all_to_all.32.got_ref = f32[128,1,256]{2,1,0:T(1,128)S(1)} all-to-all(f32[128,1,256]{2,1,0:T(1,128)S(1)} %get-tuple-element.55), channel_id=1, replica_groups=mesh['gx'=8,'gy'=4,'af'=4] {'gx','gy','af'}, dimensions={0} | all-to-all | bytes 262144 | tf_op jit(solution)/shard_map/all_to_all | solution.py:714
  77.0 1.4 %odd.2 = (f32[128,1,512]{2,1,0:T(1,128)S(1)}, f32[14,8,128]{2,1,0:T(8,128)S(1)}, f32[8,128]{1,0:T(8,128)S(1)}) custom-call(s32[1]{0:T(128)} %bitcast.me_ref, f32[128,1,256]{2,1,0:T(1,128)S(1)} %all_to_all.32.got_ref, f32[8,24,8,128]{3,2,1,0:T(8,128)S(1)} %get-tuple-element.41.cells_ref, f32[16,8,128]{2,1,0:T(8,128)S(1)} %get-tuple-element.56.field_ref, ...), custom_call_target="tpu_custom_call" | custom-call | tf_op jit(solution)/shard_map/odd/pallas_call | solution.py:702
  78.4 15.2 %all_to_all.33.got_ref = f32[128,1,512]{2,1,0:T(1,128)S(1)} all-to-all(f32[128,1,512]{2,1,0:T(1,128)S(1)} %get-tuple-element.59), channel_id=1, replica_groups=mesh['gx'=8,'gy'=4,'af'=4] {'gx','gy','af'}, dimensions={0} | all-to-all | bytes 524288 | tf_op jit(solution)/shard_map/all_to_all | solution.py:714
  93.6 1.5 %even.3 = (f32[128,1,256]{2,1,0:T(1,128)S(1)}, f32[12,8,128]{2,1,0:T(8,128)S(1)}, f32[10,8,128]{2,1,0:T(8,128)S(1)}, f32[8,128]{1,0:T(8,128)S(1)}) custom-call(s32[1]{0:T(128)} %bitcast.me_ref, f32[128,1,512]{2,1,0:T(1,128)S(1)} %all_to_all.33.got_ref, f32[8,24,8,128]{3,2,1,0:T(8,128)S(1)} %get-tuple-element.41.cells_ref, ...), custom_call_target="tpu_custom_call" | custom-call | tf_op jit(solution)/shard_map/even/pallas_call | solution.py:702
  95.2 14.2 %all_to_all.34.got_ref = f32[128,1,256]{2,1,0:T(1,128)S(1)} all-to-all(f32[128,1,256]{2,1,0:T(1,128)S(1)} %get-tuple-element.62), channel_id=1, replica_groups=mesh['gx'=8,'gy'=4,'af'=4] {'gx','gy','af'}, dimensions={0} | all-to-all | bytes 262144 | tf_op jit(solution)/shard_map/all_to_all | solution.py:714
  109.4 1.2 %odd.3 = (f32[8,8,128]{2,1,0:T(8,128)}, f32[4,256]{1,0:T(4,128)}) custom-call(s32[1]{0:T(128)} %bitcast.me_ref, f32[128,1,256]{2,1,0:T(1,128)S(1)} %all_to_all.34.got_ref, f32[8,24,8,128]{3,2,1,0:T(8,128)S(1)} %get-tuple-element.41.cells_ref, f32[10,8,128]{2,1,0:T(8,128)S(1)} %get-tuple-element.63.field_ref, s32[16,128]{1,0:T(8,128)S(1)} %get-tuple-element.43.index_ref, ...), custom_call_target="tpu_custom_call" | custom-call | tf_op jit(solution)/shard_map/odd/pallas_call | solution.py:702
  (1 shorter events, 0.0 us)
Async XLA Ops:
  3.4 23.0 %all-to-all-start = ((f32[128,1,512]{2,1,0:T(1,128)}), f32[128,1,512]{2,1,0:T(1,128)S(1)}, u32[]{:S(2)}, u32[]{:S(2)}) async-start(f32[128,1,512]{2,1,0:T(1,128)} %get-tuple-element.36), calls=%async_computation | async-start | bytes 524288 | tf_op jit(solution)/shard_map/all_to_all | solution.py:714
  14.9 7.3 %collective-permute-start.1 = (f32[3,8,8,128]{3,2,1,0:T(8,128)}, f32[3,8,8,128]{3,2,1,0:T(8,128)S(1)}, u32[]{:S(2)}, u32[]{:S(2)}) collective-permute-start(f32[3,8,8,128]{3,2,1,0:T(8,128)} %get-tuple-element.37), channel_id=1, source_target_pairs={{16,32},{48,64},{80,96},{32,16},{64,48},{96,80},{17,33},{49,65},{8... | collective-permute-start | bytes 294920 | tf_op jit(solution)/shard_map/ppermute | solution.py:719
  18.4 3.7 %collective-permute-start = (f32[3,8,8,128]{3,2,1,0:T(8,128)}, f32[3,8,8,128]{3,2,1,0:T(8,128)S(1)}, u32[]{:S(2)}, u32[]{:S(2)}) collective-permute-start(f32[3,8,8,128]{3,2,1,0:T(8,128)} %get-tuple-element.37), channel_id=1, source_target_pairs={{0,16},{32,48},{64,80},{96,112},{16,0},{48,32},{80,64},{112,96},{1... | collective-permute-start | bytes 294920 | tf_op jit(solution)/shard_map/ppermute | solution.py:719
  18.5 0.9 copy-start
